TPU v7x, 512 devices: a whole 4x8x8 slice. The times are simulated.
512 devices in a mesh: tm: 32 (over y_lo, x, core), heads: 16 (over z, y_hi).
Axes of the slice: x: 4, y: 8 (y_hi: 2, y_lo: 4; y = y_hi * 4 + y_lo), z: 8, core: 2. Of those that a mesh axis runs over, the one named last changes fastest.
Arguments:
- layer_input: bfloat16 [4096, 8192], P('tm', 'heads'), may hold values from -0.119628906 to 0.119628906
- proj_weight: bfloat16 [2048, 8192], P('tm', 'heads'), may hold values from -0.0625 to 0.0625
- ssd_input: float32 [4096, 8192], P('tm', 'heads'), may hold values from -0.036 to 0.036
- log_decay: float32 [4096, 128], P('tm', 'heads'), may hold values from -1 to 0, as said below
- out_grad: float32 [4096, 8192], P('tm', 'heads'), may hold values from -15 to 15
Outputs:
- grad_x: float32 [4096, 8192], P('tm', 'heads')
- grad_log: float32 [4096, 128], P('tm', 'heads')
- grad_input: bfloat16 [4096, 8192], P('tm', 'heads')
- grad_weight: float32 [2048, 8192], P('tm', 'heads')
Inputs may be any that keep to these rules, and one draw needn't show every extreme that they name: `log_decay`: all entries are negative.
All inputs are finite; a program needn't handle non-finite values.
Results may differ from a plain program's by a relative error of at most 0.023.
Values may be sent and summed in bfloat16 or wider, within the bound.
No kernel may reach another device: no remote copies, remote signals or barrier semaphores. Data moves between devices by JAX's collectives and lax.ppermute only.
A program may use at most 64 MiB of HBM per device.

v0:
```python
import jax
import jax.numpy as jnp
from jax import lax
from jax.sharding import PartitionSpec as P

N = 128
SPAN = 128


highest = lax.Precision.HIGHEST


def entering(array, axis, join, neutral):
    place = lax.axis_index(axis)
    gathered = jax.tree.map(
        lambda a, kind: lax.all_gather(a.astype(kind), axis),
        array,
        jax.tree.map(lambda a: jnp.bfloat16 if a.dtype == jnp.float32 else a.dtype, array),
    )
    state = jax.tree.map(lambda a, e: jnp.zeros_like(a) + jnp.asarray(e, a.dtype), array, neutral)

    def one(step, state):
        return join(
            state,
            jax.tree.map(
                lambda a, own: lax.dynamic_index_in_dim(a, step, 0, False).astype(own.dtype),
                gathered,
                array,
            ),
        )

    return lax.fori_loop(0, place, one, state)


def carried_in(array, axis, combine, identity):
    length, index = (lax.axis_size(axis), lax.axis_index(axis))
    everything = jax.tree.map(lambda part: lax.all_gather(part, axis), array)
    start = jax.tree.map(
        lambda part, zero: jnp.broadcast_to(jnp.asarray(zero, part.dtype), part.shape),
        array,
        identity,
    )

    def step(k, before):
        at = length - 1 - k
        reached = at > index
        new = combine(before, jax.tree.map(lambda part: part[at], everything))
        return jax.tree.map(lambda a, b: jnp.where(reached, a, b), new, before)

    return lax.fori_loop(0, length, step, start)


def for_sending(array):
    return jax.tree.map(lambda a: a.astype(jnp.bfloat16) if a.dtype == jnp.float32 else a, array)


def from_partner_2(block, axis, distance):
    count = lax.axis_size(axis)
    route = []
    for low in range(count):
        high = low | 1 << distance
        if high != low and high < count:
            route += [(low, high), (high, low)]
    return lax.ppermute(block, axis, route)


def span_sums(inputs, out_grads, logs, b_rows, c_rows):
    positions = jnp.arange(inputs.shape[0])
    lower_ones = (positions[:, None] >= positions[None, :]).astype(jnp.float32)
    cumlog = jnp.dot(lower_ones, logs, precision=highest)
    decay_sum = cumlog[-1]
    head_state = jnp.einsum(
        "jn,jh,jhp->hnp", b_rows, jnp.exp(decay_sum[None] - cumlog), inputs, precision=highest
    )
    grad_state = jnp.einsum("in,ih,ihp->hnp", c_rows, jnp.exp(cumlog), out_grads, precision=highest)
    return (decay_sum, head_state, grad_state)


def span_grads(inputs, out_grads, logs, b_rows, c_rows, state_in, grad_out):
    positions = jnp.arange(inputs.shape[0])
    causal = positions[:, None] >= positions[None, :]
    lower_ones = causal.astype(jnp.float32)
    strict_ones = (positions[:, None] < positions[None, :]).astype(jnp.float32)
    cumlog = jnp.dot(lower_ones, logs, precision=highest)
    decay_sum = cumlog[-1]
    log_gaps = cumlog.T[:, :, None] - cumlog.T[:, None, :]
    decay_mat = jnp.where(causal[None], jnp.exp(jnp.minimum(log_gaps, 0.0)), 0.0)
    inner_cb = jnp.dot(c_rows, b_rows.T, precision=highest)
    inner_gx = jnp.einsum("ihp,jhp->hij", out_grads, inputs, precision=highest)
    decayed_cb = decay_mat * inner_cb[None]
    decayed_gx = decay_mat * inner_gx
    to_end = jnp.exp(decay_sum[None] - cumlog)
    from_start = jnp.exp(cumlog)
    b_state = jnp.einsum("jn,hnp->jhp", b_rows, grad_out, precision=highest)
    c_state = jnp.einsum("in,hnp->ihp", c_rows, state_in, precision=highest)
    grad_in = (
        jnp.einsum("hij,ihp->jhp", decayed_cb, out_grads, precision=highest)
        + to_end[:, :, None] * b_state
    )
    x_state = jnp.einsum("jhp,hnp->jhn", inputs, grad_out, precision=highest)
    grad_b = jnp.einsum("hij,in->jn", decayed_gx, c_rows, precision=highest) + jnp.einsum(
        "jh,jhn->jn", to_end, x_state, precision=highest
    )
    g_state = jnp.einsum("ihp,hnp->ihn", out_grads, state_in, precision=highest)
    grad_c = jnp.einsum("hij,jn->in", decayed_gx, b_rows, precision=highest) + jnp.einsum(
        "ih,ihn->in", from_start, g_state, precision=highest
    )
    pair_weight = decayed_cb * inner_gx
    prefix_sum = jnp.einsum("hij,jt->hit", pair_weight, strict_ones, precision=highest)
    inside = jnp.einsum("it,hit->th", lower_ones, prefix_sum, precision=highest)
    earlier = from_start * jnp.sum(c_state * out_grads, axis=2)
    later_terms = to_end * jnp.sum(b_state * inputs, axis=2)
    across = jnp.sum(grad_out * state_in, axis=(1, 2)) * jnp.exp(decay_sum)
    grad_log = (
        inside
        + jnp.dot(lower_ones.T, earlier, precision=highest)
        + jnp.dot(strict_ones.T, later_terms, precision=highest)
        + across[None]
    )
    return (grad_in, grad_log, grad_b, grad_c)


def combine(earlier, later):
    return (earlier[0] + later[0], jnp.exp(later[0])[:, None, None] * earlier[1] + later[1])


def on_device(layer_input, proj_weight, ssd_input, log_decay, out_grad):
    weight_cols = lax.all_gather(proj_weight, "tm", axis=0, tiled=True)
    steps_here = layer_input.shape[0]
    group_width = 2 * N
    contract_cols = (((1,), (1,)), ((), ()))
    partial_bc = lax.dot_general(
        layer_input, weight_cols, contract_cols, preferred_element_type=jnp.float32
    )
    head_index = lax.axis_index("heads")
    odd_member = head_index % 2 == 1
    whole_bc = lax.psum(partial_bc, "heads")
    bc_group = lax.dynamic_slice_in_dim(whole_bc, head_index // 2 * group_width, group_width, 1)
    heads_here = log_decay.shape[1]
    head_size = ssd_input.shape[1] // heads_here
    spans = steps_here // SPAN
    inputs = ssd_input.reshape(spans, SPAN, heads_here, head_size)
    out_grads = out_grad.reshape(spans, SPAN, heads_here, head_size)
    logs = log_decay.reshape(spans, SPAN, heads_here)
    b_rows = bc_group[:, :N].reshape(spans, SPAN, N)
    c_rows = bc_group[:, N:].reshape(spans, SPAN, N)
    decay_sums, head_states, grad_states = jax.vmap(span_sums)(
        inputs, out_grads, logs, b_rows, c_rows
    )
    zero_sum = jnp.zeros((heads_here,), jnp.float32)
    zero_state = jnp.zeros((heads_here, N, head_size), jnp.float32)

    def fold_span(carry, item):
        return (combine(carry, item), None)

    local_fwd, _ = lax.scan(fold_span, (zero_sum, zero_state), (decay_sums, head_states))
    local_bwd, _ = lax.scan(
        fold_span, (zero_sum, zero_state), (decay_sums, grad_states), reverse=True
    )
    identity = (zero_sum, zero_state)
    _, slab_state = entering(local_fwd, "tm", combine, identity)
    _, slab_grad = carried_in(local_bwd, "tm", combine, identity)

    def carry_on(carry, item):
        return (jnp.exp(item[0])[:, None, None] * carry + item[1], carry)

    _, states = lax.scan(carry_on, slab_state, (decay_sums, head_states))
    _, grads = lax.scan(carry_on, slab_grad, (decay_sums, grad_states), reverse=True)
    results = lax.map(
        lambda item: span_grads(*item), (inputs, out_grads, logs, b_rows, c_rows, states, grads)
    )
    grad_x = results[0].reshape(steps_here, heads_here * head_size)
    grad_log = results[1].reshape(steps_here, heads_here)
    grad_b = results[2].reshape(steps_here, N)
    grad_c = results[3].reshape(steps_here, N)
    own_half = jnp.where(odd_member, grad_c, grad_b)
    other_half = jnp.where(odd_member, grad_b, grad_c)
    from_partner = from_partner_2(for_sending(other_half), "heads", 0).astype(other_half.dtype)
    grad_half = (own_half + from_partner).astype(jnp.bfloat16)
    grad_bc = lax.all_gather(grad_half, "heads", axis=1, tiled=True)
    grad_input = jnp.dot(grad_bc, weight_cols, preferred_element_type=jnp.float32).astype(
        jnp.bfloat16
    )
    grad_rows = lax.all_to_all(grad_bc, "tm", split_axis=1, concat_axis=0, tiled=True)
    grad_weight = lax.dot_general(
        grad_rows,
        lax.all_gather(layer_input, "tm", axis=0, tiled=True),
        (((0,), (0,)), ((), ())),
        preferred_element_type=jnp.float32,
    )
    return (grad_x, grad_log, grad_input, grad_weight)


def solution(mesh):
    return jax.shard_map(
        on_device,
        mesh=mesh,
        in_specs=(
            P("tm", "heads"),
            P("tm", "heads"),
            P("tm", "heads"),
            P("tm", "heads"),
            P("tm", "heads"),
        ),
        out_specs=(P("tm", "heads"), P("tm", "heads"), P("tm", "heads"), P("tm", "heads")),
        check_vma=False,
    )
```

profile of v0, /device:TPU:56, one launch (start us, length us, event | category | flops | bytes accessed | tf_op | source)
XLA Modules:
  0.0 575.7 jit_solution(2570399712532000757)
XLA Ops:
  8.0 68.9 %all-gather.7.cloned.1.call-done = bf16[2048,512]{1,0:T(8,128)(2,1)} async-done(((bf16[64,512]{1,0:T(8,128)(2,1)}), bf16[2048,512]{1,0:T(8,128)(2,1)}) %all-gather.7.cloned.1.call-update) | async-done | bytes 2097168 | tf_op jit(solution)/shard_map/all_gather | solution.py:128
  76.9 3.5 fusion.64
  81.0 206.1 %all-reduce.2.cloned.1.call-done = f32[128,2048]{1,0:T(8,128)} async-done(((f32[128,2048]{1,0:T(8,128)}), f32[128,2048]{1,0:T(8,128)}) %all-reduce.2.cloned.1.call-update) | async-done | bytes 1048592 | tf_op jit(solution)/shard_map/psum | solution.py:137
  287.2 1.9 fusion.12
  289.2 2.0 fusion.9
  292.1 34.5 %all-gather = f32[32,1,8]{2,1,0:T(1,128)S(1)} all-gather(f32[1,1,8]{2,1,0:T(1,128)S(1)} %bitcast.137), channel_id=1, replica_groups=mesh['tm'=32,'heads'=16] {'tm'}, dimensions={0}, use_global_device_ids=true | all-gather | bytes 1056 | tf_op jit(solution)/shard_map/all_gather | solution.py:37
  326.6 37.4 %all-gather.1 = bf16[32,1,8]{2,1,0:T(2,128)(2,1)S(1)} all-gather(bf16[1,1,8]{2,1,0:T(2,128)(2,1)S(1)} %bitcast.139), channel_id=1, replica_groups=mesh['tm'=32,'heads'=16] {'tm'}, dimensions={0}, use_global_device_ids=true | all-gather | bytes 528 | tf_op jit(solution)/shard_map/all_gather | solution.py:16
  364.0 1.1 multiply_reduce_fusion
  365.1 1.1 fusion.43
  366.9 31.5 %while.18 = (s32[]{:T(128)}, f32[8,128,64]{2,1,0:T(8,128)S(1)}, s32[]{:T(128)}, bf16[32,8]{1,0:T(8,128)(2,1)S(1)}, bf16[32,8,128,64]{2,3,1,0:T(8,128)(2,1)}, /*index=5*/s32[]{:T(128)}, s32[]{:T(128)}, s32[]{:T(128)}) while((s32[]{:T(128)}, f32[8,128,64]{2,1,0:T(8,128)S(1)}, s32[]{:T(128)}, bf16[32,8]{1,0:T(8,128)(2,1)S(1)}, ...), condition=%wide.region_4.5_spmd, body=%wide.region_3.4_spmd.sunk | while | flops 196621 | bytes 1179863 | solution.py:32
  380.0 0.9 constant_dynamic-slice_fusion.4
  383.9 0.9 constant_dynamic-slice_fusion.4
  390.5 0.9 constant_dynamic-slice_fusion.4
  397.1 0.9 constant_dynamic-slice_fusion.4
  399.3 1.2 multiply_reduce_fusion.3
  401.3 1.0 convolution_add_fusion.1
  402.3 23.9 %all-gather.9.cloned.1.call-done = f32[32,8,128,64]{2,3,1,0:T(8,128)} async-done(((f32[1,8,128,64]{2,3,1,0:T(8,128)}), f32[32,8,128,64]{2,3,1,0:T(8,128)}) %all-gather.9.cloned.1.call-update) | async-done | bytes 8388624 | tf_op jit(solution)/shard_map/all_gather | solution.py:37
  426.2 44.0 %while.19 = (s32[]{:T(128)}, f32[8,128,64]{2,1,0:T(8,128)S(1)}, s32[]{:T(128)}, f32[32,8]{1,0:T(8,128)S(1)}, f32[32,8,128,64]{2,3,1,0:T(8,128)}, /*index=5*/s32[]{:T(128)}, s32[]{:T(128)}, s32[]{:T(128)}, s32[]{:T(128)}) while((s32[]{:T(128)}, f32[8,128,64]{2,1,0:T(8,128)S(1)}, s32[]{:T(128)}, f32[32,8]{1,0:T(8,128)S(1)}, ...), condition=%wide.region_2.3_spmd.clone, body=%wide.region_1.2_spmd.clone.sunk | while | flops 262152 | bytes 1835279 | solution.py:50
  426.2 1.0 constant_dynamic-slice_fusion.5
  427.6 1.0 constant_dynamic-slice_fusion.5
  429.0 1.0 constant_dynamic-slice_fusion.5
  430.4 1.0 constant_dynamic-slice_fusion.5
  431.7 1.0 constant_dynamic-slice_fusion.5
  433.1 1.0 constant_dynamic-slice_fusion.5
  434.5 1.0 constant_dynamic-slice_fusion.5
  435.9 1.0 constant_dynamic-slice_fusion.5
  437.2 1.0 constant_dynamic-slice_fusion.5
  438.6 1.0 constant_dynamic-slice_fusion.5
  440.0 1.0 constant_dynamic-slice_fusion.5
  441.3 1.0 constant_dynamic-slice_fusion.5
  442.7 1.0 constant_dynamic-slice_fusion.5
  444.1 1.0 constant_dynamic-slice_fusion.5
  445.5 1.0 constant_dynamic-slice_fusion.5
  446.8 1.0 constant_dynamic-slice_fusion.5
  448.2 1.0 constant_dynamic-slice_fusion.5
  449.6 1.0 constant_dynamic-slice_fusion.5
  451.0 1.0 constant_dynamic-slice_fusion.5
  452.3 1.0 constant_dynamic-slice_fusion.5
  453.7 1.0 constant_dynamic-slice_fusion.5
  455.1 1.0 constant_dynamic-slice_fusion.5
  456.5 1.0 constant_dynamic-slice_fusion.5
  457.8 1.0 constant_dynamic-slice_fusion.5
  459.2 1.0 constant_dynamic-slice_fusion.5
  460.6 1.0 constant_dynamic-slice_fusion.5
  462.0 1.0 constant_dynamic-slice_fusion.5
  463.3 1.0 constant_dynamic-slice_fusion.5
  464.7 1.0 constant_dynamic-slice_fusion.5
  466.1 1.0 constant_dynamic-slice_fusion.5
  467.5 1.0 constant_dynamic-slice_fusion.5
  468.8 1.0 constant_dynamic-slice_fusion.5
  471.1 1.2 fusion.4
  472.3 1.6 copy.60
  473.9 1.2 select_convert_fusion
  475.1 4.2 collective-permute-start
  479.3 2.1 multiply_reduce_fusion.2
  481.4 3.4 collective-permute-done
  484.8 56.8 %all_gather.30 = bf16[128,2048]{1,0:T(8,128)(2,1)} all-gather(bf16[128,128]{1,0:T(8,128)(2,1)S(1)} %add_convert_fusion), channel_id=1, replica_groups=mesh['tm'=32,'heads'=16] {'heads'}, dimensions={1}, use_global_device_ids=true | all-gather | bytes 557056 | tf_op jit(solution)/shard_map/all_gather | solution.py:180
  541.7 2.0 copy.40
  543.7 8.2 %all-to-all-start = ((bf16[128,32,64]{0,2,1:T(8,128)(2,1)}), bf16[128,32,64]{0,2,1:T(8,128)(2,1)}, u32[]{:S(2)}, u32[]{:S(2)}) async-start(bf16[128,32,64]{0,2,1:T(8,128)(2,1)} %bitcast.127), calls=%async_computation | async-start | bytes 1048576 | tf_op jit(solution)/shard_map/all_to_all | solution.py:184
  551.9 1.8 fusion.7
  555.1 1.4 fusion.13
  556.5 2.2 convolution_convert_fusion
  558.7 6.7 %all-to-all-done = bf16[128,32,64]{0,2,1:T(8,128)(2,1)} async-done(((bf16[128,32,64]{0,2,1:T(8,128)(2,1)}), bf16[128,32,64]{0,2,1:T(8,128)(2,1)}, u32[]{:S(2)}, u32[]{:S(2)}) %all-to-all-start) | async-done | bytes 524320 | tf_op jit(solution)/shard_map/all_to_all | solution.py:184
  565.4 3.8 fusion.14
  (237 shorter events, 44.8 us)
Async XLA Ops:
  7.2 73.4 %copy-start = (f32[128,8]{0,1:T(8,128)S(1)}, f32[128,8]{0,1:T(8,128)}, u32[]{:S(2)}) copy-start(f32[128,8]{0,1:T(8,128)} %param.12) | copy-start | bytes 12292
  7.2 73.2 %copy-start.3 = (f32[128,512]{1,0:T(8,128)S(1)}, f32[128,512]{1,0:T(8,128)}, u32[]{:S(2)}) copy-start(f32[128,512]{1,0:T(8,128)} %param.11) | copy-start | bytes 786436
  7.2 281.9 %copy-start.4 = (f32[128,512]{1,0:T(8,128)S(1)}, f32[128,512]{1,0:T(8,128)}, u32[]{:S(2)}) copy-start(f32[128,512]{1,0:T(8,128)} %param.13) | copy-start | bytes 786436
  7.2 69.7 %all-gather.7.cloned.1.call-start = ((), (), s32[]{:S(2)}) async-start(), calls=%async_computation.1 | async-start | bytes 2162688 | tf_op jit(solution)/shard_map/all_gather | solution.py:128
  7.9 279.2 %all-reduce.2.cloned.1.call-start = ((), (), s32[]{:S(2)}) async-start(), calls=%async_computation.2 | async-start | bytes 2097152 | tf_op jit(solution)/shard_map/psum | solution.py:137
  80.3 286.5 %all-gather.11.cloned.1.call-start = ((), (), s32[]{:S(2)}) async-start(), calls=%async_computation.4 | async-start | bytes 4325376 | tf_op jit(solution)/shard_map/all_gather | solution.py:16
  289.0 137.2 %all-gather.9.cloned.1.call-start = ((), (), s32[]{:S(2)}) async-start(), calls=%async_computation.3 | async-start | bytes 8650752 | tf_op jit(solution)/shard_map/all_gather | solution.py:37
  289.2 110.1 %copy-start.2 = (f32[128,512]{0,1:T(8,128)}, f32[128,512]{0,1:T(8,128)S(1)}, u32[]{:S(2)}) copy-start(f32[128,512]{0,1:T(8,128)S(1)} %copy.29) | copy-start | bytes 786436
  291.3 267.4 %all-gather.13.cloned.1.call-start = ((), (), s32[]{:S(2)}) async-start(), calls=%async_computation.5 | async-start | bytes 4325376 | tf_op jit(solution)/shard_map/all_gather | solution.py:187
  291.9 75.0 %copy-start.5 = (pred[128,128]{1,0:T(8,128)(4,1)}, pred[128,128]{1,0:T(8,128)(4,1)S(1)}, u32[]{:S(2)}) copy-start(pred[128,128]{1,0:T(8,128)(4,1)S(1)} %iota_compare_fusion.2) | copy-start | bytes 49156
  366.2 0.6 copy-start.6
  470.2 86.3 %copy-start.1 = (bf16[2048,512]{1,0:T(8,128)(2,1)S(1)}, bf16[2048,512]{1,0:T(8,128)(2,1)}, u32[]{:S(2)}) copy-start(bf16[2048,512]{1,0:T(8,128)(2,1)} %all-gather.7.cloned.1.call-done) | copy-start | bytes 6291460
  475.1 9.8 %collective-permute-start = (bf16[128,128]{1,0:T(8,128)(2,1)S(1)}, bf16[128,128]{1,0:T(8,128)(2,1)S(1)}, u32[]{:S(2)}, u32[]{:S(2)}) collective-permute-start(bf16[128,128]{1,0:T(8,128)(2,1)S(1)} %get-tuple-element.364), channel_id=1, source_target_pairs={{0,1},{1,0},{2,3},{3,2},{4,5},{5,4},{6,7},{7,6},{8,9},{9,8},{10,11... | collective-permute-start | bytes 98312 | tf_op jit(solution)/shard_map/ppermute | solution.py:64
  543.7 21.6 %all-to-all-start = ((bf16[128,32,64]{0,2,1:T(8,128)(2,1)}), bf16[128,32,64]{0,2,1:T(8,128)(2,1)}, u32[]{:S(2)}, u32[]{:S(2)}) async-start(bf16[128,32,64]{0,2,1:T(8,128)(2,1)} %bitcast.127), calls=%async_computation | async-start | bytes 1048576 | tf_op jit(solution)/shard_map/all_to_all | solution.py:184
Sparse Core Ops, SparseCore 0:
  10.2 66.6 all-gather.6
  80.5 206.6 all-reduce.1
  290.1 63.0 all-gather.10
  355.4 70.7 all-gather.8
  428.5 65.6 all-gather.12
where the time goes:
time: 585 us; the launch traced here: 576 us
  waiting for transfers between devices  310 us (53%)
  blocking collectives  129 us (22%)
  local copies, waits for them, and re-layouts  70.9 us (12%)
  matrix products  27.6 us (5%)
  between operations  14.1 us (2%)
  starting transfers between devices  12.7 us (2%)
  other arithmetic  8.84 us (2%)
    psum x1, waiting for transfers between devices, on_device(): whole_bc = lax.psum(partial_bc, 'heads')  206 us
    all_gather x1, waiting for transfers between devices, on_device(): weight_cols = lax.all_gather(proj_weight, 'tm', axis=0, tiled=True)  68.9 us
    all_gather x1, blocking collectives, on_device(): grad_bc = lax.all_gather(grad_half, 'heads', axis=1, tiled=True)  56.8 us
    dynamic_slice x64, local copies, waits for them, and re-layouts, step(): new = combine(before, jax.tree.map(lambda part: part[at], everything))  37.6 us
    all_gather x1, blocking collectives, entering(): lax.all_gather(a.astype(kind), axis)  37.4 us
    all_gather x1, blocking collectives, carried_in(): everything = jax.tree.map(lambda part: lax.all_gather(part, axis), array)  34.5 us
    dynamic_slice x48, local copies, waits for them, and re-layouts, one(): lax.dynamic_index_in_dim(a, step, 0, False).astype(own.dtype)  26.4 us
    all_gather x1, waiting for transfers between devices, carried_in(): everything = jax.tree.map(lambda part: lax.all_gather(part, axis), array)  23.9 us
  transfers between devices with their start and end apart: 7, of which 5 were waited for; matrix products, arithmetic and copies ran while one was open for 17% of the time, Pallas kernels for 0%

commit v1 on v0

v1 whole, which is shorter than its diff:
```python
import jax
import jax.numpy as jnp
from jax import lax
from jax.experimental import pallas as pl
from jax.experimental.pallas import tpu as pltpu
from jax.sharding import Mesh
from jax.sharding import PartitionSpec as P

N = 128
EXTRA_ROWS = 8
LN2 = 0.6931471805599453
F32 = jnp.float32
BF16 = jnp.bfloat16
F16 = jnp.float16
HIGHEST = lax.Precision.HIGHEST
TM = ("ylo", "x", "core")
HEADS = ("z", "yhi")


def dot(a, b, precision=None):
    return jnp.dot(a, b, preferred_element_type=F32, precision=precision)


def dot_nt(a, b, precision=None):
    return lax.dot_general(
        a, b, (((1,), (1,)), ((), ())), preferred_element_type=F32, precision=precision
    )


def dot_tn(a, b):
    return lax.dot_general(a, b, (((0,), (0,)), ((), ())), preferred_element_type=F32)


def split(a):
    high = a.astype(BF16)
    return high, (a - high.astype(F32)).astype(BF16)


def dot_split(a, b):
    a_high, a_low = split(a)
    b_high, b_low = split(b)
    return dot(a_high, b_high) + dot(a_low, b_high) + dot(a_high, b_low)


def three_terms(row):
    high = row.astype(BF16).astype(F32)
    middle = (row - high).astype(BF16).astype(F32)
    low = row - high - middle
    term = lax.broadcasted_iota(jnp.int32, (EXTRA_ROWS, N), 0)
    return jnp.where(
        term == 0, high, jnp.where(term == 1, middle, jnp.where(term == 2, low, 0.0))
    )


def exponent_of(a):
    top = jnp.max(jnp.max(jnp.abs(a), axis=1, keepdims=True), axis=0, keepdims=True)
    return jnp.ceil(jnp.log(jnp.maximum(top, 1e-30)) * (1.0 / LN2)) - 14.0


def power(exponent):
    return jnp.exp(exponent * LN2)


def iotas(n):
    return (
        lax.broadcasted_iota(jnp.int32, (n, n), 0),
        lax.broadcasted_iota(jnp.int32, (n, n), 1),
    )


def head_spread(heads, width):
    size = width // heads
    row = lax.broadcasted_iota(jnp.int32, (heads, width), 0)
    col = lax.broadcasted_iota(jnp.int32, (heads, width), 1)
    return ((col >= row * size) & (col < (row + 1) * size)).astype(F32)


def call(kernel, outs, flops, *args, smem=0, late=()):
    several = isinstance(outs, tuple)
    out_list = outs if several else (outs,)
    read = sum(a.size * a.dtype.itemsize for a in args)
    wrote = sum(o.size * o.dtype.itemsize for o in out_list)
    spaces = [pltpu.SMEM if k < smem else pltpu.VMEM for k in range(len(args))]
    for k in late:
        spaces[k] = pl.ANY
    scratch = [pltpu.VMEM(args[k].shape, args[k].dtype) for k in late]
    if late:
        scratch.append(pltpu.SemaphoreType.DMA((len(late),)))

    def body(*refs):
        refs = list(refs)
        buffers = refs[len(args) + len(out_list) :]
        copies = [
            pltpu.make_async_copy(refs[k], buffers[i], buffers[-1].at[i])
            for i, k in enumerate(late)
        ]
        for copy in copies:
            copy.start()
        for copy in copies:
            copy.wait()
        for i, k in enumerate(late):
            refs[k] = buffers[i]
        kernel(*refs[: len(args) + len(out_list)])

    return pl.pallas_call(
        body,
        out_shape=outs,
        in_specs=[pl.BlockSpec(memory_space=space) for space in spaces],
        out_specs=jax.tree.map(lambda _: pl.BlockSpec(memory_space=pltpu.VMEM), outs),
        scratch_shapes=scratch,
        cost_estimate=pl.CostEstimate(
            flops=flops, bytes_accessed=read + wrote, transcendentals=0
        ),
        compiler_params=pltpu.CompilerParams(vmem_limit_bytes=16 * 2**20),
    )(*args)


def decay_sums(log_ref, logt_ref):
    row, col = iotas(log_ref.shape[0])
    cum = dot((row >= col).astype(F32), log_ref[...], HIGHEST)
    cumt = dot(logt_ref[...], (row <= col).astype(F32), HIGHEST)
    return cum, cumt


def decay_factors(cum, width):
    spread = head_spread(cum.shape[1], width)
    last = cum[cum.shape[0] - 1 :, :]
    return dot(jnp.exp(last - cum), spread, HIGHEST), dot(jnp.exp(cum), spread, HIGHEST)


def prepare(x_ref, dy_ref, log_ref, logt_ref, xe_ref, dyf_ref, xet_ref, dyft_ref, ds_ref):
    steps = log_ref.shape[0]
    cum, cumt = decay_sums(log_ref, logt_ref)
    to_end, from_start = decay_factors(cum, x_ref.shape[1])
    xe = x_ref[...] * to_end
    dyf = dy_ref[...] * from_start
    xe_ref[...] = xe.astype(BF16)
    dyf_ref[...] = dyf.astype(BF16)
    xet_ref[...] = xe.T
    dyft_ref[...] = dyf.T
    ds_ref[...] = jnp.broadcast_to(cumt[:, steps - 1 : steps], ds_ref.shape)


def blocks_of(first, own_ref, other_ref, group, lines):
    column, half = divmod(group, 2)
    rows = []
    for line in (2 * half, 2 * half + 1):
        at = line * lines + column
        own, other = own_ref[at], other_ref[at]
        rows += [jnp.where(first, own, other), jnp.where(first, other, own)]
    return jnp.concatenate(rows, axis=0)


def partial_kernel(core_ref, x_ref, own_ref, other_ref, out_ref):
    first = core_ref[0] == 0
    x = x_ref[...]
    steps = x.shape[0]
    groups, _, columns = out_ref.shape
    top = jnp.zeros((steps, columns), F32)
    for group in range(groups):
        part = dot_nt(x, blocks_of(first, own_ref, other_ref, group, groups // 2))
        top = jnp.maximum(top, jnp.abs(part))
        out_ref[group, :steps, :] = part
    exponent = exponent_of(top)
    scale = power(-exponent)
    for group in range(groups):
        out_ref[group, :steps, :] = out_ref[group, :steps, :] * scale
        out_ref[group, steps:, :] = jnp.broadcast_to(exponent, (EXTRA_ROWS, columns))


def sum_kernel(pieces_ref, out_ref):
    pieces, rows, columns = pieces_ref.shape
    steps = rows - EXTRA_ROWS
    exponents = [pieces_ref[k, steps:, :] for k in range(pieces)]
    top = exponents[0]
    for exponent in exponents[1:]:
        top = jnp.maximum(top, exponent)
    top = top + jnp.ceil(jnp.log(1.0 * pieces) / LN2)
    total = jnp.zeros((steps, columns), F32)
    for k in range(pieces):
        total = total + pieces_ref[k, :steps, :] * power(exponents[k] - top)[:1, :]
    out_ref[:steps, :] = total
    out_ref[steps:, :] = top


def whole_bc(own_ref, other_ref):
    steps = own_ref.shape[0] - EXTRA_ROWS
    bc = own_ref[:steps, :] * power(own_ref[steps : steps + 1, :])
    bc = bc + other_ref[:steps, :] * power(other_ref[steps : steps + 1, :])
    return bc[:, :N], bc[:, N:]


def states_kernel(own_ref, other_ref, xet_ref, dyft_ref, ds_ref, out_ref):
    b_rows, c_rows = whole_bc(own_ref, other_ref)
    heads = ds_ref.shape[0]
    parts, rows, _ = out_ref.shape
    half = (rows - EXTRA_ROWS) // 2
    state = dot_split(xet_ref[...], b_rows)
    grad = dot_split(dyft_ref[...], c_rows)
    state_exponent = exponent_of(state)
    grad_exponent = exponent_of(grad)
    out_ref[:, :half, :] = (state * power(-state_exponent)).reshape(parts, half, N)
    out_ref[:, half : 2 * half, :] = (grad * power(-grad_exponent)).reshape(parts, half, N)
    row = lax.broadcasted_iota(jnp.int32, (EXTRA_ROWS, N), 0)
    for head in range(heads):
        terms = jnp.where(row == 3, state_exponent, three_terms(ds_ref[head : head + 1, :]))
        terms = jnp.where(row == 4, grad_exponent, terms)
        for part in range(head * parts // heads, (head + 1) * parts // heads):
            out_ref[part, 2 * half :, :] = terms


def local_kernel(own_ref, other_ref, x_ref, dy_ref, log_ref, logt_ref, gx_ref, grad_ref, inside_ref):
    b_rows, c_rows = (rows.astype(BF16) for rows in whole_bc(own_ref, other_ref))
    steps, heads = log_ref.shape
    size = x_ref.shape[1] // heads
    row, col = iotas(steps)
    later = row <= col
    at_or_after = (row >= col).astype(BF16)
    bct = dot_nt(b_rows, c_rows)
    pair_sum = jnp.zeros((steps, steps), F32)
    cum, cumt = decay_sums(log_ref, logt_ref)
    for h in range(heads):
        x = x_ref[:, h * size : (h + 1) * size].astype(BF16)
        dy = dy_ref[:, h * size : (h + 1) * size].astype(BF16)
        gap = cumt[h : h + 1, :] - cum[:, h : h + 1]
        decay = jnp.where(later, jnp.exp(jnp.minimum(gap, 0.0)), 0.0)
        decayed = decay * dot_nt(x, dy)
        pair_sum = pair_sum + decayed
        gx_ref[:, h * size : (h + 1) * size] = dot((decay * bct).astype(BF16), dy)
        reach = dot((decayed * bct).astype(BF16), at_or_after)
        inside_ref[h : h + 1, :] = jnp.sum(jnp.where(row < col, reach, 0.0), axis=0, keepdims=True)
    grad_ref[:steps] = dot(pair_sum.astype(BF16), c_rows)
    grad_ref[steps:] = dot(pair_sum.T.astype(BF16), b_rows)


def scan_kernel(parts_ref, out_ref):
    slabs, rows, _ = out_ref.shape
    rows -= EXTRA_ROWS
    half = rows // 2

    def extra(t, k):
        return parts_ref[t, rows + k : rows + k + 1, :]

    decays = [jnp.exp(extra(t, 0) + extra(t, 1) + extra(t, 2)) for t in range(slabs)]
    grads = [jnp.zeros((half, N), F32)]
    for t in range(slabs - 1, 0, -1):
        grads.append(decays[t] * grads[-1] + power(extra(t, 4)) * parts_ref[t, half:rows, :])
    grads = grads[::-1]
    state = jnp.zeros((half, N), F32)
    for t in range(slabs):
        out_ref[t, :half, :] = state.astype(BF16)
        out_ref[t, half:rows, :] = grads[t].astype(BF16)
        product = jnp.sum(state * grads[t], axis=0, keepdims=True)
        out_ref[t, rows:, :] = three_terms(product).astype(BF16)
        state = decays[t] * state + power(extra(t, 3)) * parts_ref[t, :half, :]


def entering(in_ref):
    parts, rows, _ = in_ref.shape
    half = (rows - EXTRA_ROWS) // 2
    state = in_ref[:, :half, :].reshape(parts * half, N)
    grad = in_ref[:, half : 2 * half, :].reshape(parts * half, N)
    return state, grad


def bc_grad_kernel(in_ref, xe_ref, dyf_ref, local_ref, out_ref):
    state, grad = entering(in_ref)
    steps = xe_ref.shape[0]
    out_ref[:N, :] = (local_ref[:steps] + dot(xe_ref[...], grad)).T.astype(BF16)
    out_ref[N:, :] = (local_ref[steps:] + dot(dyf_ref[...], state)).T.astype(BF16)


def finish_kernel(in_ref, own_ref, other_ref, x_ref, dy_ref, log_ref, logt_ref, gx_ref, inside_ref, out_ref, out_log_ref):
    state, grad = entering(in_ref)
    b_rows, c_rows = (rows.astype(BF16) for rows in whole_bc(own_ref, other_ref))
    steps, heads = log_ref.shape
    width = x_ref.shape[1]
    row, col = iotas(steps)
    cum, cumt = decay_sums(log_ref, logt_ref)
    to_end, from_start = decay_factors(cum, width)
    b_state = to_end * dot_nt(b_rows, grad)
    c_state = from_start * dot_nt(c_rows, state)
    out_ref[...] = gx_ref[...] + b_state
    spread = head_spread(heads, width)
    earlier = dot_nt(spread, c_state * dy_ref[...], HIGHEST)
    later = dot_nt(spread, b_state * x_ref[...], HIGHEST)
    parts = in_ref.shape[0]
    products = jnp.sum(in_ref[:, -EXTRA_ROWS:, :].astype(F32), axis=1)
    products = jnp.sum(products.reshape(heads, parts // heads, N), axis=1)
    across = jnp.sum(products, axis=1, keepdims=True)
    across = across * jnp.exp(cumt[:, steps - 1 : steps])
    out_log_ref[...] = (
        inside_ref[...]
        + dot(earlier, (row >= col).astype(F32), HIGHEST)
        + dot(later, (row < col).astype(F32), HIGHEST)
        + across
    )


def grad_input_kernel(core_ref, grads_ref, own_ref, other_ref, out_ref):
    first = core_ref[0] == 0
    groups = grads_ref.shape[0]
    total = jnp.zeros(out_ref.shape, F32)
    for group in range(groups):
        rows = blocks_of(first, own_ref, other_ref, group, groups // 2)
        total = total + dot_tn(grads_ref[group], rows)
    out_ref[...] = total.astype(BF16)


def row_blocks_kernel(grads_ref, out_ref):
    lines, _, rows, _ = out_ref.shape
    for group in range(grads_ref.shape[0]):
        column, high = divmod(group, 2)
        for k in range(2):
            for core in range(2):
                at = (2 * k + core) * rows
                out_ref[2 * high + k, 2 * column + core] = grads_ref[group, at : at + rows, :]


def grad_weight_kernel(place_ref, grads_ref, x0_ref, x1_ref, x2_ref, x3_ref, keep_ref, send_ref):
    first = place_ref[0] == 0
    line = place_ref[1]
    columns, rows, width = keep_ref.shape
    x = jnp.concatenate([ref[...] for ref in (x0_ref, x1_ref, x2_ref, x3_ref)], axis=0)
    for column in range(columns):
        grads = jnp.concatenate(
            [
                grads_ref[line ^ k, 2 * column : 2 * column + 2].reshape(2 * rows, -1)
                for k in range(grads_ref.shape[0])
            ],
            axis=1,
        )
        part = dot(grads, x)
        one, other = part[:rows], part[rows:]
        keep_ref[column] = jnp.where(first, one, other)
        send_ref[column] = jnp.where(first, other, one).astype(BF16)


def chip_sum_kernel(own_ref, other_ref, out_ref):
    for k in range(out_ref.shape[0]):
        out_ref[k] = (own_ref[k] + other_ref[k].astype(F32)).astype(BF16)


def line_sum_kernel(parts_ref, out_ref):
    total = parts_ref[0].astype(F32)
    for k in range(1, parts_ref.shape[0]):
        total = total + parts_ref[k].astype(F32)
    out_ref[...] = total


def copies_kernel(own_ref, other_ref, out_ref):
    total = (own_ref[...].astype(F32) + other_ref[...].astype(F32)).astype(BF16)
    for k in range(out_ref.shape[0]):
        out_ref[k] = total


def shape(dims, dtype=F32):
    return jax.ShapeDtypeStruct(dims, dtype)


def to_all(block, axis):
    count = lax.axis_size(axis)
    return lax.all_to_all(jnp.broadcast_to(block[None], (count,) + block.shape), axis, 0, 0)


def flip(block, axis, bit):
    return lax.ppermute(block, axis, [(k, k ^ bit) for k in range(lax.axis_size(axis))])


def swap(block, axis):
    return flip(block, axis, 1)


def on_device(layer_input, proj_weight, ssd_input, log_decay, out_grad):
    steps, width = layer_input.shape
    heads = log_decay.shape[1]
    slabs = lax.axis_size(TM)
    groups = lax.axis_size("z")
    rows_here = proj_weight.shape[0]
    core = lax.axis_index("core").reshape(1)
    share = ssd_input.shape[1] // slabs
    logt = log_decay.T

    line_w = to_all(proj_weight, "ylo")
    own_w = to_all(line_w, "x").reshape(-1, rows_here, width)
    other_w = swap(own_w, "core")
    xe, dyf, xet, dyft, ds = call(
        prepare,
        (
            shape(ssd_input.shape, BF16),
            shape(ssd_input.shape, BF16),
            shape(ssd_input.shape[::-1]),
            shape(ssd_input.shape[::-1]),
            shape((heads, N)),
        ),
        10**7,
        ssd_input,
        out_grad,
        log_decay,
        logt,
    )
    partial = call(
        partial_kernel,
        shape((groups, steps + EXTRA_ROWS, 2 * N)),
        2 * steps * width * slabs * rows_here,
        core,
        layer_input,
        own_w,
        other_w,
        smem=1,
    )
    pieces = lax.all_to_all(partial.astype(F16), "z", 0, 0).astype(F32)
    own_bc = call(sum_kernel, shape((steps + EXTRA_ROWS, 2 * N)), 10**6, pieces).astype(F16)
    other_bc = swap(own_bc, "yhi").astype(F32)
    own_bc = own_bc.astype(F32)

    parts = call(
        states_kernel,
        shape((slabs, 2 * share + EXTRA_ROWS, N)),
        12 * steps * N * ssd_input.shape[1],
        own_bc,
        other_bc,
        xet,
        dyft,
        ds,
    )
    shares = lax.all_to_all(parts.astype(F16), TM, 0, 0).astype(F32)
    gx, local_grad, inside = call(
        local_kernel,
        (
            shape(ssd_input.shape),
            shape((2 * steps, N)),
            shape((heads, steps)),
        ),
        10**8,
        own_bc,
        other_bc,
        ssd_input,
        out_grad,
        log_decay,
        logt,
    )
    carried = call(scan_kernel, shape(shares.shape, BF16), 10**6, shares)
    arrived = lax.all_to_all(carried, TM, 0, 0)
    own_grad = call(
        bc_grad_kernel,
        shape((2 * N, steps), BF16),
        4 * steps * N * ssd_input.shape[1],
        arrived,
        xe,
        dyf,
        local_grad,
    )
    other_grad = swap(own_grad, "yhi")
    grad_x, grad_log = call(
        finish_kernel,
        (shape(ssd_input.shape), shape((heads, steps))),
        10**8,
        arrived,
        own_bc,
        other_bc,
        ssd_input,
        out_grad,
        log_decay,
        logt,
        gx,
        inside,
    )
    copies = call(copies_kernel, shape((groups, 2 * N, steps), BF16), 10**6, own_grad, other_grad)
    all_grads = lax.all_to_all(copies, "z", 0, 0)
    late_input, _ = lax.optimization_barrier((layer_input, copies))
    near = flip(late_input, "x", 1)
    x_along = (near, flip(late_input, "x", 2), flip(near, "x", 2))
    all_grads, x_along, grad_x, grad_log = lax.optimization_barrier(
        (all_grads, x_along, grad_x, grad_log)
    )

    columns = groups // 2
    blocks = call(
        row_blocks_kernel, shape((4, 2 * columns, rows_here, steps), BF16), 10**6, all_grads
    )
    row_grads = lax.all_to_all(blocks, "x", 0, 0)
    grad_input = call(
        grad_input_kernel,
        shape(layer_input.shape, BF16),
        2 * steps * width * slabs * rows_here,
        core,
        all_grads,
        own_w,
        other_w,
        smem=1,
    )
    row_grads, grad_input = lax.optimization_barrier((row_grads, grad_input))
    keep, send = call(
        grad_weight_kernel,
        (shape((columns, rows_here, width)), shape((columns, rows_here, width), BF16)),
        2 * steps * width * slabs * rows_here,
        jnp.concatenate([core, lax.axis_index("x").reshape(1)]),
        row_grads,
        layer_input,
        *x_along,
        smem=1,
    )
    of_chip = call(chip_sum_kernel, shape(send.shape, BF16), 10**6, keep, swap(send, "core"))
    of_line = lax.all_to_all(of_chip, "ylo", 0, 0)
    grad_weight = call(line_sum_kernel, shape(proj_weight.shape), 10**6, of_line)
    return grad_x, grad_log.T, grad_input, grad_weight


def solution(mesh):
    fine = Mesh(mesh.devices.reshape(4, 4, 2, 8, 2), TM + HEADS)
    spec = P(TM, HEADS)
    return jax.shard_map(
        on_device,
        mesh=fine,
        in_specs=(spec,) * 5,
        out_specs=(spec,) * 4,
        check_vma=False,
    )
```

time: 585 us -> 182 us (0.31); the launches traced: 576 us -> 181 us
  waiting for transfers between devices: 310 us -> 31.7 us
  local copies, waits for them, and re-layouts: 70.9 us -> 14 us
  blocking collectives: 129 us -> 88.3 us
  matrix products: 27.6 us -> 0 us
  starting transfers between devices: 12.7 us -> 36.4 us
  between operations: 14.1 us -> 0.98 us
  Pallas kernels: 0 us -> 9.17 us
  other arithmetic: 8.84 us -> 0.36 us
    psum x1 -> x0, waiting for transfers between devices: 206 us -> none  [on_device(): whole_bc = lax.psum(partial_bc, 'heads')]
    all_gather x3 -> x0, blocking collectives: 129 us -> none  [the longest x1 56.8 us: on_device(): grad_bc = lax.all_gather(grad_half, 'heads', axis=1, tiled=True)]
    all_gather x4 -> x0, waiting for transfers between devices: 92.8 us -> none  [the longest x1 68.9 us: on_device(): weight_cols = lax.all_gather(proj_weight, 'tm', axis=0, tiled=True)]
    all_to_all x0 -> x5, blocking collectives: none -> 88.3 us  [the longest x2 30.9 us: to_all(): lax.all_to_all(jnp.broadcast_to(block[None], (count,) + block.shape), axi...]
    dynamic_slice x112 -> x0, local copies, waits for them, and re-layouts: 64 us -> none  [the longest x64 37.6 us: step(): new = combine(before, jax.tree.map(lambda part: part[at], everything))]
    dot_general x16 -> x0, matrix products: 24.3 us -> none  [the longest x1 3.84 us: on_device(): lax.dot_general(grad_rows, lax.all_gather(layer_input, 'tm', axis=0, tile...]
    ppermute x1 -> x7, starting transfers between devices: 4.25 us -> 22.9 us  [flip(): lax.ppermute(block, axis, [(k, k ^ bit) for k in range(lax.axis_size(axis...]
    ppermute x1 -> x7, waiting for transfers between devices: 3.41 us -> 15.8 us  [flip(): lax.ppermute(block, axis, [(k, k ^ bit) for k in range(lax.axis_size(axis...]
  transfers between devices with their start and end apart: 7 -> 10, of which waited for: 5 -> 7; matrix products, arithmetic and copies ran while one was open for 17% -> 0% of each run, Pallas kernels for 0% -> 3%
where the time goes in v1:
time: 182 us; the launch traced here: 181 us
  blocking collectives  88.3 us (49%)
  starting transfers between devices  36.4 us (20%)
  waiting for transfers between devices  31.7 us (17%)
  local copies, waits for them, and re-layouts  14 us (8%)
  Pallas kernels  9.17 us (5%)
    all_to_all x2, blocking collectives, to_all(): lax.all_to_all(jnp.broadcast_to(block[None], (count,) + block.shape), axi...  30.9 us
    all_to_all x1, blocking collectives, on_device(): pieces = lax.all_to_all(partial.astype(F16), 'z', 0, 0).astype(F32)  28.6 us
    ppermute x7, starting transfers between devices, flip(): lax.ppermute(block, axis, [(k, k ^ bit) for k in range(lax.axis_size(axis...  22.9 us
    ppermute x7, waiting for transfers between devices, flip(): lax.ppermute(block, axis, [(k, k ^ bit) for k in range(lax.axis_size(axis...  15.8 us
    all_to_all x1, blocking collectives, on_device(): shares = lax.all_to_all(parts.astype(F16), TM, 0, 0).astype(F32)  15.6 us
    all_to_all x1, blocking collectives, on_device(): of_line = lax.all_to_all(of_chip, 'ylo', 0, 0)  13.2 us
    unnamed x53, local copies, waits for them, and re-layouts  13 us
    pallas_call x14, Pallas kernels, call(): pl.pallas_call(body, out_shape=outs, in_specs=[pl.BlockSpec(memory_space=...  9.17 us
  transfers between devices with their start and end apart: 10, of which 7 were waited for; matrix products, arithmetic and copies ran while one was open for 0% of the time, Pallas kernels for 3%

profile of v1, /device:TPU:56, one launch (start us, length us, event | category | flops | bytes accessed | tf_op | source)
XLA Modules:
  0.0 180.9 jit_solution(11346140598873573313)
XLA Ops:
  0.6 0.9 broadcast_in_dim.4
  1.5 12.1 %all_to_all.40 = bf16[4,64,512]{2,1,0:T(8,128)(2,1)S(1)} all-to-all(bf16[4,64,512]{2,1,0:T(8,128)(2,1)S(1)} %broadcast_in_dim.4), channel_id=1, replica_groups=mesh['ylo'=4,'x'=4,'core'=2,'z'=8,'yhi'=2] {'ylo'}, dimensions={0} | all-to-all | bytes 524288 | tf_op jit(solution)/shard_map/all_to_all | solution.py:363
  13.6 0.1 broadcast_in_dim.5
  13.7 0.0 copy-start.9
  13.7 18.9 %all_to_all.41 = bf16[4,4,64,512]{3,2,1,0:T(8,128)(2,1)S(1)} all-to-all(bf16[4,4,64,512]{3,2,1,0:T(8,128)(2,1)S(1)} %broadcast_in_dim.5), channel_id=1, replica_groups=mesh['ylo'=4,'x'=4,'core'=2,'z'=8,'yhi'=2] {'x'}, dimensions={0} | all-to-all | bytes 2097152 | tf_op jit(solution)/shard_map/all_to_all | solution.py:363
  32.6 1.9 %collective-permute-start = (bf16[16,64,512]{2,1,0:T(8,128)(2,1)S(1)}, bf16[16,64,512]{2,1,0:T(8,128)(2,1)S(1)}, u32[]{:S(2)}, u32[]{:S(2)}) collective-permute-start(bf16[16,64,512]{2,1,0:T(8,128)(2,1)S(1)} %bitcast.5), channel_id=1, source_target_pairs={{0,16},{16,0},{1,17},{17,1},{2,18},{18,2},{3,19},{19,3},{4,20},{20... | collective-permute-start | bytes 3145736 | tf_op jit(solution)/shard_map/ppermute | solution.py:367
  34.5 2.6 %collective-permute-done.refs_3_ = bf16[16,64,512]{2,1,0:T(8,128)(2,1)S(1)} collective-permute-done((bf16[16,64,512]{2,1,0:T(8,128)(2,1)S(1)}, bf16[16,64,512]{2,1,0:T(8,128)(2,1)S(1)}, u32[]{:S(2)}, u32[]{:S(2)}) %collective-permute-start) | collective-permute-done | bytes 1048608 | tf_op jit(solution)/shard_map/ppermute | solution.py:367
  37.1 1.0 shard_map.84
  38.1 0.1 convert_element_type.21
  38.2 28.6 %all_to_all.42 = f16[8,136,256]{2,1,0:T(8,128)(2,1)S(1)} all-to-all(f16[8,136,256]{2,1,0:T(8,128)(2,1)S(1)} %convert_element_type.21), channel_id=1, replica_groups=mesh['ylo'=4,'x'=4,'core'=2,'z'=8,'yhi'=2] {'z'}, dimensions={0} | all-to-all | bytes 1114112 | tf_op jit(solution)/shard_map/all_to_all | solution.py:412
  66.8 0.1 convert_element_type.22.refs_0_
  66.9 0.0 copy-start.25
  66.9 0.0 copy-start
  66.9 0.0 copy-start.1
  66.9 0.1 shard_map.85
  67.0 0.0 copy-start.2
  67.1 4.0 %collective-permute-start.1 = (f16[136,256]{1,0:T(8,128)(2,1)S(1)}, f16[136,256]{1,0:T(8,128)(2,1)S(1)}, u32[]{:S(2)}, u32[]{:S(2)}) collective-permute-start(f16[136,256]{1,0:T(8,128)(2,1)S(1)} %get-tuple-element.47), channel_id=1, source_target_pairs={{0,1},{1,0},{2,3},{3,2},{4,5},{5,4},{6,7},{7,6},{8,9},{9,8},{10,11... | collective-permute-start | bytes 208904 | tf_op jit(solution)/shard_map/ppermute | solution.py:367
  71.1 0.1 copy.9.refs_2_.refs_4_.refs_5_
  71.2 0.0 copy-done
  71.2 0.9 shard_map.86
  72.1 0.7 copy-done.15
  72.8 4.5 %collective-permute-done.1 = f16[136,256]{1,0:T(8,128)(2,1)S(1)} collective-permute-done((f16[136,256]{1,0:T(8,128)(2,1)S(1)}, f16[136,256]{1,0:T(8,128)(2,1)S(1)}, u32[]{:S(2)}, u32[]{:S(2)}) %collective-permute-start.1) | collective-permute-done | bytes 69664 | tf_op jit(solution)/shard_map/ppermute | solution.py:367
  77.3 0.6 shard_map.87
  78.0 15.6 %all_to_all.43 = f16[32,40,128]{2,1,0:T(8,128)(2,1)S(1)} all-to-all(f16[32,40,128]{2,1,0:T(8,128)(2,1)S(1)} %convert_element_type.26), channel_id=1, replica_groups=mesh['ylo'=4,'x'=4,'core'=2,'z'=8,'yhi'=2] {'ylo','x','core'}, dimensions={0} | all-to-all | bytes 655360 | tf_op jit(solution)/shard_map/all_to_all | solution.py:427
  93.6 0.2 shard_map.88
  93.8 0.7 copy-done.8
  94.5 6.5 %all-to-all-start.4 = ((bf16[32,40,128]{2,1,0:T(8,128)(2,1)}), bf16[32,40,128]{2,1,0:T(8,128)(2,1)S(1)}, u32[]{:S(2)}, u32[]{:S(2)}) async-start(bf16[32,40,128]{2,1,0:T(8,128)(2,1)} %copy-done.8), calls=%async_computation.4 | async-start | bytes 655360 | tf_op jit(solution)/shard_map/all_to_all | solution.py:444
  101.0 0.9 shard_map.89
  102.0 0.7 copy-done.11
  102.7 0.6 copy-done.17
  103.3 7.5 %all-to-all-done.4.refs_0_ = bf16[32,40,128]{2,1,0:T(8,128)(2,1)S(1)} async-done(((bf16[32,40,128]{2,1,0:T(8,128)(2,1)}), bf16[32,40,128]{2,1,0:T(8,128)(2,1)S(1)}, u32[]{:S(2)}, u32[]{:S(2)}) %all-to-all-start.4) | async-done | bytes 327712 | tf_op jit(solution)/shard_map/all_to_all | solution.py:444
  110.9 0.9 copy-done.14
  111.8 0.9 copy-done.16
  112.7 0.9 copy-done.18
  113.6 0.3 shard_map.90.refs_0_
  113.9 4.2 %collective-permute-start.2 = (bf16[256,128]{1,0:T(8,128)(2,1)S(1)}, bf16[256,128]{1,0:T(8,128)(2,1)S(1)}, u32[]{:S(2)}, u32[]{:S(2)}) collective-permute-start(bf16[256,128]{1,0:T(8,128)(2,1)S(1)} %shard_map.90.refs_0_), channel_id=1, source_target_pairs={{0,1},{1,0},{2,3},{3,2},{4,5},{5,4},{6,7},{7,6},{8,9},{9,8},{10,11... | collective-permute-start | bytes 196616 | tf_op jit(solution)/shard_map/ppermute | solution.py:367
  118.1 7.0 %collective-permute-done.2.refs_1_ = bf16[256,128]{1,0:T(8,128)(2,1)S(1)} collective-permute-done((bf16[256,128]{1,0:T(8,128)(2,1)S(1)}, bf16[256,128]{1,0:T(8,128)(2,1)S(1)}, u32[]{:S(2)}, u32[]{:S(2)}) %collective-permute-start.2) | collective-permute-done | bytes 65568 | tf_op jit(solution)/shard_map/ppermute | solution.py:367
  125.2 0.8 copy-done.6
  126.0 3.5 %all-to-all-start.5 = ((bf16[8,256,128]{2,1,0:T(8,128)(2,1)}), bf16[8,256,128]{2,1,0:T(8,128)(2,1)S(1)}, u32[]{:S(2)}, u32[]{:S(2)}) async-start(bf16[8,256,128]{2,1,0:T(8,128)(2,1)} %copy-done.6), calls=%async_computation.5 | async-start | bytes 1048576 | tf_op jit(solution)/shard_map/all_to_all | solution.py:470
  129.5 2.3 %collective-permute-start.3 = (bf16[128,512]{1,0:T(8,128)(2,1)}, bf16[128,512]{1,0:T(8,128)(2,1)S(1)}, u32[]{:S(2)}, u32[]{:S(2)}) collective-permute-start(bf16[128,512]{1,0:T(8,128)(2,1)} %refs_2_.4), channel_id=1, source_target_pairs={{0,32},{32,0},{64,96},{96,64},{1,33},{33,1},{65,97},{97,65},{2,34}... | collective-permute-start | bytes 393224 | tf_op jit(solution)/shard_map/ppermute | solution.py:367
  131.8 4.6 %collective-permute-start.4 = (bf16[128,512]{1,0:T(8,128)(2,1)}, bf16[128,512]{1,0:T(8,128)(2,1)S(1)}, u32[]{:S(2)}, u32[]{:S(2)}) collective-permute-start(bf16[128,512]{1,0:T(8,128)(2,1)} %refs_2_.4), channel_id=1, source_target_pairs={{0,64},{32,96},{64,0},{96,32},{1,65},{33,97},{65,1},{97,33},{2,66}... | collective-permute-start | bytes 393224 | tf_op jit(solution)/shard_map/ppermute | solution.py:367
  136.4 0.1 collective-permute-done.3.refs_3_
  136.6 3.9 %collective-permute-start.5 = (bf16[128,512]{1,0:T(8,128)(2,1)S(1)}, bf16[128,512]{1,0:T(8,128)(2,1)S(1)}, u32[]{:S(2)}, u32[]{:S(2)}) collective-permute-start(bf16[128,512]{1,0:T(8,128)(2,1)S(1)} %collective-permute-done.3.refs_3_), channel_id=1, source_target_pairs={{0,64},{32,96},{64,0},{96,32},{1,65},{33,97},{65,1},{97,33},{2,66}... | collective-permute-start | bytes 393224 | tf_op jit(solution)/shard_map/ppermute | solution.py:367
  140.5 0.9 copy-done.3
  141.4 0.9 copy-done.5
  142.3 0.9 copy-done.12
  143.3 2.2 %shard_map.92 = (f32[128,512]{1,0:T(8,128)}, f32[8,128]{1,0:T(8,128)}) custom-call(bf16[32,40,128]{2,1,0:T(8,128)(2,1)S(1)} %all-to-all-done.4.refs_0_, f32[136,256]{1,0:T(8,128)S(1)} %copy-done.3, f32[136,256]{1,0:T(8,128)S(1)} %copy-done.5, f32[128,512]{1,0:T(8,128)S(1)} %copy-done, f32[128,512]{1,0:T(8,128)S(1)} %copy-done.1, ...), custom_call_target="tpu_custom_call" | custom-call | flops 100000000 | bytes 1671168 | tf_op jit(solution)/shard_map/pallas_call | solution.py:105
  145.5 0.0 collective-permute-done.4.refs_4_
  145.5 0.6 copy-done.21
  146.1 0.0 collective-permute-done.5.refs_5_
  146.1 0.7 copy-done.23
  146.8 0.0 all-to-all-done.5.refs_0_.refs_1_
  146.8 0.8 copy-done.7
  147.6 3.5 %all-to-all-start.6 = ((bf16[4,8,64,128]{3,2,1,0:T(8,128)(2,1)}), bf16[4,8,64,128]{3,2,1,0:T(8,128)(2,1)S(1)}, u32[]{:S(2)}, u32[]{:S(2)}) async-start(bf16[4,8,64,128]{3,2,1,0:T(8,128)(2,1)} %copy-done.7), calls=%async_computation.6 | async-start | bytes 1048576 | tf_op jit(solution)/shard_map/all_to_all | solution.py:482
  151.1 0.1 pad_add_fusion.refs_0_
  151.2 1.1 shard_map.94
  152.3 8.4 %all-to-all-done.6.refs_1_ = bf16[4,8,64,128]{3,2,1,0:T(8,128)(2,1)S(1)} async-done(((bf16[4,8,64,128]{3,2,1,0:T(8,128)(2,1)}), bf16[4,8,64,128]{3,2,1,0:T(8,128)(2,1)S(1)}, u32[]{:S(2)}, u32[]{:S(2)}) %all-to-all-start.6) | async-done | bytes 524320 | tf_op jit(solution)/shard_map/all_to_all | solution.py:482
  160.7 0.9 copy-done.22
  161.6 0.9 copy-done.24
  162.5 1.0 shard_map.95
  163.5 1.9 %collective-permute-start.6 = (bf16[4,64,512]{2,1,0:T(8,128)(2,1)S(1)}, bf16[4,64,512]{2,1,0:T(8,128)(2,1)S(1)}, u32[]{:S(2)}, u32[]{:S(2)}) collective-permute-start(bf16[4,64,512]{2,1,0:T(8,128)(2,1)S(1)} %get-tuple-element.45), channel_id=1, source_target_pairs={{0,16},{16,0},{1,17},{17,1},{2,18},{18,2},{3,19},{19,3},{4,20},{20... | collective-permute-start | bytes 786440 | tf_op jit(solution)/shard_map/ppermute | solution.py:367
  165.4 1.5 collective-permute-done.6.refs_1_
  167.0 13.2 %all_to_all.44.refs_0_ = bf16[4,64,512]{2,1,0:T(8,128)(2,1)S(1)} all-to-all(bf16[4,64,512]{2,1,0:T(8,128)(2,1)S(1)} %shard_map.96), channel_id=1, replica_groups=mesh['ylo'=4,'x'=4,'core'=2,'z'=8,'yhi'=2] {'ylo'}, dimensions={0} | all-to-all | bytes 524288 | tf_op jit(solution)/shard_map/all_to_all | solution.py:505
  180.2 0.7 shard_map.97
  (37 shorter events, 0.3 us)
Async XLA Ops:
  13.7 23.4 %copy-start.9 = (bf16[128,512]{1,0:T(8,128)(2,1)S(1)}, bf16[128,512]{1,0:T(8,128)(2,1)}, u32[]{:S(2)}) copy-start(bf16[128,512]{1,0:T(8,128)(2,1)} %refs_2_.4) | copy-start | bytes 393220
  32.6 4.5 %collective-permute-start = (bf16[16,64,512]{2,1,0:T(8,128)(2,1)S(1)}, bf16[16,64,512]{2,1,0:T(8,128)(2,1)S(1)}, u32[]{:S(2)}, u32[]{:S(2)}) collective-permute-start(bf16[16,64,512]{2,1,0:T(8,128)(2,1)S(1)} %bitcast.5), channel_id=1, source_target_pairs={{0,16},{16,0},{1,17},{17,1},{2,18},{18,2},{3,19},{19,3},{4,20},{20... | collective-permute-start | bytes 3145736 | tf_op jit(solution)/shard_map/ppermute | solution.py:367
  66.9 4.2 %copy-start.25 = (f32[128,8]{0,1:T(8,128)S(1)}, f32[128,8]{0,1:T(8,128)}, u32[]{:S(2)}) copy-start(f32[128,8]{0,1:T(8,128)} %param.8) | copy-start | bytes 12292
  66.9 4.3 %copy-start = (f32[128,512]{1,0:T(8,128)S(1)}, f32[128,512]{1,0:T(8,128)}, u32[]{:S(2)}) copy-start(f32[128,512]{1,0:T(8,128)} %refs_3_.3) | copy-start | bytes 786436
  66.9 4.3 %copy-start.1 = (f32[128,512]{1,0:T(8,128)S(1)}, f32[128,512]{1,0:T(8,128)}, u32[]{:S(2)}) copy-start(f32[128,512]{1,0:T(8,128)} %refs_4_.2) | copy-start | bytes 786436
  67.0 34.0 %copy-start.2 = (f32[136,256]{1,0:T(8,128)}, f32[136,256]{1,0:T(8,128)S(1)}, u32[]{:S(2)}) copy-start(f32[136,256]{1,0:T(8,128)S(1)} %get-tuple-element.46.refs_0_.refs_1_) | copy-start | bytes 417796
  67.1 10.2 %collective-permute-start.1 = (f16[136,256]{1,0:T(8,128)(2,1)S(1)}, f16[136,256]{1,0:T(8,128)(2,1)S(1)}, u32[]{:S(2)}, u32[]{:S(2)}) collective-permute-start(f16[136,256]{1,0:T(8,128)(2,1)S(1)} %get-tuple-element.47), channel_id=1, source_target_pairs={{0,1},{1,0},{2,3},{3,2},{4,5},{5,4},{6,7},{7,6},{8,9},{9,8},{10,11... | collective-permute-start | bytes 208904 | tf_op jit(solution)/shard_map/ppermute | solution.py:367
  72.1 0.7 copy-start.15
  72.8 4.5 %copy-start.13 = (bf16[128,512]{1,0:T(8,128)(2,1)}, bf16[128,512]{1,0:T(8,128)(2,1)S(1)}, u32[]{:S(2)}) copy-start(bf16[128,512]{1,0:T(8,128)(2,1)S(1)} %get-tuple-element.28.refs_1_) | copy-start | bytes 393220
  77.3 23.7 %copy-start.4 = (f32[136,256]{1,0:T(8,128)}, f32[136,256]{1,0:T(8,128)S(1)}, u32[]{:S(2)}) copy-start(f32[136,256]{1,0:T(8,128)S(1)} %convert_element_type.25.refs_1_.refs_2_) | copy-start | bytes 417796
  93.8 0.7 copy-start.8
  94.5 16.3 %all-to-all-start.4 = ((bf16[32,40,128]{2,1,0:T(8,128)(2,1)}), bf16[32,40,128]{2,1,0:T(8,128)(2,1)S(1)}, u32[]{:S(2)}, u32[]{:S(2)}) async-start(bf16[32,40,128]{2,1,0:T(8,128)(2,1)} %copy-done.8), calls=%async_computation.4 | async-start | bytes 655360 | tf_op jit(solution)/shard_map/all_to_all | solution.py:444
  102.0 0.7 copy-start.11
  102.7 0.6 copy-start.17
  110.9 0.9 copy-start.14
  111.8 0.9 copy-start.16
  112.7 0.9 copy-start.18
  113.9 11.3 %collective-permute-start.2 = (bf16[256,128]{1,0:T(8,128)(2,1)S(1)}, bf16[256,128]{1,0:T(8,128)(2,1)S(1)}, u32[]{:S(2)}, u32[]{:S(2)}) collective-permute-start(bf16[256,128]{1,0:T(8,128)(2,1)S(1)} %shard_map.90.refs_0_), channel_id=1, source_target_pairs={{0,1},{1,0},{2,3},{3,2},{4,5},{5,4},{6,7},{7,6},{8,9},{9,8},{10,11... | collective-permute-start | bytes 196616 | tf_op jit(solution)/shard_map/ppermute | solution.py:367
  125.2 0.8 copy-start.6
  126.0 20.8 %all-to-all-start.5 = ((bf16[8,256,128]{2,1,0:T(8,128)(2,1)}), bf16[8,256,128]{2,1,0:T(8,128)(2,1)S(1)}, u32[]{:S(2)}, u32[]{:S(2)}) async-start(bf16[8,256,128]{2,1,0:T(8,128)(2,1)} %copy-done.6), calls=%async_computation.5 | async-start | bytes 1048576 | tf_op jit(solution)/shard_map/all_to_all | solution.py:470
  129.5 7.1 %collective-permute-start.3 = (bf16[128,512]{1,0:T(8,128)(2,1)}, bf16[128,512]{1,0:T(8,128)(2,1)S(1)}, u32[]{:S(2)}, u32[]{:S(2)}) collective-permute-start(bf16[128,512]{1,0:T(8,128)(2,1)} %refs_2_.4), channel_id=1, source_target_pairs={{0,32},{32,0},{64,96},{96,64},{1,33},{33,1},{65,97},{97,65},{2,34}... | collective-permute-start | bytes 393224 | tf_op jit(solution)/shard_map/ppermute | solution.py:367
  131.8 13.7 %collective-permute-start.4 = (bf16[128,512]{1,0:T(8,128)(2,1)}, bf16[128,512]{1,0:T(8,128)(2,1)S(1)}, u32[]{:S(2)}, u32[]{:S(2)}) collective-permute-start(bf16[128,512]{1,0:T(8,128)(2,1)} %refs_2_.4), channel_id=1, source_target_pairs={{0,64},{32,96},{64,0},{96,32},{1,65},{33,97},{65,1},{97,33},{2,66}... | collective-permute-start | bytes 393224 | tf_op jit(solution)/shard_map/ppermute | solution.py:367
  136.6 8.9 %copy-start.19 = (bf16[128,512]{1,0:T(8,128)(2,1)}, bf16[128,512]{1,0:T(8,128)(2,1)S(1)}, u32[]{:S(2)}) copy-start(bf16[128,512]{1,0:T(8,128)(2,1)S(1)} %collective-permute-done.3.refs_3_) | copy-start | bytes 393220
  136.6 9.6 %collective-permute-start.5 = (bf16[128,512]{1,0:T(8,128)(2,1)S(1)}, bf16[128,512]{1,0:T(8,128)(2,1)S(1)}, u32[]{:S(2)}, u32[]{:S(2)}) collective-permute-start(bf16[128,512]{1,0:T(8,128)(2,1)S(1)} %collective-permute-done.3.refs_3_), channel_id=1, source_target_pairs={{0,64},{32,96},{64,0},{96,32},{1,65},{33,97},{65,1},{97,33},{2,66}... | collective-permute-start | bytes 393224 | tf_op jit(solution)/shard_map/ppermute | solution.py:367
  140.5 0.9 copy-start.3
  141.4 0.9 copy-start.5
  142.3 0.9 copy-start.12
  145.5 0.6 copy-start.21
  146.1 0.7 copy-start.23
  146.8 0.8 copy-start.7
  147.6 13.1 %all-to-all-start.6 = ((bf16[4,8,64,128]{3,2,1,0:T(8,128)(2,1)}), bf16[4,8,64,128]{3,2,1,0:T(8,128)(2,1)S(1)}, u32[]{:S(2)}, u32[]{:S(2)}) async-start(bf16[4,8,64,128]{3,2,1,0:T(8,128)(2,1)} %copy-done.7), calls=%async_computation.6 | async-start | bytes 1048576 | tf_op jit(solution)/shard_map/all_to_all | solution.py:482
  151.2 9.5 %copy-start.10 = (bf16[128,512]{1,0:T(8,128)(2,1)S(1)}, bf16[128,512]{1,0:T(8,128)(2,1)}, u32[]{:S(2)}) copy-start(bf16[128,512]{1,0:T(8,128)(2,1)} %refs_2_.4) | copy-start | bytes 393220
  151.2 9.5 %copy-start.20 = (bf16[128,512]{1,0:T(8,128)(2,1)S(1)}, bf16[128,512]{1,0:T(8,128)(2,1)}, u32[]{:S(2)}) copy-start(bf16[128,512]{1,0:T(8,128)(2,1)} %copy-done.19) | copy-start | bytes 393220
  160.7 0.9 copy-start.22
  161.6 0.9 copy-start.24
  163.5 3.4 %collective-permute-start.6 = (bf16[4,64,512]{2,1,0:T(8,128)(2,1)S(1)}, bf16[4,64,512]{2,1,0:T(8,128)(2,1)S(1)}, u32[]{:S(2)}, u32[]{:S(2)}) collective-permute-start(bf16[4,64,512]{2,1,0:T(8,128)(2,1)S(1)} %get-tuple-element.45), channel_id=1, source_target_pairs={{0,16},{16,0},{1,17},{17,1},{2,18},{18,2},{3,19},{19,3},{4,20},{20... | collective-permute-start | bytes 786440 | tf_op jit(solution)/shard_map/ppermute | solution.py:367

commit v2 on v1

--- a/solution.py
+++ b/solution.py
@@ -75,39 +75,16 @@
     return ((col >= row * size) & (col < (row + 1) * size)).astype(F32)
 
 
-def call(kernel, outs, flops, *args, smem=0, late=()):
-    several = isinstance(outs, tuple)
-    out_list = outs if several else (outs,)
+def call(kernel, outs, flops, *args, smem=0):
+    out_list = outs if isinstance(outs, tuple) else (outs,)
     read = sum(a.size * a.dtype.itemsize for a in args)
     wrote = sum(o.size * o.dtype.itemsize for o in out_list)
     spaces = [pltpu.SMEM if k < smem else pltpu.VMEM for k in range(len(args))]
-    for k in late:
-        spaces[k] = pl.ANY
-    scratch = [pltpu.VMEM(args[k].shape, args[k].dtype) for k in late]
-    if late:
-        scratch.append(pltpu.SemaphoreType.DMA((len(late),)))
-
-    def body(*refs):
-        refs = list(refs)
-        buffers = refs[len(args) + len(out_list) :]
-        copies = [
-            pltpu.make_async_copy(refs[k], buffers[i], buffers[-1].at[i])
-            for i, k in enumerate(late)
-        ]
-        for copy in copies:
-            copy.start()
-        for copy in copies:
-            copy.wait()
-        for i, k in enumerate(late):
-            refs[k] = buffers[i]
-        kernel(*refs[: len(args) + len(out_list)])
-
     return pl.pallas_call(
-        body,
+        kernel,
         out_shape=outs,
         in_specs=[pl.BlockSpec(memory_space=space) for space in spaces],
         out_specs=jax.tree.map(lambda _: pl.BlockSpec(memory_space=pltpu.VMEM), outs),
-        scratch_shapes=scratch,
         cost_estimate=pl.CostEstimate(
             flops=flops, bytes_accessed=read + wrote, transcendentals=0
         ),
@@ -128,16 +105,12 @@
     return dot(jnp.exp(last - cum), spread, HIGHEST), dot(jnp.exp(cum), spread, HIGHEST)
 
 
-def prepare(x_ref, dy_ref, log_ref, logt_ref, xe_ref, dyf_ref, xet_ref, dyft_ref, ds_ref):
+def prepare(x_ref, dy_ref, log_ref, logt_ref, xet_ref, dyft_ref, ds_ref):
     steps = log_ref.shape[0]
     cum, cumt = decay_sums(log_ref, logt_ref)
     to_end, from_start = decay_factors(cum, x_ref.shape[1])
-    xe = x_ref[...] * to_end
-    dyf = dy_ref[...] * from_start
-    xe_ref[...] = xe.astype(BF16)
-    dyf_ref[...] = dyf.astype(BF16)
-    xet_ref[...] = xe.T
-    dyft_ref[...] = dyf.T
+    xet_ref[...] = (x_ref[...] * to_end).T
+    dyft_ref[...] = (dy_ref[...] * from_start).T
     ds_ref[...] = jnp.broadcast_to(cumt[:, steps - 1 : steps], ds_ref.shape)
 
 
@@ -209,7 +182,7 @@
             out_ref[part, 2 * half :, :] = terms
 
 
-def local_kernel(own_ref, other_ref, x_ref, dy_ref, log_ref, logt_ref, gx_ref, grad_ref, inside_ref):
+def local_kernel(own_ref, other_ref, x_ref, dy_ref, log_ref, logt_ref, gx_ref, terms_ref, inside_ref):
     b_rows, c_rows = (rows.astype(BF16) for rows in whole_bc(own_ref, other_ref))
     steps, heads = log_ref.shape
     size = x_ref.shape[1] // heads
@@ -229,8 +202,12 @@
         gx_ref[:, h * size : (h + 1) * size] = dot((decay * bct).astype(BF16), dy)
         reach = dot((decayed * bct).astype(BF16), at_or_after)
         inside_ref[h : h + 1, :] = jnp.sum(jnp.where(row < col, reach, 0.0), axis=0, keepdims=True)
-    grad_ref[:steps] = dot(pair_sum.astype(BF16), c_rows)
-    grad_ref[steps:] = dot(pair_sum.T.astype(BF16), b_rows)
+    width = x_ref.shape[1]
+    to_end, from_start = decay_factors(cum, width)
+    terms_ref[:, :width] = x_ref[...] * to_end
+    terms_ref[:, width : 2 * width] = dy_ref[...] * from_start
+    terms_ref[:, 2 * width : 2 * width + N] = dot(pair_sum.astype(BF16), c_rows)
+    terms_ref[:, 2 * width + N :] = dot(pair_sum.T.astype(BF16), b_rows)
 
 
 def scan_kernel(parts_ref, out_ref):
@@ -263,11 +240,13 @@
     return state, grad
 
 
-def bc_grad_kernel(in_ref, xe_ref, dyf_ref, local_ref, out_ref):
+def bc_grad_kernel(in_ref, terms_ref, out_ref):
     state, grad = entering(in_ref)
-    steps = xe_ref.shape[0]
-    out_ref[:N, :] = (local_ref[:steps] + dot(xe_ref[...], grad)).T.astype(BF16)
-    out_ref[N:, :] = (local_ref[steps:] + dot(dyf_ref[...], state)).T.astype(BF16)
+    width = state.shape[0]
+    from_grad = dot(terms_ref[:, :width].astype(BF16), grad)
+    from_state = dot(terms_ref[:, width : 2 * width].astype(BF16), state)
+    out_ref[:N, :] = (terms_ref[:, 2 * width : 2 * width + N] + from_grad).T.astype(BF16)
+    out_ref[N:, :] = (terms_ref[:, 2 * width + N :] + from_state).T.astype(BF16)
 
 
 def finish_kernel(in_ref, own_ref, other_ref, x_ref, dy_ref, log_ref, logt_ref, gx_ref, inside_ref, out_ref, out_log_ref):
@@ -317,11 +296,17 @@
                 out_ref[2 * high + k, 2 * column + core] = grads_ref[group, at : at + rows, :]
 
 
-def grad_weight_kernel(place_ref, grads_ref, x0_ref, x1_ref, x2_ref, x3_ref, keep_ref, send_ref):
+def stack_kernel(x0_ref, x1_ref, x2_ref, x3_ref, out_ref):
+    steps = x0_ref.shape[0]
+    for k, ref in enumerate((x0_ref, x1_ref, x2_ref, x3_ref)):
+        out_ref[k * steps : (k + 1) * steps, :] = ref[...]
+
+
+def grad_weight_kernel(place_ref, grads_ref, x_ref, keep_ref, send_ref):
     first = place_ref[0] == 0
     line = place_ref[1]
     columns, rows, width = keep_ref.shape
-    x = jnp.concatenate([ref[...] for ref in (x0_ref, x1_ref, x2_ref, x3_ref)], axis=0)
+    x = x_ref[...]
     for column in range(columns):
         grads = jnp.concatenate(
             [
@@ -384,11 +369,9 @@
     line_w = to_all(proj_weight, "ylo")
     own_w = to_all(line_w, "x").reshape(-1, rows_here, width)
     other_w = swap(own_w, "core")
-    xe, dyf, xet, dyft, ds = call(
+    xet, dyft, ds = call(
         prepare,
         (
-            shape(ssd_input.shape, BF16),
-            shape(ssd_input.shape, BF16),
             shape(ssd_input.shape[::-1]),
             shape(ssd_input.shape[::-1]),
             shape((heads, N)),
@@ -425,11 +408,11 @@
         ds,
     )
     shares = lax.all_to_all(parts.astype(F16), TM, 0, 0).astype(F32)
-    gx, local_grad, inside = call(
+    gx, terms, inside = call(
         local_kernel,
         (
             shape(ssd_input.shape),
-            shape((2 * steps, N)),
+            shape((steps, 2 * (ssd_input.shape[1] + N))),
             shape((heads, steps)),
         ),
         10**8,
@@ -447,9 +430,7 @@
         shape((2 * N, steps), BF16),
         4 * steps * N * ssd_input.shape[1],
         arrived,
-        xe,
-        dyf,
-        local_grad,
+        terms,
     )
     other_grad = swap(own_grad, "yhi")
     grad_x, grad_log = call(
@@ -466,14 +447,21 @@
         gx,
         inside,
     )
+    other_grad, grad_x, grad_log = lax.optimization_barrier((other_grad, grad_x, grad_log))
     copies = call(copies_kernel, shape((groups, 2 * N, steps), BF16), 10**6, own_grad, other_grad)
     all_grads = lax.all_to_all(copies, "z", 0, 0)
     late_input, _ = lax.optimization_barrier((layer_input, copies))
     near = flip(late_input, "x", 1)
-    x_along = (near, flip(late_input, "x", 2), flip(near, "x", 2))
-    all_grads, x_along, grad_x, grad_log = lax.optimization_barrier(
-        (all_grads, x_along, grad_x, grad_log)
-    )
+    x_along = call(
+        stack_kernel,
+        shape((4 * steps, width), BF16),
+        10**6,
+        late_input,
+        near,
+        flip(late_input, "x", 2),
+        flip(near, "x", 2),
+    )
+    all_grads, x_along = lax.optimization_barrier((all_grads, x_along))
 
     columns = groups // 2
     blocks = call(
@@ -497,8 +485,7 @@
         2 * steps * width * slabs * rows_here,
         jnp.concatenate([core, lax.axis_index("x").reshape(1)]),
         row_grads,
-        layer_input,
-        *x_along,
+        x_along,
         smem=1,
     )
     of_chip = call(chip_sum_kernel, shape(send.shape, BF16), 10**6, keep, swap(send, "core"))

time: 182 us -> 180 us (0.989)
  local copies, waits for them, and re-layouts: 14 us -> 4.52 us
  waiting for transfers between devices: 31.7 us -> 35.5 us
  Pallas kernels: 9.17 us -> 11.6 us
    unnamed x53 -> x19, local copies, waits for them, and re-layouts: 13 us -> 3.56 us
    ppermute x7, waiting for transfers between devices: 15.8 us -> 18.7 us  [flip(): lax.ppermute(block, axis, [(k, k ^ bit) for k in range(lax.axis_size(axis...]
    pallas_call x14 -> x15, Pallas kernels: 9.17 us -> 11.6 us  [call(): pl.pallas_call(kernel, out_shape=outs, in_specs=[pl.BlockSpec(memory_spac...]
  transfers between devices with their start and end apart: 10 -> 10, of which waited for: 7 -> 9; matrix products, arithmetic and copies ran while one was open for 0% -> 0% of each run, Pallas kernels for 3% -> 3%
where the time goes in v2:
time: 180 us; the launch traced here: 179 us
  blocking collectives  89 us (49%)
  starting transfers between devices  37 us (21%)
  waiting for transfers between devices  35.5 us (20%)
  Pallas kernels  11.6 us (6%)
  local copies, waits for them, and re-layouts  4.52 us (3%)
    all_to_all x2, blocking collectives, to_all(): lax.all_to_all(jnp.broadcast_to(block[None], (count,) + block.shape), axi...  30.9 us
    all_to_all x1, blocking collectives, on_device(): pieces = lax.all_to_all(partial.astype(F16), 'z', 0, 0).astype(F32)  28.6 us
    ppermute x7, starting transfers between devices, flip(): lax.ppermute(block, axis, [(k, k ^ bit) for k in range(lax.axis_size(axis...  22.9 us
    ppermute x7, waiting for transfers between devices, flip(): lax.ppermute(block, axis, [(k, k ^ bit) for k in range(lax.axis_size(axis...  18.7 us
    all_to_all x1, blocking collectives, on_device(): shares = lax.all_to_all(parts.astype(F16), TM, 0, 0).astype(F32)  15.6 us
    all_to_all x1, blocking collectives, on_device(): of_line = lax.all_to_all(of_chip, 'ylo', 0, 0)  13.9 us
    pallas_call x15, Pallas kernels, call(): pl.pallas_call(kernel, out_shape=outs, in_specs=[pl.BlockSpec(memory_spac...  11.6 us
    all_to_all x1, waiting for transfers between devices, on_device(): row_grads = lax.all_to_all(blocks, 'x', 0, 0)  8.27 us
  transfers between devices with their start and end apart: 10, of which 9 were waited for; matrix products, arithmetic and copies ran while one was open for 0% of the time, Pallas kernels for 3%

profile of v2, /device:TPU:56, one launch (start us, length us, event | category | flops | bytes accessed | tf_op | source)
XLA Modules:
  0.0 178.9 jit_solution(12728208878770329903)
XLA Ops:
  0.6 0.9 broadcast_in_dim.4
  1.5 12.1 %all_to_all.40 = bf16[4,64,512]{2,1,0:T(8,128)(2,1)S(1)} all-to-all(bf16[4,64,512]{2,1,0:T(8,128)(2,1)S(1)} %broadcast_in_dim.4), channel_id=1, replica_groups=mesh['ylo'=4,'x'=4,'core'=2,'z'=8,'yhi'=2] {'ylo'}, dimensions={0} | all-to-all | bytes 524288 | tf_op jit(solution)/shard_map/all_to_all | solution.py:348
  13.6 0.1 broadcast_in_dim.5
  13.7 0.0 copy-start.5
  13.7 18.9 %all_to_all.41 = bf16[4,4,64,512]{3,2,1,0:T(8,128)(2,1)S(1)} all-to-all(bf16[4,4,64,512]{3,2,1,0:T(8,128)(2,1)S(1)} %broadcast_in_dim.5), channel_id=1, replica_groups=mesh['ylo'=4,'x'=4,'core'=2,'z'=8,'yhi'=2] {'x'}, dimensions={0} | all-to-all | bytes 2097152 | tf_op jit(solution)/shard_map/all_to_all | solution.py:348
  32.6 1.9 %collective-permute-start = (bf16[16,64,512]{2,1,0:T(8,128)(2,1)S(1)}, bf16[16,64,512]{2,1,0:T(8,128)(2,1)S(1)}, u32[]{:S(2)}, u32[]{:S(2)}) collective-permute-start(bf16[16,64,512]{2,1,0:T(8,128)(2,1)S(1)} %bitcast.5), channel_id=1, source_target_pairs={{0,16},{16,0},{1,17},{17,1},{2,18},{18,2},{3,19},{19,3},{4,20},{20... | collective-permute-start | bytes 3145736 | tf_op jit(solution)/shard_map/ppermute | solution.py:352
  34.5 2.6 %collective-permute-done.other_ref = bf16[16,64,512]{2,1,0:T(8,128)(2,1)S(1)} collective-permute-done((bf16[16,64,512]{2,1,0:T(8,128)(2,1)S(1)}, bf16[16,64,512]{2,1,0:T(8,128)(2,1)S(1)}, u32[]{:S(2)}, u32[]{:S(2)}) %collective-permute-start) | collective-permute-done | bytes 1048608 | tf_op jit(solution)/shard_map/ppermute | solution.py:352
  37.1 0.0 copy-done.5
  37.1 1.0 shard_map.84
  38.1 0.1 convert_element_type.21
  38.2 28.6 %all_to_all.42 = f16[8,136,256]{2,1,0:T(8,128)(2,1)S(1)} all-to-all(f16[8,136,256]{2,1,0:T(8,128)(2,1)S(1)} %convert_element_type.21), channel_id=1, replica_groups=mesh['ylo'=4,'x'=4,'core'=2,'z'=8,'yhi'=2] {'z'}, dimensions={0} | all-to-all | bytes 1114112 | tf_op jit(solution)/shard_map/all_to_all | solution.py:395
  66.8 0.1 convert_element_type.22.pieces_ref
  66.9 0.0 copy-start.8
  66.9 0.0 copy-start
  66.9 0.0 copy-start.1
  66.9 0.1 shard_map.85
  67.0 4.2 %collective-permute-start.1 = (f16[136,256]{1,0:T(8,128)(2,1)S(1)}, f16[136,256]{1,0:T(8,128)(2,1)S(1)}, u32[]{:S(2)}, u32[]{:S(2)}) collective-permute-start(f16[136,256]{1,0:T(8,128)(2,1)S(1)} %get-tuple-element.41), channel_id=1, source_target_pairs={{0,1},{1,0},{2,3},{3,2},{4,5},{5,4},{6,7},{7,6},{8,9},{9,8},{10,11... | collective-permute-start | bytes 208904 | tf_op jit(solution)/shard_map/ppermute | solution.py:352
  71.2 0.0 copy-done.8
  71.2 0.1 copy.9.log_ref
  71.3 0.0 copy-done
  71.3 0.0 copy-done.1
  71.3 0.9 shard_map.86
  72.2 5.2 %collective-permute-done.1 = f16[136,256]{1,0:T(8,128)(2,1)S(1)} collective-permute-done((f16[136,256]{1,0:T(8,128)(2,1)S(1)}, f16[136,256]{1,0:T(8,128)(2,1)S(1)}, u32[]{:S(2)}, u32[]{:S(2)}) %collective-permute-start.1) | collective-permute-done | bytes 69664 | tf_op jit(solution)/shard_map/ppermute | solution.py:352
  77.4 0.6 shard_map.87
  78.1 15.6 %all_to_all.43 = f16[32,40,128]{2,1,0:T(8,128)(2,1)S(1)} all-to-all(f16[32,40,128]{2,1,0:T(8,128)(2,1)S(1)} %convert_element_type.26), channel_id=1, replica_groups=mesh['ylo'=4,'x'=4,'core'=2,'z'=8,'yhi'=2] {'ylo','x','core'}, dimensions={0} | all-to-all | bytes 655360 | tf_op jit(solution)/shard_map/all_to_all | solution.py:410
  93.7 0.9 shard_map.88
  94.6 6.5 %all-to-all-start.4 = ((bf16[32,40,128]{2,1,0:T(8,128)(2,1)}), bf16[32,40,128]{2,1,0:T(8,128)(2,1)S(1)}, u32[]{:S(2)}, u32[]{:S(2)}) async-start(bf16[32,40,128]{2,1,0:T(8,128)(2,1)} %shard_map.88), calls=%async_computation.4 | async-start | bytes 655360 | tf_op jit(solution)/shard_map/all_to_all | solution.py:427
  101.1 1.3 shard_map.89
  102.4 0.0 copy-start.3
  102.4 0.8 copy-done.3
  103.3 0.0 copy-start.6
  103.3 0.7 copy-done.6
  104.0 7.0 %all-to-all-done.4.in_ref = bf16[32,40,128]{2,1,0:T(8,128)(2,1)S(1)} async-done(((bf16[32,40,128]{2,1,0:T(8,128)(2,1)}), bf16[32,40,128]{2,1,0:T(8,128)(2,1)S(1)}, u32[]{:S(2)}, u32[]{:S(2)}) %all-to-all-start.4) | async-done | bytes 327712 | tf_op jit(solution)/shard_map/all_to_all | solution.py:427
  111.0 0.0 copy-start.4
  111.0 1.1 copy-done.4
  112.1 0.0 copy-start.7
  112.1 0.3 shard_map.90.own_ref
  112.3 4.2 %collective-permute-start.2 = (bf16[256,128]{1,0:T(8,128)(2,1)S(1)}, bf16[256,128]{1,0:T(8,128)(2,1)S(1)}, u32[]{:S(2)}, u32[]{:S(2)}) collective-permute-start(bf16[256,128]{1,0:T(8,128)(2,1)S(1)} %shard_map.90.own_ref), channel_id=1, source_target_pairs={{0,1},{1,0},{2,3},{3,2},{4,5},{5,4},{6,7},{7,6},{8,9},{9,8},{10,11... | collective-permute-start | bytes 196616 | tf_op jit(solution)/shard_map/ppermute | solution.py:352
  116.6 0.0 copy-done.7
  116.6 2.2 %shard_map.91 = (f32[128,512]{1,0:T(8,128)}, f32[8,128]{1,0:T(8,128)}) custom-call(bf16[32,40,128]{2,1,0:T(8,128)(2,1)S(1)} %all-to-all-done.4.in_ref, f32[136,256]{1,0:T(8,128)S(1)} %get-tuple-element.40.own_ref, f32[136,256]{1,0:T(8,128)S(1)} %convert_element_type.25.other_ref, f32[128,512]{1,0:T(8,128)S(1)} %copy-done, f32[128,512]{1,0:T(8,128)S(1)} %copy-done.1, ...), custom_call_target="tpu_custom_call" | custom-call | flops 100000000 | bytes 1671168 | tf_op jit(solution)/shard_map/pallas_call | solution.py:83
  118.8 4.8 %collective-permute-done.2.other_ref = bf16[256,128]{1,0:T(8,128)(2,1)S(1)} collective-permute-done((bf16[256,128]{1,0:T(8,128)(2,1)S(1)}, bf16[256,128]{1,0:T(8,128)(2,1)S(1)}, u32[]{:S(2)}, u32[]{:S(2)}) %collective-permute-start.2) | collective-permute-done | bytes 65568 | tf_op jit(solution)/shard_map/ppermute | solution.py:352
  123.6 0.8 shard_map.92
  124.5 3.5 %all-to-all-start.5 = ((bf16[8,256,128]{2,1,0:T(8,128)(2,1)}), bf16[8,256,128]{2,1,0:T(8,128)(2,1)S(1)}, u32[]{:S(2)}, u32[]{:S(2)}) async-start(bf16[8,256,128]{2,1,0:T(8,128)(2,1)} %shard_map.92), calls=%async_computation.5 | async-start | bytes 1048576 | tf_op jit(solution)/shard_map/all_to_all | solution.py:452
  128.0 2.3 %collective-permute-start.3 = (bf16[128,512]{1,0:T(8,128)(2,1)S(1)}, bf16[128,512]{1,0:T(8,128)(2,1)S(1)}, u32[]{:S(2)}, u32[]{:S(2)}) collective-permute-start(bf16[128,512]{1,0:T(8,128)(2,1)S(1)} %copy-done.5), channel_id=1, source_target_pairs={{0,32},{32,0},{64,96},{96,64},{1,33},{33,1},{65,97},{97,65},{2,34}... | collective-permute-start | bytes 393224 | tf_op jit(solution)/shard_map/ppermute | solution.py:352
  130.3 4.6 %collective-permute-start.4 = (bf16[128,512]{1,0:T(8,128)(2,1)S(1)}, bf16[128,512]{1,0:T(8,128)(2,1)S(1)}, u32[]{:S(2)}, u32[]{:S(2)}) collective-permute-start(bf16[128,512]{1,0:T(8,128)(2,1)S(1)} %copy-done.5), channel_id=1, source_target_pairs={{0,64},{32,96},{64,0},{96,32},{1,65},{33,97},{65,1},{97,33},{2,66}... | collective-permute-start | bytes 393224 | tf_op jit(solution)/shard_map/ppermute | solution.py:352
  134.9 0.0 collective-permute-done.3.x1_ref
  134.9 3.7 %collective-permute-start.5 = (bf16[128,512]{1,0:T(8,128)(2,1)S(1)}, bf16[128,512]{1,0:T(8,128)(2,1)S(1)}, u32[]{:S(2)}, u32[]{:S(2)}) collective-permute-start(bf16[128,512]{1,0:T(8,128)(2,1)S(1)} %collective-permute-done.3.x1_ref), channel_id=1, source_target_pairs={{0,64},{32,96},{64,0},{96,32},{1,65},{33,97},{65,1},{97,33},{2,66}... | collective-permute-start | bytes 393224 | tf_op jit(solution)/shard_map/ppermute | solution.py:352
  138.7 0.5 collective-permute-done.4.x2_ref
  139.1 4.2 %collective-permute-done.5.x3_ref = bf16[128,512]{1,0:T(8,128)(2,1)S(1)} collective-permute-done((bf16[128,512]{1,0:T(8,128)(2,1)S(1)}, bf16[128,512]{1,0:T(8,128)(2,1)S(1)}, u32[]{:S(2)}, u32[]{:S(2)}) %collective-permute-start.5) | collective-permute-done | bytes 131104 | tf_op jit(solution)/shard_map/ppermute | solution.py:352
  143.3 1.5 all-to-all-done.5.grads_ref
  144.9 0.0 copy-start.2
  144.9 0.8 copy-done.2
  145.7 4.1 %all-to-all-start.6 = ((bf16[4,8,64,128]{3,2,1,0:T(8,128)(2,1)}), bf16[4,8,64,128]{3,2,1,0:T(8,128)(2,1)}, u32[]{:S(2)}, u32[]{:S(2)}) async-start(bf16[4,8,64,128]{3,2,1,0:T(8,128)(2,1)} %copy-done.2), calls=%async_computation.6 | async-start | bytes 1048576 | tf_op jit(solution)/shard_map/all_to_all | solution.py:470
  149.8 0.1 pad_add_fusion.place_ref
  149.9 1.1 shard_map.95
  151.0 8.3 %all-to-all-done.6.grads_ref = bf16[4,8,64,128]{3,2,1,0:T(8,128)(2,1)} async-done(((bf16[4,8,64,128]{3,2,1,0:T(8,128)(2,1)}), bf16[4,8,64,128]{3,2,1,0:T(8,128)(2,1)}, u32[]{:S(2)}, u32[]{:S(2)}) %all-to-all-start.6) | async-done | bytes 524320 | tf_op jit(solution)/shard_map/all_to_all | solution.py:470
  159.3 1.5 shard_map.96
  160.8 1.9 %collective-permute-start.6 = (bf16[4,64,512]{2,1,0:T(8,128)(2,1)S(1)}, bf16[4,64,512]{2,1,0:T(8,128)(2,1)S(1)}, u32[]{:S(2)}, u32[]{:S(2)}) collective-permute-start(bf16[4,64,512]{2,1,0:T(8,128)(2,1)S(1)} %get-tuple-element.39), channel_id=1, source_target_pairs={{0,16},{16,0},{1,17},{17,1},{2,18},{18,2},{3,19},{19,3},{4,20},{20... | collective-permute-start | bytes 786440 | tf_op jit(solution)/shard_map/ppermute | solution.py:352
  162.7 1.5 collective-permute-done.6.other_ref
  164.2 0.1 shard_map.97
  164.3 13.9 %all_to_all.44.parts_ref = bf16[4,64,512]{2,1,0:T(8,128)(2,1)S(1)} all-to-all(bf16[4,64,512]{2,1,0:T(8,128)(2,1)S(1)} %shard_map.97), channel_id=1, replica_groups=mesh['ylo'=4,'x'=4,'core'=2,'z'=8,'yhi'=2] {'ylo'}, dimensions={0} | all-to-all | bytes 524288 | tf_op jit(solution)/shard_map/all_to_all | solution.py:492
  178.2 0.7 shard_map.98
  (6 shorter events, 0.2 us)
Async XLA Ops:
  13.7 23.4 %copy-start.5 = (bf16[128,512]{1,0:T(8,128)(2,1)S(1)}, bf16[128,512]{1,0:T(8,128)(2,1)}, u32[]{:S(2)}) copy-start(bf16[128,512]{1,0:T(8,128)(2,1)} %x0_ref) | copy-start | bytes 393220
  32.6 4.5 %collective-permute-start = (bf16[16,64,512]{2,1,0:T(8,128)(2,1)S(1)}, bf16[16,64,512]{2,1,0:T(8,128)(2,1)S(1)}, u32[]{:S(2)}, u32[]{:S(2)}) collective-permute-start(bf16[16,64,512]{2,1,0:T(8,128)(2,1)S(1)} %bitcast.5), channel_id=1, source_target_pairs={{0,16},{16,0},{1,17},{17,1},{2,18},{18,2},{3,19},{19,3},{4,20},{20... | collective-permute-start | bytes 3145736 | tf_op jit(solution)/shard_map/ppermute | solution.py:352
  66.9 4.3 %copy-start.8 = (f32[128,8]{0,1:T(8,128)S(1)}, f32[128,8]{0,1:T(8,128)}, u32[]{:S(2)}) copy-start(f32[128,8]{0,1:T(8,128)} %param.8) | copy-start | bytes 12292
  66.9 4.4 %copy-start = (f32[128,512]{1,0:T(8,128)S(1)}, f32[128,512]{1,0:T(8,128)}, u32[]{:S(2)}) copy-start(f32[128,512]{1,0:T(8,128)} %x_ref.7) | copy-start | bytes 786436
  66.9 4.4 %copy-start.1 = (f32[128,512]{1,0:T(8,128)S(1)}, f32[128,512]{1,0:T(8,128)}, u32[]{:S(2)}) copy-start(f32[128,512]{1,0:T(8,128)} %dy_ref.5) | copy-start | bytes 786436
  67.0 10.4 %collective-permute-start.1 = (f16[136,256]{1,0:T(8,128)(2,1)S(1)}, f16[136,256]{1,0:T(8,128)(2,1)S(1)}, u32[]{:S(2)}, u32[]{:S(2)}) collective-permute-start(f16[136,256]{1,0:T(8,128)(2,1)S(1)} %get-tuple-element.41), channel_id=1, source_target_pairs={{0,1},{1,0},{2,3},{3,2},{4,5},{5,4},{6,7},{7,6},{8,9},{9,8},{10,11... | collective-permute-start | bytes 208904 | tf_op jit(solution)/shard_map/ppermute | solution.py:352
  94.6 16.3 %all-to-all-start.4 = ((bf16[32,40,128]{2,1,0:T(8,128)(2,1)}), bf16[32,40,128]{2,1,0:T(8,128)(2,1)S(1)}, u32[]{:S(2)}, u32[]{:S(2)}) async-start(bf16[32,40,128]{2,1,0:T(8,128)(2,1)} %shard_map.88), calls=%async_computation.4 | async-start | bytes 655360 | tf_op jit(solution)/shard_map/all_to_all | solution.py:427
  102.4 0.9 copy-start.3
  103.3 0.7 copy-start.6
  111.0 1.1 copy-start.4
  112.1 4.5 %copy-start.7 = (f32[128,512]{1,0:T(8,128)S(1)}, f32[128,512]{1,0:T(8,128)}, u32[]{:S(2)}) copy-start(f32[128,512]{1,0:T(8,128)} %copy-done.6) | copy-start | bytes 786436
  112.3 11.3 %collective-permute-start.2 = (bf16[256,128]{1,0:T(8,128)(2,1)S(1)}, bf16[256,128]{1,0:T(8,128)(2,1)S(1)}, u32[]{:S(2)}, u32[]{:S(2)}) collective-permute-start(bf16[256,128]{1,0:T(8,128)(2,1)S(1)} %shard_map.90.own_ref), channel_id=1, source_target_pairs={{0,1},{1,0},{2,3},{3,2},{4,5},{5,4},{6,7},{7,6},{8,9},{9,8},{10,11... | collective-permute-start | bytes 196616 | tf_op jit(solution)/shard_map/ppermute | solution.py:352
  124.5 20.4 %all-to-all-start.5 = ((bf16[8,256,128]{2,1,0:T(8,128)(2,1)}), bf16[8,256,128]{2,1,0:T(8,128)(2,1)S(1)}, u32[]{:S(2)}, u32[]{:S(2)}) async-start(bf16[8,256,128]{2,1,0:T(8,128)(2,1)} %shard_map.92), calls=%async_computation.5 | async-start | bytes 1048576 | tf_op jit(solution)/shard_map/all_to_all | solution.py:452
  128.0 7.0 %collective-permute-start.3 = (bf16[128,512]{1,0:T(8,128)(2,1)S(1)}, bf16[128,512]{1,0:T(8,128)(2,1)S(1)}, u32[]{:S(2)}, u32[]{:S(2)}) collective-permute-start(bf16[128,512]{1,0:T(8,128)(2,1)S(1)} %copy-done.5), channel_id=1, source_target_pairs={{0,32},{32,0},{64,96},{96,64},{1,33},{33,1},{65,97},{97,65},{2,34}... | collective-permute-start | bytes 393224 | tf_op jit(solution)/shard_map/ppermute | solution.py:352
  130.3 8.8 %collective-permute-start.4 = (bf16[128,512]{1,0:T(8,128)(2,1)S(1)}, bf16[128,512]{1,0:T(8,128)(2,1)S(1)}, u32[]{:S(2)}, u32[]{:S(2)}) collective-permute-start(bf16[128,512]{1,0:T(8,128)(2,1)S(1)} %copy-done.5), channel_id=1, source_target_pairs={{0,64},{32,96},{64,0},{96,32},{1,65},{33,97},{65,1},{97,33},{2,66}... | collective-permute-start | bytes 393224 | tf_op jit(solution)/shard_map/ppermute | solution.py:352
  134.9 8.4 %collective-permute-start.5 = (bf16[128,512]{1,0:T(8,128)(2,1)S(1)}, bf16[128,512]{1,0:T(8,128)(2,1)S(1)}, u32[]{:S(2)}, u32[]{:S(2)}) collective-permute-start(bf16[128,512]{1,0:T(8,128)(2,1)S(1)} %collective-permute-done.3.x1_ref), channel_id=1, source_target_pairs={{0,64},{32,96},{64,0},{96,32},{1,65},{33,97},{65,1},{97,33},{2,66}... | collective-permute-start | bytes 393224 | tf_op jit(solution)/shard_map/ppermute | solution.py:352
  144.9 0.8 copy-start.2
  145.7 13.6 %all-to-all-start.6 = ((bf16[4,8,64,128]{3,2,1,0:T(8,128)(2,1)}), bf16[4,8,64,128]{3,2,1,0:T(8,128)(2,1)}, u32[]{:S(2)}, u32[]{:S(2)}) async-start(bf16[4,8,64,128]{3,2,1,0:T(8,128)(2,1)} %copy-done.2), calls=%async_computation.6 | async-start | bytes 1048576 | tf_op jit(solution)/shard_map/all_to_all | solution.py:470
  160.8 3.4 %collective-permute-start.6 = (bf16[4,64,512]{2,1,0:T(8,128)(2,1)S(1)}, bf16[4,64,512]{2,1,0:T(8,128)(2,1)S(1)}, u32[]{:S(2)}, u32[]{:S(2)}) collective-permute-start(bf16[4,64,512]{2,1,0:T(8,128)(2,1)S(1)} %get-tuple-element.39), channel_id=1, source_target_pairs={{0,16},{16,0},{1,17},{17,1},{2,18},{18,2},{3,19},{19,3},{4,20},{20... | collective-permute-start | bytes 786440 | tf_op jit(solution)/shard_map/ppermute | solution.py:352

commit v3 on v2

--- a/solution.py
+++ b/solution.py
@@ -156,15 +156,16 @@
     out_ref[steps:, :] = top
 
 
-def whole_bc(own_ref, other_ref):
-    steps = own_ref.shape[0] - EXTRA_ROWS
-    bc = own_ref[:steps, :] * power(own_ref[steps : steps + 1, :])
-    bc = bc + other_ref[:steps, :] * power(other_ref[steps : steps + 1, :])
+def whole_bc(halves_ref):
+    steps = halves_ref.shape[1] - EXTRA_ROWS
+    bc = sum(
+        halves_ref[k, :steps, :] * power(halves_ref[k, steps : steps + 1, :]) for k in range(2)
+    )
     return bc[:, :N], bc[:, N:]
 
 
-def states_kernel(own_ref, other_ref, xet_ref, dyft_ref, ds_ref, out_ref):
-    b_rows, c_rows = whole_bc(own_ref, other_ref)
+def states_kernel(halves_ref, xet_ref, dyft_ref, ds_ref, out_ref):
+    b_rows, c_rows = whole_bc(halves_ref)
     heads = ds_ref.shape[0]
     parts, rows, _ = out_ref.shape
     half = (rows - EXTRA_ROWS) // 2
@@ -182,8 +183,8 @@
             out_ref[part, 2 * half :, :] = terms
 
 
-def local_kernel(own_ref, other_ref, x_ref, dy_ref, log_ref, logt_ref, gx_ref, terms_ref, inside_ref):
-    b_rows, c_rows = (rows.astype(BF16) for rows in whole_bc(own_ref, other_ref))
+def local_kernel(halves_ref, x_ref, dy_ref, log_ref, logt_ref, gx_ref, terms_ref, inside_ref):
+    b_rows, c_rows = (rows.astype(BF16) for rows in whole_bc(halves_ref))
     steps, heads = log_ref.shape
     size = x_ref.shape[1] // heads
     row, col = iotas(steps)
@@ -249,9 +250,9 @@
     out_ref[N:, :] = (terms_ref[:, 2 * width + N :] + from_state).T.astype(BF16)
 
 
-def finish_kernel(in_ref, own_ref, other_ref, x_ref, dy_ref, log_ref, logt_ref, gx_ref, inside_ref, out_ref, out_log_ref):
+def finish_kernel(in_ref, halves_ref, x_ref, dy_ref, log_ref, logt_ref, gx_ref, inside_ref, out_ref, out_log_ref):
     state, grad = entering(in_ref)
-    b_rows, c_rows = (rows.astype(BF16) for rows in whole_bc(own_ref, other_ref))
+    b_rows, c_rows = (rows.astype(BF16) for rows in whole_bc(halves_ref))
     steps, heads = log_ref.shape
     width = x_ref.shape[1]
     row, col = iotas(steps)
@@ -296,17 +297,11 @@
                 out_ref[2 * high + k, 2 * column + core] = grads_ref[group, at : at + rows, :]
 
 
-def stack_kernel(x0_ref, x1_ref, x2_ref, x3_ref, out_ref):
-    steps = x0_ref.shape[0]
-    for k, ref in enumerate((x0_ref, x1_ref, x2_ref, x3_ref)):
-        out_ref[k * steps : (k + 1) * steps, :] = ref[...]
-
-
-def grad_weight_kernel(place_ref, grads_ref, x_ref, keep_ref, send_ref):
+def grad_weight_kernel(place_ref, grads_ref, low_ref, high_ref, keep_ref, send_ref):
     first = place_ref[0] == 0
     line = place_ref[1]
     columns, rows, width = keep_ref.shape
-    x = x_ref[...]
+    x = jnp.concatenate([low_ref[...], high_ref[...]], axis=0)
     for column in range(columns):
         grads = jnp.concatenate(
             [
@@ -333,8 +328,8 @@
     out_ref[...] = total
 
 
-def copies_kernel(own_ref, other_ref, out_ref):
-    total = (own_ref[...].astype(F32) + other_ref[...].astype(F32)).astype(BF16)
+def copies_kernel(halves_ref, out_ref):
+    total = (halves_ref[0].astype(F32) + halves_ref[1].astype(F32)).astype(BF16)
     for k in range(out_ref.shape[0]):
         out_ref[k] = total
 
@@ -382,6 +377,7 @@
         log_decay,
         logt,
     )
+    other_w, xet, dyft, ds = lax.optimization_barrier((other_w, xet, dyft, ds))
     partial = call(
         partial_kernel,
         shape((groups, steps + EXTRA_ROWS, 2 * N)),
@@ -393,16 +389,14 @@
         smem=1,
     )
     pieces = lax.all_to_all(partial.astype(F16), "z", 0, 0).astype(F32)
-    own_bc = call(sum_kernel, shape((steps + EXTRA_ROWS, 2 * N)), 10**6, pieces).astype(F16)
-    other_bc = swap(own_bc, "yhi").astype(F32)
-    own_bc = own_bc.astype(F32)
+    half_bc = call(sum_kernel, shape((steps + EXTRA_ROWS, 2 * N)), 10**6, pieces).astype(F16)
+    halves = lax.all_gather(half_bc, "yhi").astype(F32)
 
     parts = call(
         states_kernel,
         shape((slabs, 2 * share + EXTRA_ROWS, N)),
         12 * steps * N * ssd_input.shape[1],
-        own_bc,
-        other_bc,
+        halves,
         xet,
         dyft,
         ds,
@@ -416,8 +410,7 @@
             shape((heads, steps)),
         ),
         10**8,
-        own_bc,
-        other_bc,
+        halves,
         ssd_input,
         out_grad,
         log_decay,
@@ -432,14 +425,16 @@
         arrived,
         terms,
     )
-    other_grad = swap(own_grad, "yhi")
+    near_input, _ = lax.optimization_barrier((layer_input, carried))
+    pair = jnp.concatenate([near_input, flip(near_input, "x", 1)], axis=0)
+    own_grad, pair = lax.optimization_barrier((own_grad, pair))
+    halves_grad = lax.all_gather(own_grad, "yhi")
     grad_x, grad_log = call(
         finish_kernel,
         (shape(ssd_input.shape), shape((heads, steps))),
         10**8,
         arrived,
-        own_bc,
-        other_bc,
+        halves,
         ssd_input,
         out_grad,
         log_decay,
@@ -447,22 +442,11 @@
         gx,
         inside,
     )
-    other_grad, grad_x, grad_log = lax.optimization_barrier((other_grad, grad_x, grad_log))
-    copies = call(copies_kernel, shape((groups, 2 * N, steps), BF16), 10**6, own_grad, other_grad)
+    copies = call(copies_kernel, shape((groups, 2 * N, steps), BF16), 10**6, halves_grad)
     all_grads = lax.all_to_all(copies, "z", 0, 0)
-    late_input, _ = lax.optimization_barrier((layer_input, copies))
-    near = flip(late_input, "x", 1)
-    x_along = call(
-        stack_kernel,
-        shape((4 * steps, width), BF16),
-        10**6,
-        late_input,
-        near,
-        flip(late_input, "x", 2),
-        flip(near, "x", 2),
-    )
-    all_grads, x_along = lax.optimization_barrier((all_grads, x_along))
-
+    pair, _ = lax.optimization_barrier((pair, copies))
+    far_pair = flip(pair, "x", 2)
+    all_grads, pair, far_pair = lax.optimization_barrier((all_grads, pair, far_pair))
     columns = groups // 2
     blocks = call(
         row_blocks_kernel, shape((4, 2 * columns, rows_here, steps), BF16), 10**6, all_grads
@@ -478,14 +462,17 @@
         other_w,
         smem=1,
     )
-    row_grads, grad_input = lax.optimization_barrier((row_grads, grad_input))
+    row_grads, grad_input, grad_x, grad_log = lax.optimization_barrier(
+        (row_grads, grad_input, grad_x, grad_log)
+    )
     keep, send = call(
         grad_weight_kernel,
         (shape((columns, rows_here, width)), shape((columns, rows_here, width), BF16)),
         2 * steps * width * slabs * rows_here,
         jnp.concatenate([core, lax.axis_index("x").reshape(1)]),
         row_grads,
-        x_along,
+        pair,
+        far_pair,
         smem=1,
     )
     of_chip = call(chip_sum_kernel, shape(send.shape, BF16), 10**6, keep, swap(send, "core"))

time: 180 us -> 177 us (0.983)
  blocking collectives: 89 us -> 109 us
  waiting for transfers between devices: 35.5 us -> 20.1 us
  starting transfers between devices: 37 us -> 24.6 us
  local copies, waits for them, and re-layouts: 4.52 us -> 10.1 us
    all_gather x0 -> x2, blocking collectives: none -> 19.1 us  [the longest x1 10.1 us: on_device(): halves_grad = lax.all_gather(own_grad, 'yhi')]
    ppermute x7 -> x4, starting transfers between devices: 22.9 us -> 10.5 us  [flip(): lax.ppermute(block, axis, [(k, k ^ bit) for k in range(lax.axis_size(axis...]
    all_to_all x1, waiting for transfers between devices: 8.27 us -> 1.2 us  [on_device(): row_grads = lax.all_to_all(blocks, 'x', 0, 0)]
    all_to_all x1, waiting for transfers between devices: 7 us -> 0.22 us  [on_device(): arrived = lax.all_to_all(carried, TM, 0, 0)]
    unnamed x19 -> x39, local copies, waits for them, and re-layouts: 3.56 us -> 9.1 us
    ppermute x7 -> x4, waiting for transfers between devices: 18.7 us -> 13.3 us  [flip(): lax.ppermute(block, axis, [(k, k ^ bit) for k in range(lax.axis_size(axis...]
    all_to_all x1, waiting for transfers between devices: 1.51 us -> 5.33 us  [on_device(): all_grads = lax.all_to_all(copies, 'z', 0, 0)]
    pallas_call x15 -> x14, Pallas kernels: 11.6 us -> 10 us  [call(): pl.pallas_call(kernel, out_shape=outs, in_specs=[pl.BlockSpec(memory_spac...]
  transfers between devices with their start and end apart: 10 -> 7, of which waited for: 9 -> 7; matrix products, arithmetic and copies ran while one was open for 0% -> 1% of each run, Pallas kernels for 3% -> 3%
where the time goes in v3:
time: 177 us; the launch traced here: 176 us
  blocking collectives  109 us (62%)
  starting transfers between devices  24.6 us (14%)
  waiting for transfers between devices  20.1 us (11%)
  local copies, waits for them, and re-layouts  10.1 us (6%)
  Pallas kernels  10 us (6%)
    all_to_all x2, blocking collectives, to_all(): lax.all_to_all(jnp.broadcast_to(block[None], (count,) + block.shape), axi...  30.9 us
    all_to_all x1, blocking collectives, on_device(): pieces = lax.all_to_all(partial.astype(F16), 'z', 0, 0).astype(F32)  28.6 us
    all_to_all x1, blocking collectives, on_device(): shares = lax.all_to_all(parts.astype(F16), TM, 0, 0).astype(F32)  15.6 us
    all_to_all x1, blocking collectives, on_device(): of_line = lax.all_to_all(of_chip, 'ylo', 0, 0)  14.9 us
    ppermute x4, waiting for transfers between devices, flip(): lax.ppermute(block, axis, [(k, k ^ bit) for k in range(lax.axis_size(axis...  13.3 us
    ppermute x4, starting transfers between devices, flip(): lax.ppermute(block, axis, [(k, k ^ bit) for k in range(lax.axis_size(axis...  10.5 us
    all_gather x1, blocking collectives, on_device(): halves_grad = lax.all_gather(own_grad, 'yhi')  10.1 us
    pallas_call x14, Pallas kernels, call(): pl.pallas_call(kernel, out_shape=outs, in_specs=[pl.BlockSpec(memory_spac...  10 us
  transfers between devices with their start and end apart: 7, of which 7 were waited for; matrix products, arithmetic and copies ran while one was open for 1% of the time, Pallas kernels for 3%

profile of v3, /device:TPU:56, one launch (start us, length us, event | category | flops | bytes accessed | tf_op | source)
XLA Modules:
  0.0 176.4 jit_solution(1914624692318837352)
XLA Ops:
  0.6 0.9 broadcast_in_dim.4
  1.5 12.1 %all_to_all.40 = bf16[4,64,512]{2,1,0:T(8,128)(2,1)S(1)} all-to-all(bf16[4,64,512]{2,1,0:T(8,128)(2,1)S(1)} %broadcast_in_dim.4), channel_id=1, replica_groups=mesh['ylo'=4,'x'=4,'core'=2,'z'=8,'yhi'=2] {'ylo'}, dimensions={0} | all-to-all | bytes 524288 | tf_op jit(solution)/shard_map/all_to_all | solution.py:343
  13.6 0.1 broadcast_in_dim.5
  13.7 0.0 copy-start.14
  13.7 0.0 copy-start
  13.7 0.0 copy-start.1
  13.7 0.0 copy-start.9
  13.7 18.9 %all_to_all.41 = bf16[4,4,64,512]{3,2,1,0:T(8,128)(2,1)S(1)} all-to-all(bf16[4,4,64,512]{3,2,1,0:T(8,128)(2,1)S(1)} %broadcast_in_dim.5), channel_id=1, replica_groups=mesh['ylo'=4,'x'=4,'core'=2,'z'=8,'yhi'=2] {'x'}, dimensions={0} | all-to-all | bytes 2097152 | tf_op jit(solution)/shard_map/all_to_all | solution.py:343
  32.6 1.9 %collective-permute-start = (bf16[16,64,512]{2,1,0:T(8,128)(2,1)S(1)}, bf16[16,64,512]{2,1,0:T(8,128)(2,1)S(1)}, u32[]{:S(2)}, u32[]{:S(2)}) collective-permute-start(bf16[16,64,512]{2,1,0:T(8,128)(2,1)S(1)} %bitcast.8), channel_id=1, source_target_pairs={{0,16},{16,0},{1,17},{17,1},{2,18},{18,2},{3,19},{19,3},{4,20},{20... | collective-permute-start | bytes 3145736 | tf_op jit(solution)/shard_map/ppermute | solution.py:347
  34.5 0.0 copy-done.14
  34.5 0.1 copy.9.log_ref
  34.6 0.0 copy-done
  34.6 0.0 copy-done.1
  34.6 0.9 shard_map.84
  35.5 1.6 collective-permute-done.other_ref
  37.1 0.0 copy-done.9
  37.1 1.0 shard_map.85
  38.1 0.1 convert_element_type.18
  38.2 28.6 %all_to_all.42 = f16[8,136,256]{2,1,0:T(8,128)(2,1)S(1)} all-to-all(f16[8,136,256]{2,1,0:T(8,128)(2,1)S(1)} %convert_element_type.18), channel_id=1, replica_groups=mesh['ylo'=4,'x'=4,'core'=2,'z'=8,'yhi'=2] {'z'}, dimensions={0} | all-to-all | bytes 1114112 | tf_op jit(solution)/shard_map/all_to_all | solution.py:391
  66.8 0.1 convert_element_type.19.pieces_ref
  66.9 0.1 shard_map.86
  67.0 9.0 %all-gather = f16[272,256]{1,0:T(8,128)(2,1)S(1)} all-gather(f16[136,256]{1,0:T(8,128)(2,1)S(1)} %convert_element_type.20), channel_id=2, replica_groups=mesh['ylo'=4,'x'=4,'core'=2,'z'=8,'yhi'=2] {'yhi'}, dimensions={0}, use_global_device_ids=true | all-gather | bytes 208896 | tf_op jit(solution)/shard_map/all_gather | solution.py:393
  76.1 0.6 shard_map.87
  76.7 15.6 %all_to_all.43 = f16[32,40,128]{2,1,0:T(8,128)(2,1)S(1)} all-to-all(f16[32,40,128]{2,1,0:T(8,128)(2,1)S(1)} %convert_element_type.22), channel_id=1, replica_groups=mesh['ylo'=4,'x'=4,'core'=2,'z'=8,'yhi'=2] {'ylo','x','core'}, dimensions={0} | all-to-all | bytes 655360 | tf_op jit(solution)/shard_map/all_to_all | solution.py:404
  92.3 0.2 shard_map.88
  92.6 0.0 copy-start.5
  92.6 0.7 copy-done.5
  93.3 6.5 %all-to-all-start.4 = ((bf16[32,40,128]{2,1,0:T(8,128)(2,1)}), bf16[32,40,128]{2,1,0:T(8,128)(2,1)S(1)}, u32[]{:S(2)}, u32[]{:S(2)}) async-start(bf16[32,40,128]{2,1,0:T(8,128)(2,1)} %copy-done.5), calls=%async_computation.4 | async-start | bytes 655360 | tf_op jit(solution)/shard_map/all_to_all | solution.py:420
  99.8 3.4 %collective-permute-start.1 = (bf16[128,512]{1,0:T(8,128)(2,1)S(1)}, bf16[128,512]{1,0:T(8,128)(2,1)S(1)}, u32[]{:S(2)}, u32[]{:S(2)}) collective-permute-start(bf16[128,512]{1,0:T(8,128)(2,1)S(1)} %copy-done.9), channel_id=1, source_target_pairs={{0,32},{32,0},{64,96},{96,64},{1,33},{33,1},{65,97},{97,65},{2,34}... | collective-permute-start | bytes 393224 | tf_op jit(solution)/shard_map/ppermute | solution.py:347
  103.2 1.3 shard_map.89
  104.5 0.0 copy-start.7
  104.5 0.8 copy-done.7
  105.3 0.7 copy-done.10
  106.0 2.7 %collective-permute-done.1 = bf16[128,512]{1,0:T(8,128)(2,1)S(1)} collective-permute-done((bf16[128,512]{1,0:T(8,128)(2,1)S(1)}, bf16[128,512]{1,0:T(8,128)(2,1)S(1)}, u32[]{:S(2)}, u32[]{:S(2)}) %collective-permute-start.1) | collective-permute-done | bytes 131104 | tf_op jit(solution)/shard_map/ppermute | solution.py:347
  108.7 0.7 pad_maximum_fusion.low_ref
  109.4 0.2 all-to-all-done.4.in_ref
  109.7 1.1 copy-done.8
  110.7 0.3 shard_map.90
  111.0 10.1 %all-gather.1 = bf16[512,128]{1,0:T(8,128)(2,1)S(1)} all-gather(bf16[256,128]{1,0:T(8,128)(2,1)S(1)} %shard_map.90), channel_id=3, replica_groups=mesh['ylo'=4,'x'=4,'core'=2,'z'=8,'yhi'=2] {'yhi'}, dimensions={0}, use_global_device_ids=true | all-gather | bytes 196608 | tf_op jit(solution)/shard_map/all_gather | solution.py:431
  121.1 0.0 copy-done.16
  121.1 0.0 copy-start.3
  121.2 0.8 copy-done.3
  122.0 3.5 %all-to-all-start.5 = ((bf16[8,256,128]{2,1,0:T(8,128)(2,1)}), bf16[8,256,128]{2,1,0:T(8,128)(2,1)S(1)}, u32[]{:S(2)}, u32[]{:S(2)}) async-start(bf16[8,256,128]{2,1,0:T(8,128)(2,1)} %copy-done.3), calls=%async_computation.5 | async-start | bytes 1048576 | tf_op jit(solution)/shard_map/all_to_all | solution.py:446
  125.4 3.3 %collective-permute-start.2 = (bf16[256,512]{1,0:T(8,128)(2,1)}, bf16[256,512]{1,0:T(8,128)(2,1)S(1)}, u32[]{:S(2)}, u32[]{:S(2)}) collective-permute-start(bf16[256,512]{1,0:T(8,128)(2,1)} %pad_maximum_fusion.low_ref), channel_id=1, source_target_pairs={{0,64},{32,96},{64,0},{96,32},{1,65},{33,97},{65,1},{97,33},{2,66}... | collective-permute-start | bytes 786440 | tf_op jit(solution)/shard_map/ppermute | solution.py:347
  128.7 7.6 %collective-permute-done.2.high_ref = bf16[256,512]{1,0:T(8,128)(2,1)S(1)} collective-permute-done((bf16[256,512]{1,0:T(8,128)(2,1)}, bf16[256,512]{1,0:T(8,128)(2,1)S(1)}, u32[]{:S(2)}, u32[]{:S(2)}) %collective-permute-start.2) | collective-permute-done | bytes 262176 | tf_op jit(solution)/shard_map/ppermute | solution.py:347
  136.3 0.7 copy-done.12
  137.0 5.3 %all-to-all-done.5.grads_ref = bf16[8,256,128]{2,1,0:T(8,128)(2,1)S(1)} async-done(((bf16[8,256,128]{2,1,0:T(8,128)(2,1)}), bf16[8,256,128]{2,1,0:T(8,128)(2,1)S(1)}, u32[]{:S(2)}, u32[]{:S(2)}) %all-to-all-start.5) | async-done | bytes 524320 | tf_op jit(solution)/shard_map/all_to_all | solution.py:446
  142.4 0.0 copy-start.4
  142.4 0.8 copy-done.4
  143.2 4.1 %all-to-all-start.6 = ((bf16[4,8,64,128]{3,2,1,0:T(8,128)(2,1)}), bf16[4,8,64,128]{3,2,1,0:T(8,128)(2,1)}, u32[]{:S(2)}, u32[]{:S(2)}) async-start(bf16[4,8,64,128]{3,2,1,0:T(8,128)(2,1)} %copy-done.4), calls=%async_computation.6 | async-start | bytes 1048576 | tf_op jit(solution)/shard_map/all_to_all | solution.py:454
  147.3 0.6 pad_add_fusion.place_ref
  147.9 0.9 copy-done.2
  148.9 0.9 copy-done.11
  149.8 0.7 copy-done.15
  150.5 0.7 copy-done.17
  151.2 2.2 %shard_map.94 = (f32[128,512]{1,0:T(8,128)}, f32[8,128]{1,0:T(8,128)}) custom-call(bf16[32,40,128]{2,1,0:T(8,128)(2,1)S(1)} %all-to-all-done.4.in_ref, f32[2,136,256]{2,1,0:T(8,128)S(1)} %convert.halves_ref, f32[128,512]{1,0:T(8,128)S(1)} %copy-done, f32[128,512]{1,0:T(8,128)S(1)} %copy-done.2, f32[128,8]{1,0:T(8,128)S(1)} %copy.9.log_ref, ...), custom_call_target="tpu_custom_call" | custom-call | flops 100000000 | bytes 1671168 | tf_op jit(solution)/shard_map/pallas_call | solution.py:83
  153.5 1.1 shard_map.93
  154.6 1.2 all-to-all-done.6.grads_ref
  155.8 1.5 shard_map.95
  157.3 1.9 %collective-permute-start.3 = (bf16[4,64,512]{2,1,0:T(8,128)(2,1)S(1)}, bf16[4,64,512]{2,1,0:T(8,128)(2,1)S(1)}, u32[]{:S(2)}, u32[]{:S(2)}) collective-permute-start(bf16[4,64,512]{2,1,0:T(8,128)(2,1)S(1)} %get-tuple-element.53), channel_id=1, source_target_pairs={{0,16},{16,0},{1,17},{17,1},{2,18},{18,2},{3,19},{19,3},{4,20},{20... | collective-permute-start | bytes 786440 | tf_op jit(solution)/shard_map/ppermute | solution.py:347
  159.2 1.5 collective-permute-done.3.other_ref
  160.7 0.1 shard_map.96
  160.8 14.9 %all_to_all.44.parts_ref = bf16[4,64,512]{2,1,0:T(8,128)(2,1)S(1)} all-to-all(bf16[4,64,512]{2,1,0:T(8,128)(2,1)S(1)} %shard_map.96), channel_id=1, replica_groups=mesh['ylo'=4,'x'=4,'core'=2,'z'=8,'yhi'=2] {'ylo'}, dimensions={0} | all-to-all | bytes 524288 | tf_op jit(solution)/shard_map/all_to_all | solution.py:479
  175.7 0.7 shard_map.97
  (20 shorter events, 0.2 us)
Async XLA Ops:
  13.7 20.8 %copy-start.14 = (f32[128,8]{0,1:T(8,128)S(1)}, f32[128,8]{0,1:T(8,128)}, u32[]{:S(2)}) copy-start(f32[128,8]{0,1:T(8,128)} %param.8) | copy-start | bytes 12292
  13.7 20.9 %copy-start = (f32[128,512]{1,0:T(8,128)S(1)}, f32[128,512]{1,0:T(8,128)}, u32[]{:S(2)}) copy-start(f32[128,512]{1,0:T(8,128)} %x_ref.7) | copy-start | bytes 786436
  13.7 20.9 %copy-start.1 = (f32[128,512]{1,0:T(8,128)S(1)}, f32[128,512]{1,0:T(8,128)}, u32[]{:S(2)}) copy-start(f32[128,512]{1,0:T(8,128)} %dy_ref.5) | copy-start | bytes 786436
  13.7 23.4 %copy-start.9 = (bf16[128,512]{1,0:T(8,128)(2,1)S(1)}, bf16[128,512]{1,0:T(8,128)(2,1)}, u32[]{:S(2)}) copy-start(bf16[128,512]{1,0:T(8,128)(2,1)} %x_ref.5) | copy-start | bytes 393220
  32.6 4.5 %collective-permute-start = (bf16[16,64,512]{2,1,0:T(8,128)(2,1)S(1)}, bf16[16,64,512]{2,1,0:T(8,128)(2,1)S(1)}, u32[]{:S(2)}, u32[]{:S(2)}) collective-permute-start(bf16[16,64,512]{2,1,0:T(8,128)(2,1)S(1)} %bitcast.8), channel_id=1, source_target_pairs={{0,16},{16,0},{1,17},{17,1},{2,18},{18,2},{3,19},{19,3},{4,20},{20... | collective-permute-start | bytes 3145736 | tf_op jit(solution)/shard_map/ppermute | solution.py:347
  92.6 0.8 copy-start.5
  93.3 16.3 %all-to-all-start.4 = ((bf16[32,40,128]{2,1,0:T(8,128)(2,1)}), bf16[32,40,128]{2,1,0:T(8,128)(2,1)S(1)}, u32[]{:S(2)}, u32[]{:S(2)}) async-start(bf16[32,40,128]{2,1,0:T(8,128)(2,1)} %copy-done.5), calls=%async_computation.4 | async-start | bytes 655360 | tf_op jit(solution)/shard_map/all_to_all | solution.py:420
  99.8 8.9 %collective-permute-start.1 = (bf16[128,512]{1,0:T(8,128)(2,1)S(1)}, bf16[128,512]{1,0:T(8,128)(2,1)S(1)}, u32[]{:S(2)}, u32[]{:S(2)}) collective-permute-start(bf16[128,512]{1,0:T(8,128)(2,1)S(1)} %copy-done.9), channel_id=1, source_target_pairs={{0,32},{32,0},{64,96},{96,64},{1,33},{33,1},{65,97},{97,65},{2,34}... | collective-permute-start | bytes 393224 | tf_op jit(solution)/shard_map/ppermute | solution.py:347
  104.5 0.8 copy-start.7
  105.3 0.7 copy-start.10
  106.0 15.1 %copy-start.16 = (f32[8,128]{1,0:T(8,128)}, f32[8,128]{1,0:T(8,128)S(1)}, u32[]{:S(2)}) copy-start(f32[8,128]{1,0:T(8,128)S(1)} %get-tuple-element.43.inside_ref) | copy-start | bytes 12292
  109.7 1.1 copy-start.8
  121.1 0.8 copy-start.3
  122.0 20.4 %all-to-all-start.5 = ((bf16[8,256,128]{2,1,0:T(8,128)(2,1)}), bf16[8,256,128]{2,1,0:T(8,128)(2,1)S(1)}, u32[]{:S(2)}, u32[]{:S(2)}) async-start(bf16[8,256,128]{2,1,0:T(8,128)(2,1)} %copy-done.3), calls=%async_computation.5 | async-start | bytes 1048576 | tf_op jit(solution)/shard_map/all_to_all | solution.py:446
  125.4 10.8 %collective-permute-start.2 = (bf16[256,512]{1,0:T(8,128)(2,1)}, bf16[256,512]{1,0:T(8,128)(2,1)S(1)}, u32[]{:S(2)}, u32[]{:S(2)}) collective-permute-start(bf16[256,512]{1,0:T(8,128)(2,1)} %pad_maximum_fusion.low_ref), channel_id=1, source_target_pairs={{0,64},{32,96},{64,0},{96,32},{1,65},{33,97},{65,1},{97,33},{2,66}... | collective-permute-start | bytes 786440 | tf_op jit(solution)/shard_map/ppermute | solution.py:347
  136.3 0.7 copy-start.12
  142.4 0.8 copy-start.4
  143.2 12.6 %all-to-all-start.6 = ((bf16[4,8,64,128]{3,2,1,0:T(8,128)(2,1)}), bf16[4,8,64,128]{3,2,1,0:T(8,128)(2,1)}, u32[]{:S(2)}, u32[]{:S(2)}) async-start(bf16[4,8,64,128]{3,2,1,0:T(8,128)(2,1)} %copy-done.4), calls=%async_computation.6 | async-start | bytes 1048576 | tf_op jit(solution)/shard_map/all_to_all | solution.py:454
  147.9 0.9 copy-start.2
  148.9 0.9 copy-start.11
  149.8 0.7 copy-start.15
  150.5 0.7 copy-start.17
  153.5 2.3 %copy-start.6 = (bf16[256,512]{1,0:T(8,128)(2,1)S(1)}, bf16[256,512]{1,0:T(8,128)(2,1)}, u32[]{:S(2)}) copy-start(bf16[256,512]{1,0:T(8,128)(2,1)} %pad_maximum_fusion.low_ref) | copy-start | bytes 786436
  153.5 2.3 %copy-start.13 = (bf16[256,512]{1,0:T(8,128)(2,1)S(1)}, bf16[256,512]{1,0:T(8,128)(2,1)}, u32[]{:S(2)}) copy-start(bf16[256,512]{1,0:T(8,128)(2,1)} %copy-done.12) | copy-start | bytes 786436
  153.5 2.3 %copy-start.18 = (s32[2]{0:T(128)S(1)}, s32[2]{0:T(128)}, u32[]{:S(2)}) copy-start(s32[2]{0:T(128)} %pad_add_fusion.place_ref) | copy-start | bytes 28
  157.3 3.4 %collective-permute-start.3 = (bf16[4,64,512]{2,1,0:T(8,128)(2,1)S(1)}, bf16[4,64,512]{2,1,0:T(8,128)(2,1)S(1)}, u32[]{:S(2)}, u32[]{:S(2)}) collective-permute-start(bf16[4,64,512]{2,1,0:T(8,128)(2,1)S(1)} %get-tuple-element.53), channel_id=1, source_target_pairs={{0,16},{16,0},{1,17},{17,1},{2,18},{18,2},{3,19},{19,3},{4,20},{20... | collective-permute-start | bytes 786440 | tf_op jit(solution)/shard_map/ppermute | solution.py:347

commit v4 on v3

--- a/solution.py
+++ b/solution.py
@@ -446,12 +446,26 @@
     all_grads = lax.all_to_all(copies, "z", 0, 0)
     pair, _ = lax.optimization_barrier((pair, copies))
     far_pair = flip(pair, "x", 2)
-    all_grads, pair, far_pair = lax.optimization_barrier((all_grads, pair, far_pair))
+    all_grads, pair, far_pair, grad_x, grad_log = lax.optimization_barrier(
+        (all_grads, pair, far_pair, grad_x, grad_log)
+    )
     columns = groups // 2
     blocks = call(
         row_blocks_kernel, shape((4, 2 * columns, rows_here, steps), BF16), 10**6, all_grads
     )
     row_grads = lax.all_to_all(blocks, "x", 0, 0)
+    keep, send = call(
+        grad_weight_kernel,
+        (shape((columns, rows_here, width)), shape((columns, rows_here, width), BF16)),
+        2 * steps * width * slabs * rows_here,
+        jnp.concatenate([core, lax.axis_index("x").reshape(1)]),
+        row_grads,
+        pair,
+        far_pair,
+        smem=1,
+    )
+    from_core = swap(send, "core")
+    all_grads, _ = lax.optimization_barrier((all_grads, send))
     grad_input = call(
         grad_input_kernel,
         shape(layer_input.shape, BF16),
@@ -462,20 +476,8 @@
         other_w,
         smem=1,
     )
-    row_grads, grad_input, grad_x, grad_log = lax.optimization_barrier(
-        (row_grads, grad_input, grad_x, grad_log)
-    )
-    keep, send = call(
-        grad_weight_kernel,
-        (shape((columns, rows_here, width)), shape((columns, rows_here, width), BF16)),
-        2 * steps * width * slabs * rows_here,
-        jnp.concatenate([core, lax.axis_index("x").reshape(1)]),
-        row_grads,
-        pair,
-        far_pair,
-        smem=1,
-    )
-    of_chip = call(chip_sum_kernel, shape(send.shape, BF16), 10**6, keep, swap(send, "core"))
+    from_core, grad_input = lax.optimization_barrier((from_core, grad_input))
+    of_chip = call(chip_sum_kernel, shape(send.shape, BF16), 10**6, keep, from_core)
     of_line = lax.all_to_all(of_chip, "ylo", 0, 0)
     grad_weight = call(line_sum_kernel, shape(proj_weight.shape), 10**6, of_line)
     return grad_x, grad_log.T, grad_input, grad_weight

time: 177 us -> 177 us (level)
    all_to_all x1, waiting for transfers between devices: 1.2 us -> 8.3 us  [on_device(): row_grads = lax.all_to_all(blocks, 'x', 0, 0)]
    ppermute x4, waiting for transfers between devices: 13.3 us -> 6.7 us  [flip(): lax.ppermute(block, axis, [(k, k ^ bit) for k in range(lax.axis_size(axis...]
    unnamed x39 -> x37, local copies, waits for them, and re-layouts: 9.1 us -> 10 us
where the time goes in v4:
time: 177 us; the launch traced here: 176 us
  blocking collectives  109 us (62%)
  starting transfers between devices  23.9 us (14%)
  waiting for transfers between devices  20.5 us (12%)
  local copies, waits for them, and re-layouts  11 us (6%)
  Pallas kernels  9.53 us (5%)
    all_to_all x2, blocking collectives, to_all(): lax.all_to_all(jnp.broadcast_to(block[None], (count,) + block.shape), axi...  30.9 us
    all_to_all x1, blocking collectives, on_device(): pieces = lax.all_to_all(partial.astype(F16), 'z', 0, 0).astype(F32)  28.6 us
    all_to_all x1, blocking collectives, on_device(): shares = lax.all_to_all(parts.astype(F16), TM, 0, 0).astype(F32)  15.6 us
    all_to_all x1, blocking collectives, on_device(): of_line = lax.all_to_all(of_chip, 'ylo', 0, 0)  14.9 us
    ppermute x4, starting transfers between devices, flip(): lax.ppermute(block, axis, [(k, k ^ bit) for k in range(lax.axis_size(axis...  10.5 us
    all_gather x1, blocking collectives, on_device(): halves_grad = lax.all_gather(own_grad, 'yhi')  10.1 us
    unnamed x37, local copies, waits for them, and re-layouts  10 us
    pallas_call x14, Pallas kernels, call(): pl.pallas_call(kernel, out_shape=outs, in_specs=[pl.BlockSpec(memory_spac...  9.53 us
  transfers between devices with their start and end apart: 7, of which 7 were waited for; matrix products, arithmetic and copies ran while one was open for 1% of the time, Pallas kernels for 3%

profile of v4, /device:TPU:56, one launch (start us, length us, event | category | flops | bytes accessed | tf_op | source)
XLA Modules:
  0.0 176.1 jit_solution(13323350183568109057)
XLA Ops:
  0.6 0.9 broadcast_in_dim.4
  1.5 12.1 %all_to_all.40 = bf16[4,64,512]{2,1,0:T(8,128)(2,1)S(1)} all-to-all(bf16[4,64,512]{2,1,0:T(8,128)(2,1)S(1)} %broadcast_in_dim.4), channel_id=1, replica_groups=mesh['ylo'=4,'x'=4,'core'=2,'z'=8,'yhi'=2] {'ylo'}, dimensions={0} | all-to-all | bytes 524288 | tf_op jit(solution)/shard_map/all_to_all | solution.py:343
  13.6 0.1 broadcast_in_dim.5
  13.7 0.0 copy-start.14
  13.7 0.0 copy-start
  13.7 0.0 copy-start.1
  13.7 0.0 copy-start.9
  13.7 18.9 %all_to_all.41 = bf16[4,4,64,512]{3,2,1,0:T(8,128)(2,1)S(1)} all-to-all(bf16[4,4,64,512]{3,2,1,0:T(8,128)(2,1)S(1)} %broadcast_in_dim.5), channel_id=1, replica_groups=mesh['ylo'=4,'x'=4,'core'=2,'z'=8,'yhi'=2] {'x'}, dimensions={0} | all-to-all | bytes 2097152 | tf_op jit(solution)/shard_map/all_to_all | solution.py:343
  32.6 1.9 %collective-permute-start = (bf16[16,64,512]{2,1,0:T(8,128)(2,1)S(1)}, bf16[16,64,512]{2,1,0:T(8,128)(2,1)S(1)}, u32[]{:S(2)}, u32[]{:S(2)}) collective-permute-start(bf16[16,64,512]{2,1,0:T(8,128)(2,1)S(1)} %bitcast.8), channel_id=1, source_target_pairs={{0,16},{16,0},{1,17},{17,1},{2,18},{18,2},{3,19},{19,3},{4,20},{20... | collective-permute-start | bytes 3145736 | tf_op jit(solution)/shard_map/ppermute | solution.py:347
  34.5 0.0 copy-done.14
  34.5 0.1 copy.9.log_ref
  34.6 0.0 copy-done
  34.6 0.0 copy-done.1
  34.6 0.9 shard_map.84
  35.5 1.6 collective-permute-done.other_ref
  37.1 0.0 copy-done.9
  37.1 1.0 shard_map.85
  38.1 0.1 convert_element_type.18
  38.2 28.6 %all_to_all.42 = f16[8,136,256]{2,1,0:T(8,128)(2,1)S(1)} all-to-all(f16[8,136,256]{2,1,0:T(8,128)(2,1)S(1)} %convert_element_type.18), channel_id=1, replica_groups=mesh['ylo'=4,'x'=4,'core'=2,'z'=8,'yhi'=2] {'z'}, dimensions={0} | all-to-all | bytes 1114112 | tf_op jit(solution)/shard_map/all_to_all | solution.py:391
  66.8 0.1 convert_element_type.19.pieces_ref
  66.9 0.1 shard_map.86
  67.0 9.0 %all-gather = f16[272,256]{1,0:T(8,128)(2,1)S(1)} all-gather(f16[136,256]{1,0:T(8,128)(2,1)S(1)} %convert_element_type.20), channel_id=2, replica_groups=mesh['ylo'=4,'x'=4,'core'=2,'z'=8,'yhi'=2] {'yhi'}, dimensions={0}, use_global_device_ids=true | all-gather | bytes 208896 | tf_op jit(solution)/shard_map/all_gather | solution.py:393
  76.1 0.6 shard_map.87
  76.7 15.6 %all_to_all.43 = f16[32,40,128]{2,1,0:T(8,128)(2,1)S(1)} all-to-all(f16[32,40,128]{2,1,0:T(8,128)(2,1)S(1)} %convert_element_type.22), channel_id=1, replica_groups=mesh['ylo'=4,'x'=4,'core'=2,'z'=8,'yhi'=2] {'ylo','x','core'}, dimensions={0} | all-to-all | bytes 655360 | tf_op jit(solution)/shard_map/all_to_all | solution.py:404
  92.3 0.2 shard_map.88
  92.6 0.0 copy-start.5
  92.6 0.7 copy-done.5
  93.3 6.5 %all-to-all-start.4 = ((bf16[32,40,128]{2,1,0:T(8,128)(2,1)}), bf16[32,40,128]{2,1,0:T(8,128)(2,1)S(1)}, u32[]{:S(2)}, u32[]{:S(2)}) async-start(bf16[32,40,128]{2,1,0:T(8,128)(2,1)} %copy-done.5), calls=%async_computation.4 | async-start | bytes 655360 | tf_op jit(solution)/shard_map/all_to_all | solution.py:420
  99.8 3.4 %collective-permute-start.1 = (bf16[128,512]{1,0:T(8,128)(2,1)S(1)}, bf16[128,512]{1,0:T(8,128)(2,1)S(1)}, u32[]{:S(2)}, u32[]{:S(2)}) collective-permute-start(bf16[128,512]{1,0:T(8,128)(2,1)S(1)} %copy-done.9), channel_id=1, source_target_pairs={{0,32},{32,0},{64,96},{96,64},{1,33},{33,1},{65,97},{97,65},{2,34}... | collective-permute-start | bytes 393224 | tf_op jit(solution)/shard_map/ppermute | solution.py:347
  103.2 1.3 shard_map.89
  104.5 0.0 copy-start.7
  104.5 0.8 copy-done.7
  105.3 0.7 copy-done.12
  106.0 2.7 %collective-permute-done.1 = bf16[128,512]{1,0:T(8,128)(2,1)S(1)} collective-permute-done((bf16[128,512]{1,0:T(8,128)(2,1)S(1)}, bf16[128,512]{1,0:T(8,128)(2,1)S(1)}, u32[]{:S(2)}, u32[]{:S(2)}) %collective-permute-start.1) | collective-permute-done | bytes 131104 | tf_op jit(solution)/shard_map/ppermute | solution.py:347
  108.7 0.7 pad_maximum_fusion.low_ref
  109.4 0.2 all-to-all-done.4.in_ref
  109.6 1.1 copy-done.8
  110.7 0.3 shard_map.90
  111.0 10.1 %all-gather.1 = bf16[512,128]{1,0:T(8,128)(2,1)S(1)} all-gather(bf16[256,128]{1,0:T(8,128)(2,1)S(1)} %shard_map.90), channel_id=3, replica_groups=mesh['ylo'=4,'x'=4,'core'=2,'z'=8,'yhi'=2] {'yhi'}, dimensions={0}, use_global_device_ids=true | all-gather | bytes 196608 | tf_op jit(solution)/shard_map/all_gather | solution.py:431
  121.1 0.8 copy-done.3
  121.9 3.5 %all-to-all-start.5 = ((bf16[8,256,128]{2,1,0:T(8,128)(2,1)}), bf16[8,256,128]{2,1,0:T(8,128)(2,1)S(1)}, u32[]{:S(2)}, u32[]{:S(2)}) async-start(bf16[8,256,128]{2,1,0:T(8,128)(2,1)} %copy-done.3), calls=%async_computation.5 | async-start | bytes 1048576 | tf_op jit(solution)/shard_map/all_to_all | solution.py:446
  125.4 3.3 %collective-permute-start.2 = (bf16[256,512]{1,0:T(8,128)(2,1)}, bf16[256,512]{1,0:T(8,128)(2,1)S(1)}, u32[]{:S(2)}, u32[]{:S(2)}) collective-permute-start(bf16[256,512]{1,0:T(8,128)(2,1)} %pad_maximum_fusion.low_ref), channel_id=1, source_target_pairs={{0,64},{32,96},{64,0},{96,32},{1,65},{33,97},{65,1},{97,33},{2,66}... | collective-permute-start | bytes 786440 | tf_op jit(solution)/shard_map/ppermute | solution.py:347
  128.7 0.0 copy-start.2
  128.7 0.9 copy-done.2
  129.7 0.9 copy-done.13
  130.6 0.7 copy-done.15
  131.3 0.7 copy-done.17
  132.0 2.2 %shard_map.92 = (f32[128,512]{1,0:T(8,128)}, f32[8,128]{1,0:T(8,128)}) custom-call(bf16[32,40,128]{2,1,0:T(8,128)(2,1)S(1)} %all-to-all-done.4.in_ref, f32[2,136,256]{2,1,0:T(8,128)S(1)} %convert.halves_ref, f32[128,512]{1,0:T(8,128)S(1)} %copy-done, f32[128,512]{1,0:T(8,128)S(1)} %copy-done.2, f32[128,8]{1,0:T(8,128)S(1)} %copy.9.log_ref, ...), custom_call_target="tpu_custom_call" | custom-call | flops 100000000 | bytes 1671168 | tf_op jit(solution)/shard_map/pallas_call | solution.py:83
  134.2 2.0 %collective-permute-done.2.high_ref = bf16[256,512]{1,0:T(8,128)(2,1)S(1)} collective-permute-done((bf16[256,512]{1,0:T(8,128)(2,1)}, bf16[256,512]{1,0:T(8,128)(2,1)S(1)}, u32[]{:S(2)}, u32[]{:S(2)}) %collective-permute-start.2) | collective-permute-done | bytes 262176 | tf_op jit(solution)/shard_map/ppermute | solution.py:347
  136.3 0.7 copy-done.10
  137.0 5.3 %all-to-all-done.5.grads_ref = bf16[8,256,128]{2,1,0:T(8,128)(2,1)S(1)} async-done(((bf16[8,256,128]{2,1,0:T(8,128)(2,1)}), bf16[8,256,128]{2,1,0:T(8,128)(2,1)S(1)}, u32[]{:S(2)}, u32[]{:S(2)}) %all-to-all-start.5) | async-done | bytes 524320 | tf_op jit(solution)/shard_map/all_to_all | solution.py:446
  142.4 0.8 copy-done.4
  143.2 3.5 %all-to-all-start.6 = ((bf16[4,8,64,128]{3,2,1,0:T(8,128)(2,1)}), bf16[4,8,64,128]{3,2,1,0:T(8,128)(2,1)S(1)}, u32[]{:S(2)}, u32[]{:S(2)}) async-start(bf16[4,8,64,128]{3,2,1,0:T(8,128)(2,1)} %copy-done.4), calls=%async_computation.6 | async-start | bytes 1048576 | tf_op jit(solution)/shard_map/all_to_all | solution.py:456
  146.6 0.1 pad_add_fusion.place_ref
  146.7 8.3 %all-to-all-done.6.grads_ref = bf16[4,8,64,128]{3,2,1,0:T(8,128)(2,1)S(1)} async-done(((bf16[4,8,64,128]{3,2,1,0:T(8,128)(2,1)}), bf16[4,8,64,128]{3,2,1,0:T(8,128)(2,1)S(1)}, u32[]{:S(2)}, u32[]{:S(2)}) %all-to-all-start.6) | async-done | bytes 524320 | tf_op jit(solution)/shard_map/all_to_all | solution.py:456
  155.0 0.0 copy-done.6
  155.0 0.9 copy-done.11
  156.0 1.0 shard_map.94
  157.0 1.9 %collective-permute-start.3 = (bf16[4,64,512]{2,1,0:T(8,128)(2,1)S(1)}, bf16[4,64,512]{2,1,0:T(8,128)(2,1)S(1)}, u32[]{:S(2)}, u32[]{:S(2)}) collective-permute-start(bf16[4,64,512]{2,1,0:T(8,128)(2,1)S(1)} %get-tuple-element.51), channel_id=1, source_target_pairs={{0,16},{16,0},{1,17},{17,1},{2,18},{18,2},{3,19},{19,3},{4,20},{20... | collective-permute-start | bytes 786440 | tf_op jit(solution)/shard_map/ppermute | solution.py:347
  158.9 1.1 shard_map.95
  160.0 0.4 collective-permute-done.3.other_ref
  160.4 0.1 shard_map.96
  160.5 14.9 %all_to_all.44.parts_ref = bf16[4,64,512]{2,1,0:T(8,128)(2,1)S(1)} all-to-all(bf16[4,64,512]{2,1,0:T(8,128)(2,1)S(1)} %shard_map.96), channel_id=1, replica_groups=mesh['ylo'=4,'x'=4,'core'=2,'z'=8,'yhi'=2] {'ylo'}, dimensions={0} | all-to-all | bytes 524288 | tf_op jit(solution)/shard_map/all_to_all | solution.py:481
  175.4 0.7 shard_map.97
  (18 shorter events, 0.2 us)
Async XLA Ops:
  13.7 20.8 %copy-start.14 = (f32[128,8]{0,1:T(8,128)S(1)}, f32[128,8]{0,1:T(8,128)}, u32[]{:S(2)}) copy-start(f32[128,8]{0,1:T(8,128)} %param.8) | copy-start | bytes 12292
  13.7 20.9 %copy-start = (f32[128,512]{1,0:T(8,128)S(1)}, f32[128,512]{1,0:T(8,128)}, u32[]{:S(2)}) copy-start(f32[128,512]{1,0:T(8,128)} %x_ref.7) | copy-start | bytes 786436
  13.7 20.9 %copy-start.1 = (f32[128,512]{1,0:T(8,128)S(1)}, f32[128,512]{1,0:T(8,128)}, u32[]{:S(2)}) copy-start(f32[128,512]{1,0:T(8,128)} %dy_ref.5) | copy-start | bytes 786436
  13.7 23.4 %copy-start.9 = (bf16[128,512]{1,0:T(8,128)(2,1)S(1)}, bf16[128,512]{1,0:T(8,128)(2,1)}, u32[]{:S(2)}) copy-start(bf16[128,512]{1,0:T(8,128)(2,1)} %x_ref.5) | copy-start | bytes 393220
  32.6 4.5 %collective-permute-start = (bf16[16,64,512]{2,1,0:T(8,128)(2,1)S(1)}, bf16[16,64,512]{2,1,0:T(8,128)(2,1)S(1)}, u32[]{:S(2)}, u32[]{:S(2)}) collective-permute-start(bf16[16,64,512]{2,1,0:T(8,128)(2,1)S(1)} %bitcast.8), channel_id=1, source_target_pairs={{0,16},{16,0},{1,17},{17,1},{2,18},{18,2},{3,19},{19,3},{4,20},{20... | collective-permute-start | bytes 3145736 | tf_op jit(solution)/shard_map/ppermute | solution.py:347
  92.6 0.7 copy-start.5
  93.3 16.3 %all-to-all-start.4 = ((bf16[32,40,128]{2,1,0:T(8,128)(2,1)}), bf16[32,40,128]{2,1,0:T(8,128)(2,1)S(1)}, u32[]{:S(2)}, u32[]{:S(2)}) async-start(bf16[32,40,128]{2,1,0:T(8,128)(2,1)} %copy-done.5), calls=%async_computation.4 | async-start | bytes 655360 | tf_op jit(solution)/shard_map/all_to_all | solution.py:420
  99.8 8.9 %collective-permute-start.1 = (bf16[128,512]{1,0:T(8,128)(2,1)S(1)}, bf16[128,512]{1,0:T(8,128)(2,1)S(1)}, u32[]{:S(2)}, u32[]{:S(2)}) collective-permute-start(bf16[128,512]{1,0:T(8,128)(2,1)S(1)} %copy-done.9), channel_id=1, source_target_pairs={{0,32},{32,0},{64,96},{96,64},{1,33},{33,1},{65,97},{97,65},{2,34}... | collective-permute-start | bytes 393224 | tf_op jit(solution)/shard_map/ppermute | solution.py:347
  104.5 0.8 copy-start.7
  105.3 0.7 copy-start.12
  106.0 15.1 %copy-start.16 = (f32[8,128]{1,0:T(8,128)}, f32[8,128]{1,0:T(8,128)S(1)}, u32[]{:S(2)}) copy-start(f32[8,128]{1,0:T(8,128)S(1)} %get-tuple-element.43.inside_ref) | copy-start | bytes 12292
  109.6 1.1 copy-start.8
  121.1 0.8 copy-start.3
  121.9 20.4 %all-to-all-start.5 = ((bf16[8,256,128]{2,1,0:T(8,128)(2,1)}), bf16[8,256,128]{2,1,0:T(8,128)(2,1)S(1)}, u32[]{:S(2)}, u32[]{:S(2)}) async-start(bf16[8,256,128]{2,1,0:T(8,128)(2,1)} %copy-done.3), calls=%async_computation.5 | async-start | bytes 1048576 | tf_op jit(solution)/shard_map/all_to_all | solution.py:446
  125.4 10.8 %collective-permute-start.2 = (bf16[256,512]{1,0:T(8,128)(2,1)}, bf16[256,512]{1,0:T(8,128)(2,1)S(1)}, u32[]{:S(2)}, u32[]{:S(2)}) collective-permute-start(bf16[256,512]{1,0:T(8,128)(2,1)} %pad_maximum_fusion.low_ref), channel_id=1, source_target_pairs={{0,64},{32,96},{64,0},{96,32},{1,65},{33,97},{65,1},{97,33},{2,66}... | collective-permute-start | bytes 786440 | tf_op jit(solution)/shard_map/ppermute | solution.py:347
  128.7 1.0 copy-start.2
  129.7 0.9 copy-start.13
  130.6 0.7 copy-start.15
  131.3 0.7 copy-start.17
  134.2 20.8 %copy-start.6 = (bf16[256,512]{1,0:T(8,128)(2,1)S(1)}, bf16[256,512]{1,0:T(8,128)(2,1)}, u32[]{:S(2)}) copy-start(bf16[256,512]{1,0:T(8,128)(2,1)} %pad_maximum_fusion.low_ref) | copy-start | bytes 786436
  136.3 0.7 copy-start.10
  142.3 0.8 copy-start.4
  143.2 11.9 %all-to-all-start.6 = ((bf16[4,8,64,128]{3,2,1,0:T(8,128)(2,1)}), bf16[4,8,64,128]{3,2,1,0:T(8,128)(2,1)S(1)}, u32[]{:S(2)}, u32[]{:S(2)}) async-start(bf16[4,8,64,128]{3,2,1,0:T(8,128)(2,1)} %copy-done.4), calls=%async_computation.6 | async-start | bytes 1048576 | tf_op jit(solution)/shard_map/all_to_all | solution.py:456
  155.0 1.0 copy-start.11
  157.0 3.4 %collective-permute-start.3 = (bf16[4,64,512]{2,1,0:T(8,128)(2,1)S(1)}, bf16[4,64,512]{2,1,0:T(8,128)(2,1)S(1)}, u32[]{:S(2)}, u32[]{:S(2)}) collective-permute-start(bf16[4,64,512]{2,1,0:T(8,128)(2,1)S(1)} %get-tuple-element.51), channel_id=1, source_target_pairs={{0,16},{16,0},{1,17},{17,1},{2,18},{18,2},{3,19},{19,3},{4,20},{20... | collective-permute-start | bytes 786440 | tf_op jit(solution)/shard_map/ppermute | solution.py:347

commit v5 on v4

--- a/solution.py
+++ b/solution.py
@@ -9,6 +9,7 @@
 N = 128
 EXTRA_ROWS = 8
 LN2 = 0.6931471805599453
+SCALE = 256.0
 F32 = jnp.float32
 BF16 = jnp.bfloat16
 F16 = jnp.float16
@@ -177,7 +178,7 @@
     out_ref[:, half : 2 * half, :] = (grad * power(-grad_exponent)).reshape(parts, half, N)
     row = lax.broadcasted_iota(jnp.int32, (EXTRA_ROWS, N), 0)
     for head in range(heads):
-        terms = jnp.where(row == 3, state_exponent, three_terms(ds_ref[head : head + 1, :]))
+        terms = jnp.where(row == 3, state_exponent, three_terms(SCALE * ds_ref[head : head + 1, :]))
         terms = jnp.where(row == 4, grad_exponent, terms)
         for part in range(head * parts // heads, (head + 1) * parts // heads):
             out_ref[part, 2 * half :, :] = terms
@@ -219,7 +220,7 @@
     def extra(t, k):
         return parts_ref[t, rows + k : rows + k + 1, :]
 
-    decays = [jnp.exp(extra(t, 0) + extra(t, 1) + extra(t, 2)) for t in range(slabs)]
+    decays = [jnp.exp((extra(t, 0) + extra(t, 1) + extra(t, 2)) / SCALE) for t in range(slabs)]
     grads = [jnp.zeros((half, N), F32)]
     for t in range(slabs - 1, 0, -1):
         grads.append(decays[t] * grads[-1] + power(extra(t, 4)) * parts_ref[t, half:rows, :])

time: 177 us -> 177 us (level)
  no operation moved by 1% of the time
where the time goes in v5:
time: 177 us; the launch traced here: 176 us
  blocking collectives  109 us (62%)
  starting transfers between devices  24 us (14%)
  waiting for transfers between devices  20.5 us (12%)
  local copies, waits for them, and re-layouts  11 us (6%)
  Pallas kernels  9.55 us (5%)
    all_to_all x2, blocking collectives, to_all(): lax.all_to_all(jnp.broadcast_to(block[None], (count,) + block.shape), axi...  30.9 us
    all_to_all x1, blocking collectives, on_device(): pieces = lax.all_to_all(partial.astype(F16), 'z', 0, 0).astype(F32)  28.6 us
    all_to_all x1, blocking collectives, on_device(): shares = lax.all_to_all(parts.astype(F16), TM, 0, 0).astype(F32)  15.6 us
    all_to_all x1, blocking collectives, on_device(): of_line = lax.all_to_all(of_chip, 'ylo', 0, 0)  14.9 us
    ppermute x4, starting transfers between devices, flip(): lax.ppermute(block, axis, [(k, k ^ bit) for k in range(lax.axis_size(axis...  10.5 us
    all_gather x1, blocking collectives, on_device(): halves_grad = lax.all_gather(own_grad, 'yhi')  10.1 us
    unnamed x37, local copies, waits for them, and re-layouts  10 us
    pallas_call x14, Pallas kernels, call(): pl.pallas_call(kernel, out_shape=outs, in_specs=[pl.BlockSpec(memory_spac...  9.55 us
  transfers between devices with their start and end apart: 7, of which 7 were waited for; matrix products, arithmetic and copies ran while one was open for 1% of the time, Pallas kernels for 3%

profile of v5, /device:TPU:56, one launch (start us, length us, event | category | flops | bytes accessed | tf_op | source)
XLA Modules:
  0.0 176.1 jit_solution(14918996173774313677)
XLA Ops:
  0.6 0.9 broadcast_in_dim.4
  1.5 12.1 %all_to_all.40 = bf16[4,64,512]{2,1,0:T(8,128)(2,1)S(1)} all-to-all(bf16[4,64,512]{2,1,0:T(8,128)(2,1)S(1)} %broadcast_in_dim.4), channel_id=1, replica_groups=mesh['ylo'=4,'x'=4,'core'=2,'z'=8,'yhi'=2] {'ylo'}, dimensions={0} | all-to-all | bytes 524288 | tf_op jit(solution)/shard_map/all_to_all | solution.py:344
  13.6 0.1 broadcast_in_dim.5
  13.7 0.0 copy-start.14
  13.7 0.0 copy-start
  13.7 0.0 copy-start.1
  13.7 0.0 copy-start.9
  13.7 18.9 %all_to_all.41 = bf16[4,4,64,512]{3,2,1,0:T(8,128)(2,1)S(1)} all-to-all(bf16[4,4,64,512]{3,2,1,0:T(8,128)(2,1)S(1)} %broadcast_in_dim.5), channel_id=1, replica_groups=mesh['ylo'=4,'x'=4,'core'=2,'z'=8,'yhi'=2] {'x'}, dimensions={0} | all-to-all | bytes 2097152 | tf_op jit(solution)/shard_map/all_to_all | solution.py:344
  32.6 1.9 %collective-permute-start = (bf16[16,64,512]{2,1,0:T(8,128)(2,1)S(1)}, bf16[16,64,512]{2,1,0:T(8,128)(2,1)S(1)}, u32[]{:S(2)}, u32[]{:S(2)}) collective-permute-start(bf16[16,64,512]{2,1,0:T(8,128)(2,1)S(1)} %bitcast.8), channel_id=1, source_target_pairs={{0,16},{16,0},{1,17},{17,1},{2,18},{18,2},{3,19},{19,3},{4,20},{20... | collective-permute-start | bytes 3145736 | tf_op jit(solution)/shard_map/ppermute | solution.py:348
  34.5 0.0 copy-done.14
  34.5 0.1 copy.9.log_ref
  34.6 0.0 copy-done
  34.6 0.0 copy-done.1
  34.6 0.9 shard_map.84
  35.5 1.6 collective-permute-done.other_ref
  37.1 0.0 copy-done.9
  37.1 1.0 shard_map.85
  38.1 0.1 convert_element_type.18
  38.2 28.6 %all_to_all.42 = f16[8,136,256]{2,1,0:T(8,128)(2,1)S(1)} all-to-all(f16[8,136,256]{2,1,0:T(8,128)(2,1)S(1)} %convert_element_type.18), channel_id=1, replica_groups=mesh['ylo'=4,'x'=4,'core'=2,'z'=8,'yhi'=2] {'z'}, dimensions={0} | all-to-all | bytes 1114112 | tf_op jit(solution)/shard_map/all_to_all | solution.py:392
  66.8 0.1 convert_element_type.19.pieces_ref
  66.9 0.1 shard_map.86
  67.0 9.0 %all-gather = f16[272,256]{1,0:T(8,128)(2,1)S(1)} all-gather(f16[136,256]{1,0:T(8,128)(2,1)S(1)} %convert_element_type.20), channel_id=2, replica_groups=mesh['ylo'=4,'x'=4,'core'=2,'z'=8,'yhi'=2] {'yhi'}, dimensions={0}, use_global_device_ids=true | all-gather | bytes 208896 | tf_op jit(solution)/shard_map/all_gather | solution.py:394
  76.1 0.6 shard_map.87
  76.7 15.6 %all_to_all.43 = f16[32,40,128]{2,1,0:T(8,128)(2,1)S(1)} all-to-all(f16[32,40,128]{2,1,0:T(8,128)(2,1)S(1)} %convert_element_type.22), channel_id=1, replica_groups=mesh['ylo'=4,'x'=4,'core'=2,'z'=8,'yhi'=2] {'ylo','x','core'}, dimensions={0} | all-to-all | bytes 655360 | tf_op jit(solution)/shard_map/all_to_all | solution.py:405
  92.3 0.2 shard_map.88
  92.6 0.0 copy-start.5
  92.6 0.7 copy-done.5
  93.3 6.5 %all-to-all-start.4 = ((bf16[32,40,128]{2,1,0:T(8,128)(2,1)}), bf16[32,40,128]{2,1,0:T(8,128)(2,1)S(1)}, u32[]{:S(2)}, u32[]{:S(2)}) async-start(bf16[32,40,128]{2,1,0:T(8,128)(2,1)} %copy-done.5), calls=%async_computation.4 | async-start | bytes 655360 | tf_op jit(solution)/shard_map/all_to_all | solution.py:421
  99.8 3.4 %collective-permute-start.1 = (bf16[128,512]{1,0:T(8,128)(2,1)S(1)}, bf16[128,512]{1,0:T(8,128)(2,1)S(1)}, u32[]{:S(2)}, u32[]{:S(2)}) collective-permute-start(bf16[128,512]{1,0:T(8,128)(2,1)S(1)} %copy-done.9), channel_id=1, source_target_pairs={{0,32},{32,0},{64,96},{96,64},{1,33},{33,1},{65,97},{97,65},{2,34}... | collective-permute-start | bytes 393224 | tf_op jit(solution)/shard_map/ppermute | solution.py:348
  103.2 1.3 shard_map.89
  104.5 0.0 copy-start.7
  104.5 0.8 copy-done.7
  105.3 0.7 copy-done.12
  106.0 2.7 %collective-permute-done.1 = bf16[128,512]{1,0:T(8,128)(2,1)S(1)} collective-permute-done((bf16[128,512]{1,0:T(8,128)(2,1)S(1)}, bf16[128,512]{1,0:T(8,128)(2,1)S(1)}, u32[]{:S(2)}, u32[]{:S(2)}) %collective-permute-start.1) | collective-permute-done | bytes 131104 | tf_op jit(solution)/shard_map/ppermute | solution.py:348
  108.7 0.7 pad_maximum_fusion.low_ref
  109.4 0.2 all-to-all-done.4.in_ref
  109.7 1.1 copy-done.8
  110.7 0.3 shard_map.90
  111.0 10.1 %all-gather.1 = bf16[512,128]{1,0:T(8,128)(2,1)S(1)} all-gather(bf16[256,128]{1,0:T(8,128)(2,1)S(1)} %shard_map.90), channel_id=3, replica_groups=mesh['ylo'=4,'x'=4,'core'=2,'z'=8,'yhi'=2] {'yhi'}, dimensions={0}, use_global_device_ids=true | all-gather | bytes 196608 | tf_op jit(solution)/shard_map/all_gather | solution.py:432
  121.1 0.8 copy-done.3
  121.9 3.5 %all-to-all-start.5 = ((bf16[8,256,128]{2,1,0:T(8,128)(2,1)}), bf16[8,256,128]{2,1,0:T(8,128)(2,1)S(1)}, u32[]{:S(2)}, u32[]{:S(2)}) async-start(bf16[8,256,128]{2,1,0:T(8,128)(2,1)} %copy-done.3), calls=%async_computation.5 | async-start | bytes 1048576 | tf_op jit(solution)/shard_map/all_to_all | solution.py:447
  125.4 3.3 %collective-permute-start.2 = (bf16[256,512]{1,0:T(8,128)(2,1)}, bf16[256,512]{1,0:T(8,128)(2,1)S(1)}, u32[]{:S(2)}, u32[]{:S(2)}) collective-permute-start(bf16[256,512]{1,0:T(8,128)(2,1)} %pad_maximum_fusion.low_ref), channel_id=1, source_target_pairs={{0,64},{32,96},{64,0},{96,32},{1,65},{33,97},{65,1},{97,33},{2,66}... | collective-permute-start | bytes 786440 | tf_op jit(solution)/shard_map/ppermute | solution.py:348
  128.8 0.0 copy-start.2
  128.8 0.9 copy-done.2
  129.7 0.9 copy-done.13
  130.7 0.7 copy-done.15
  131.4 0.7 copy-done.17
  132.0 2.2 %shard_map.92 = (f32[128,512]{1,0:T(8,128)}, f32[8,128]{1,0:T(8,128)}) custom-call(bf16[32,40,128]{2,1,0:T(8,128)(2,1)S(1)} %all-to-all-done.4.in_ref, f32[2,136,256]{2,1,0:T(8,128)S(1)} %convert.halves_ref, f32[128,512]{1,0:T(8,128)S(1)} %copy-done, f32[128,512]{1,0:T(8,128)S(1)} %copy-done.2, f32[128,8]{1,0:T(8,128)S(1)} %copy.9.log_ref, ...), custom_call_target="tpu_custom_call" | custom-call | flops 100000000 | bytes 1671168 | tf_op jit(solution)/shard_map/pallas_call | solution.py:84
  134.3 2.0 %collective-permute-done.2.high_ref = bf16[256,512]{1,0:T(8,128)(2,1)S(1)} collective-permute-done((bf16[256,512]{1,0:T(8,128)(2,1)}, bf16[256,512]{1,0:T(8,128)(2,1)S(1)}, u32[]{:S(2)}, u32[]{:S(2)}) %collective-permute-start.2) | collective-permute-done | bytes 262176 | tf_op jit(solution)/shard_map/ppermute | solution.py:348
  136.3 0.7 copy-done.10
  137.0 5.3 %all-to-all-done.5.grads_ref = bf16[8,256,128]{2,1,0:T(8,128)(2,1)S(1)} async-done(((bf16[8,256,128]{2,1,0:T(8,128)(2,1)}), bf16[8,256,128]{2,1,0:T(8,128)(2,1)S(1)}, u32[]{:S(2)}, u32[]{:S(2)}) %all-to-all-start.5) | async-done | bytes 524320 | tf_op jit(solution)/shard_map/all_to_all | solution.py:447
  142.4 0.0 copy-start.4
  142.4 0.8 copy-done.4
  143.2 3.5 %all-to-all-start.6 = ((bf16[4,8,64,128]{3,2,1,0:T(8,128)(2,1)}), bf16[4,8,64,128]{3,2,1,0:T(8,128)(2,1)S(1)}, u32[]{:S(2)}, u32[]{:S(2)}) async-start(bf16[4,8,64,128]{3,2,1,0:T(8,128)(2,1)} %copy-done.4), calls=%async_computation.6 | async-start | bytes 1048576 | tf_op jit(solution)/shard_map/all_to_all | solution.py:457
  146.6 0.1 pad_add_fusion.place_ref
  146.7 8.3 %all-to-all-done.6.grads_ref = bf16[4,8,64,128]{3,2,1,0:T(8,128)(2,1)S(1)} async-done(((bf16[4,8,64,128]{3,2,1,0:T(8,128)(2,1)}), bf16[4,8,64,128]{3,2,1,0:T(8,128)(2,1)S(1)}, u32[]{:S(2)}, u32[]{:S(2)}) %all-to-all-start.6) | async-done | bytes 524320 | tf_op jit(solution)/shard_map/all_to_all | solution.py:457
  155.0 0.9 copy-done.11
  156.0 1.0 shard_map.94
  157.0 1.9 %collective-permute-start.3 = (bf16[4,64,512]{2,1,0:T(8,128)(2,1)S(1)}, bf16[4,64,512]{2,1,0:T(8,128)(2,1)S(1)}, u32[]{:S(2)}, u32[]{:S(2)}) collective-permute-start(bf16[4,64,512]{2,1,0:T(8,128)(2,1)S(1)} %get-tuple-element.51), channel_id=1, source_target_pairs={{0,16},{16,0},{1,17},{17,1},{2,18},{18,2},{3,19},{19,3},{4,20},{20... | collective-permute-start | bytes 786440 | tf_op jit(solution)/shard_map/ppermute | solution.py:348
  158.9 1.1 shard_map.95
  160.0 0.4 collective-permute-done.3.other_ref
  160.4 0.1 shard_map.96
  160.5 14.9 %all_to_all.44.parts_ref = bf16[4,64,512]{2,1,0:T(8,128)(2,1)S(1)} all-to-all(bf16[4,64,512]{2,1,0:T(8,128)(2,1)S(1)} %shard_map.96), channel_id=1, replica_groups=mesh['ylo'=4,'x'=4,'core'=2,'z'=8,'yhi'=2] {'ylo'}, dimensions={0} | all-to-all | bytes 524288 | tf_op jit(solution)/shard_map/all_to_all | solution.py:482
  175.4 0.7 shard_map.97
  (18 shorter events, 0.2 us)
Async XLA Ops:
  13.7 20.8 %copy-start.14 = (f32[128,8]{0,1:T(8,128)S(1)}, f32[128,8]{0,1:T(8,128)}, u32[]{:S(2)}) copy-start(f32[128,8]{0,1:T(8,128)} %param.8) | copy-start | bytes 12292
  13.7 20.9 %copy-start = (f32[128,512]{1,0:T(8,128)S(1)}, f32[128,512]{1,0:T(8,128)}, u32[]{:S(2)}) copy-start(f32[128,512]{1,0:T(8,128)} %x_ref.7) | copy-start | bytes 786436
  13.7 20.9 %copy-start.1 = (f32[128,512]{1,0:T(8,128)S(1)}, f32[128,512]{1,0:T(8,128)}, u32[]{:S(2)}) copy-start(f32[128,512]{1,0:T(8,128)} %dy_ref.5) | copy-start | bytes 786436
  13.7 23.4 %copy-start.9 = (bf16[128,512]{1,0:T(8,128)(2,1)S(1)}, bf16[128,512]{1,0:T(8,128)(2,1)}, u32[]{:S(2)}) copy-start(bf16[128,512]{1,0:T(8,128)(2,1)} %x_ref.5) | copy-start | bytes 393220
  32.6 4.5 %collective-permute-start = (bf16[16,64,512]{2,1,0:T(8,128)(2,1)S(1)}, bf16[16,64,512]{2,1,0:T(8,128)(2,1)S(1)}, u32[]{:S(2)}, u32[]{:S(2)}) collective-permute-start(bf16[16,64,512]{2,1,0:T(8,128)(2,1)S(1)} %bitcast.8), channel_id=1, source_target_pairs={{0,16},{16,0},{1,17},{17,1},{2,18},{18,2},{3,19},{19,3},{4,20},{20... | collective-permute-start | bytes 3145736 | tf_op jit(solution)/shard_map/ppermute | solution.py:348
  92.6 0.7 copy-start.5
  93.3 16.3 %all-to-all-start.4 = ((bf16[32,40,128]{2,1,0:T(8,128)(2,1)}), bf16[32,40,128]{2,1,0:T(8,128)(2,1)S(1)}, u32[]{:S(2)}, u32[]{:S(2)}) async-start(bf16[32,40,128]{2,1,0:T(8,128)(2,1)} %copy-done.5), calls=%async_computation.4 | async-start | bytes 655360 | tf_op jit(solution)/shard_map/all_to_all | solution.py:421
  99.8 8.9 %collective-permute-start.1 = (bf16[128,512]{1,0:T(8,128)(2,1)S(1)}, bf16[128,512]{1,0:T(8,128)(2,1)S(1)}, u32[]{:S(2)}, u32[]{:S(2)}) collective-permute-start(bf16[128,512]{1,0:T(8,128)(2,1)S(1)} %copy-done.9), channel_id=1, source_target_pairs={{0,32},{32,0},{64,96},{96,64},{1,33},{33,1},{65,97},{97,65},{2,34}... | collective-permute-start | bytes 393224 | tf_op jit(solution)/shard_map/ppermute | solution.py:348
  104.5 0.8 copy-start.7
  105.3 0.7 copy-start.12
  106.0 15.1 %copy-start.16 = (f32[8,128]{1,0:T(8,128)}, f32[8,128]{1,0:T(8,128)S(1)}, u32[]{:S(2)}) copy-start(f32[8,128]{1,0:T(8,128)S(1)} %get-tuple-element.43.inside_ref) | copy-start | bytes 12292
  109.6 1.1 copy-start.8
  121.1 0.8 copy-start.3
  121.9 20.4 %all-to-all-start.5 = ((bf16[8,256,128]{2,1,0:T(8,128)(2,1)}), bf16[8,256,128]{2,1,0:T(8,128)(2,1)S(1)}, u32[]{:S(2)}, u32[]{:S(2)}) async-start(bf16[8,256,128]{2,1,0:T(8,128)(2,1)} %copy-done.3), calls=%async_computation.5 | async-start | bytes 1048576 | tf_op jit(solution)/shard_map/all_to_all | solution.py:447
  125.4 10.8 %collective-permute-start.2 = (bf16[256,512]{1,0:T(8,128)(2,1)}, bf16[256,512]{1,0:T(8,128)(2,1)S(1)}, u32[]{:S(2)}, u32[]{:S(2)}) collective-permute-start(bf16[256,512]{1,0:T(8,128)(2,1)} %pad_maximum_fusion.low_ref), channel_id=1, source_target_pairs={{0,64},{32,96},{64,0},{96,32},{1,65},{33,97},{65,1},{97,33},{2,66}... | collective-permute-start | bytes 786440 | tf_op jit(solution)/shard_map/ppermute | solution.py:348
  128.8 1.0 copy-start.2
  129.7 0.9 copy-start.13
  130.7 0.7 copy-start.15
  131.4 0.7 copy-start.17
  134.3 20.7 %copy-start.6 = (bf16[256,512]{1,0:T(8,128)(2,1)S(1)}, bf16[256,512]{1,0:T(8,128)(2,1)}, u32[]{:S(2)}) copy-start(bf16[256,512]{1,0:T(8,128)(2,1)} %pad_maximum_fusion.low_ref) | copy-start | bytes 786436
  136.3 0.7 copy-start.10
  142.4 0.8 copy-start.4
  143.2 11.9 %all-to-all-start.6 = ((bf16[4,8,64,128]{3,2,1,0:T(8,128)(2,1)}), bf16[4,8,64,128]{3,2,1,0:T(8,128)(2,1)S(1)}, u32[]{:S(2)}, u32[]{:S(2)}) async-start(bf16[4,8,64,128]{3,2,1,0:T(8,128)(2,1)} %copy-done.4), calls=%async_computation.6 | async-start | bytes 1048576 | tf_op jit(solution)/shard_map/all_to_all | solution.py:457
  155.0 1.0 copy-start.11
  157.0 3.4 %collective-permute-start.3 = (bf16[4,64,512]{2,1,0:T(8,128)(2,1)S(1)}, bf16[4,64,512]{2,1,0:T(8,128)(2,1)S(1)}, u32[]{:S(2)}, u32[]{:S(2)}) collective-permute-start(bf16[4,64,512]{2,1,0:T(8,128)(2,1)S(1)} %get-tuple-element.51), channel_id=1, source_target_pairs={{0,16},{16,0},{1,17},{17,1},{2,18},{18,2},{3,19},{19,3},{4,20},{20... | collective-permute-start | bytes 786440 | tf_op jit(solution)/shard_map/ppermute | solution.py:348

commit v6 on v5

--- a/solution.py
+++ b/solution.py
@@ -130,15 +130,10 @@
     x = x_ref[...]
     steps = x.shape[0]
     groups, _, columns = out_ref.shape
-    top = jnp.zeros((steps, columns), F32)
     for group in range(groups):
         part = dot_nt(x, blocks_of(first, own_ref, other_ref, group, groups // 2))
-        top = jnp.maximum(top, jnp.abs(part))
-        out_ref[group, :steps, :] = part
-    exponent = exponent_of(top)
-    scale = power(-exponent)
-    for group in range(groups):
-        out_ref[group, :steps, :] = out_ref[group, :steps, :] * scale
+        exponent = exponent_of(part)
+        out_ref[group, :steps, :] = part * power(-exponent)
         out_ref[group, steps:, :] = jnp.broadcast_to(exponent, (EXTRA_ROWS, columns))
 
 
@@ -206,10 +201,10 @@
         inside_ref[h : h + 1, :] = jnp.sum(jnp.where(row < col, reach, 0.0), axis=0, keepdims=True)
     width = x_ref.shape[1]
     to_end, from_start = decay_factors(cum, width)
-    terms_ref[:, :width] = x_ref[...] * to_end
-    terms_ref[:, width : 2 * width] = dy_ref[...] * from_start
-    terms_ref[:, 2 * width : 2 * width + N] = dot(pair_sum.astype(BF16), c_rows)
-    terms_ref[:, 2 * width + N :] = dot(pair_sum.T.astype(BF16), b_rows)
+    terms_ref[:, :width] = (x_ref[...] * to_end).astype(BF16)
+    terms_ref[:, width : 2 * width] = (dy_ref[...] * from_start).astype(BF16)
+    terms_ref[:, 2 * width : 2 * width + N] = dot(pair_sum.astype(BF16), c_rows).astype(BF16)
+    terms_ref[:, 2 * width + N :] = dot(pair_sum.T.astype(BF16), b_rows).astype(BF16)
 
 
 def scan_kernel(parts_ref, out_ref):
@@ -245,10 +240,10 @@
 def bc_grad_kernel(in_ref, terms_ref, out_ref):
     state, grad = entering(in_ref)
     width = state.shape[0]
-    from_grad = dot(terms_ref[:, :width].astype(BF16), grad)
-    from_state = dot(terms_ref[:, width : 2 * width].astype(BF16), state)
-    out_ref[:N, :] = (terms_ref[:, 2 * width : 2 * width + N] + from_grad).T.astype(BF16)
-    out_ref[N:, :] = (terms_ref[:, 2 * width + N :] + from_state).T.astype(BF16)
+    from_grad = dot(terms_ref[:, :width], grad)
+    from_state = dot(terms_ref[:, width : 2 * width], state)
+    out_ref[:N, :] = (terms_ref[:, 2 * width : 2 * width + N].astype(F32) + from_grad).T.astype(BF16)
+    out_ref[N:, :] = (terms_ref[:, 2 * width + N :].astype(F32) + from_state).T.astype(BF16)
 
 
 def finish_kernel(in_ref, halves_ref, x_ref, dy_ref, log_ref, logt_ref, gx_ref, inside_ref, out_ref, out_log_ref):
@@ -407,7 +402,7 @@
         local_kernel,
         (
             shape(ssd_input.shape),
-            shape((steps, 2 * (ssd_input.shape[1] + N))),
+            shape((steps, 2 * (ssd_input.shape[1] + N)), BF16),
             shape((heads, steps)),
         ),
         10**8,

time: 177 us -> 177 us (level)
  no operation moved by 1% of the time
where the time goes in v6:
time: 177 us; the launch traced here: 176 us
  blocking collectives  109 us (62%)
  starting transfers between devices  24 us (14%)
  waiting for transfers between devices  20.6 us (12%)
  local copies, waits for them, and re-layouts  10.7 us (6%)
  Pallas kernels  9.52 us (5%)
    all_to_all x2, blocking collectives, to_all(): lax.all_to_all(jnp.broadcast_to(block[None], (count,) + block.shape), axi...  30.9 us
    all_to_all x1, blocking collectives, on_device(): pieces = lax.all_to_all(partial.astype(F16), 'z', 0, 0).astype(F32)  28.6 us
    all_to_all x1, blocking collectives, on_device(): shares = lax.all_to_all(parts.astype(F16), TM, 0, 0).astype(F32)  15.6 us
    all_to_all x1, blocking collectives, on_device(): of_line = lax.all_to_all(of_chip, 'ylo', 0, 0)  14.9 us
    ppermute x4, starting transfers between devices, flip(): lax.ppermute(block, axis, [(k, k ^ bit) for k in range(lax.axis_size(axis...  10.5 us
    all_gather x1, blocking collectives, on_device(): halves_grad = lax.all_gather(own_grad, 'yhi')  10.1 us
    unnamed x37, local copies, waits for them, and re-layouts  9.78 us
    pallas_call x14, Pallas kernels, call(): pl.pallas_call(kernel, out_shape=outs, in_specs=[pl.BlockSpec(memory_spac...  9.52 us
  transfers between devices with their start and end apart: 7, of which 7 were waited for; matrix products, arithmetic and copies ran while one was open for 1% of the time, Pallas kernels for 3%

profile of v6, /device:TPU:56, one launch (start us, length us, event | category | flops | bytes accessed | tf_op | source)
XLA Modules:
  0.0 175.9 jit_solution(17063113646176886645)
XLA Ops:
  0.6 0.9 broadcast_in_dim.4
  1.5 12.1 %all_to_all.40 = bf16[4,64,512]{2,1,0:T(8,128)(2,1)S(1)} all-to-all(bf16[4,64,512]{2,1,0:T(8,128)(2,1)S(1)} %broadcast_in_dim.4), channel_id=1, replica_groups=mesh['ylo'=4,'x'=4,'core'=2,'z'=8,'yhi'=2] {'ylo'}, dimensions={0} | all-to-all | bytes 524288 | tf_op jit(solution)/shard_map/all_to_all | solution.py:339
  13.6 0.1 broadcast_in_dim.5
  13.7 0.0 copy-start.14
  13.7 0.0 copy-start
  13.7 0.0 copy-start.1
  13.7 0.0 copy-start.7
  13.7 18.9 %all_to_all.41 = bf16[4,4,64,512]{3,2,1,0:T(8,128)(2,1)S(1)} all-to-all(bf16[4,4,64,512]{3,2,1,0:T(8,128)(2,1)S(1)} %broadcast_in_dim.5), channel_id=1, replica_groups=mesh['ylo'=4,'x'=4,'core'=2,'z'=8,'yhi'=2] {'x'}, dimensions={0} | all-to-all | bytes 2097152 | tf_op jit(solution)/shard_map/all_to_all | solution.py:339
  32.6 1.9 %collective-permute-start = (bf16[16,64,512]{2,1,0:T(8,128)(2,1)S(1)}, bf16[16,64,512]{2,1,0:T(8,128)(2,1)S(1)}, u32[]{:S(2)}, u32[]{:S(2)}) collective-permute-start(bf16[16,64,512]{2,1,0:T(8,128)(2,1)S(1)} %bitcast.8), channel_id=1, source_target_pairs={{0,16},{16,0},{1,17},{17,1},{2,18},{18,2},{3,19},{19,3},{4,20},{20... | collective-permute-start | bytes 3145736 | tf_op jit(solution)/shard_map/ppermute | solution.py:343
  34.5 0.0 copy-done.14
  34.5 0.1 copy.9.log_ref
  34.6 0.0 copy-done
  34.6 0.0 copy-done.1
  34.6 0.9 shard_map.84
  35.5 1.6 collective-permute-done.other_ref
  37.1 0.0 copy-done.7
  37.1 1.0 shard_map.85
  38.1 0.1 convert_element_type.18
  38.2 28.6 %all_to_all.42 = f16[8,136,256]{2,1,0:T(8,128)(2,1)S(1)} all-to-all(f16[8,136,256]{2,1,0:T(8,128)(2,1)S(1)} %convert_element_type.18), channel_id=1, replica_groups=mesh['ylo'=4,'x'=4,'core'=2,'z'=8,'yhi'=2] {'z'}, dimensions={0} | all-to-all | bytes 1114112 | tf_op jit(solution)/shard_map/all_to_all | solution.py:387
  66.8 0.1 convert_element_type.19.pieces_ref
  66.9 0.1 shard_map.86
  67.0 9.0 %all-gather = f16[272,256]{1,0:T(8,128)(2,1)S(1)} all-gather(f16[136,256]{1,0:T(8,128)(2,1)S(1)} %convert_element_type.20), channel_id=2, replica_groups=mesh['ylo'=4,'x'=4,'core'=2,'z'=8,'yhi'=2] {'yhi'}, dimensions={0}, use_global_device_ids=true | all-gather | bytes 208896 | tf_op jit(solution)/shard_map/all_gather | solution.py:389
  76.1 0.6 shard_map.87
  76.7 15.6 %all_to_all.43 = f16[32,40,128]{2,1,0:T(8,128)(2,1)S(1)} all-to-all(f16[32,40,128]{2,1,0:T(8,128)(2,1)S(1)} %convert_element_type.22), channel_id=1, replica_groups=mesh['ylo'=4,'x'=4,'core'=2,'z'=8,'yhi'=2] {'ylo','x','core'}, dimensions={0} | all-to-all | bytes 655360 | tf_op jit(solution)/shard_map/all_to_all | solution.py:400
  92.3 0.2 shard_map.88
  92.5 0.0 copy-start.5
  92.6 0.7 copy-done.5
  93.3 6.5 %all-to-all-start.4 = ((bf16[32,40,128]{2,1,0:T(8,128)(2,1)}), bf16[32,40,128]{2,1,0:T(8,128)(2,1)S(1)}, u32[]{:S(2)}, u32[]{:S(2)}) async-start(bf16[32,40,128]{2,1,0:T(8,128)(2,1)} %copy-done.5), calls=%async_computation.4 | async-start | bytes 655360 | tf_op jit(solution)/shard_map/all_to_all | solution.py:416
  99.7 3.4 %collective-permute-start.1 = (bf16[128,512]{1,0:T(8,128)(2,1)S(1)}, bf16[128,512]{1,0:T(8,128)(2,1)S(1)}, u32[]{:S(2)}, u32[]{:S(2)}) collective-permute-start(bf16[128,512]{1,0:T(8,128)(2,1)S(1)} %copy-done.7), channel_id=1, source_target_pairs={{0,32},{32,0},{64,96},{96,64},{1,33},{33,1},{65,97},{97,65},{2,34}... | collective-permute-start | bytes 393224 | tf_op jit(solution)/shard_map/ppermute | solution.py:343
  103.1 1.3 shard_map.89
  104.4 0.0 copy-start.8
  104.4 0.7 copy-done.8
  105.2 0.7 copy-done.12
  105.9 2.8 %collective-permute-done.1 = bf16[128,512]{1,0:T(8,128)(2,1)S(1)} collective-permute-done((bf16[128,512]{1,0:T(8,128)(2,1)S(1)}, bf16[128,512]{1,0:T(8,128)(2,1)S(1)}, u32[]{:S(2)}, u32[]{:S(2)}) %collective-permute-start.1) | collective-permute-done | bytes 131104 | tf_op jit(solution)/shard_map/ppermute | solution.py:343
  108.7 0.7 pad_maximum_fusion.low_ref
  109.4 0.2 all-to-all-done.4.in_ref
  109.6 1.0 copy-done.9
  110.6 0.3 shard_map.90
  110.9 10.1 %all-gather.1 = bf16[512,128]{1,0:T(8,128)(2,1)S(1)} all-gather(bf16[256,128]{1,0:T(8,128)(2,1)S(1)} %shard_map.90), channel_id=3, replica_groups=mesh['ylo'=4,'x'=4,'core'=2,'z'=8,'yhi'=2] {'yhi'}, dimensions={0}, use_global_device_ids=true | all-gather | bytes 196608 | tf_op jit(solution)/shard_map/all_gather | solution.py:427
  121.0 0.8 copy-done.3
  121.8 3.5 %all-to-all-start.5 = ((bf16[8,256,128]{2,1,0:T(8,128)(2,1)}), bf16[8,256,128]{2,1,0:T(8,128)(2,1)S(1)}, u32[]{:S(2)}, u32[]{:S(2)}) async-start(bf16[8,256,128]{2,1,0:T(8,128)(2,1)} %copy-done.3), calls=%async_computation.5 | async-start | bytes 1048576 | tf_op jit(solution)/shard_map/all_to_all | solution.py:442
  125.3 3.3 %collective-permute-start.2 = (bf16[256,512]{1,0:T(8,128)(2,1)}, bf16[256,512]{1,0:T(8,128)(2,1)S(1)}, u32[]{:S(2)}, u32[]{:S(2)}) collective-permute-start(bf16[256,512]{1,0:T(8,128)(2,1)} %pad_maximum_fusion.low_ref), channel_id=1, source_target_pairs={{0,64},{32,96},{64,0},{96,32},{1,65},{33,97},{65,1},{97,33},{2,66}... | collective-permute-start | bytes 786440 | tf_op jit(solution)/shard_map/ppermute | solution.py:343
  128.6 0.0 copy-start.2
  128.6 0.9 copy-done.2
  129.6 0.9 copy-done.13
  130.5 0.7 copy-done.15
  131.2 0.7 copy-done.17
  131.9 2.2 %shard_map.92 = (f32[128,512]{1,0:T(8,128)}, f32[8,128]{1,0:T(8,128)}) custom-call(bf16[32,40,128]{2,1,0:T(8,128)(2,1)S(1)} %all-to-all-done.4.in_ref, f32[2,136,256]{2,1,0:T(8,128)S(1)} %convert.halves_ref, f32[128,512]{1,0:T(8,128)S(1)} %copy-done, f32[128,512]{1,0:T(8,128)S(1)} %copy-done.2, f32[128,8]{1,0:T(8,128)S(1)} %copy.9.log_ref, ...), custom_call_target="tpu_custom_call" | custom-call | flops 100000000 | bytes 1671168 | tf_op jit(solution)/shard_map/pallas_call | solution.py:84
  134.1 2.0 %collective-permute-done.2.high_ref = bf16[256,512]{1,0:T(8,128)(2,1)S(1)} collective-permute-done((bf16[256,512]{1,0:T(8,128)(2,1)}, bf16[256,512]{1,0:T(8,128)(2,1)S(1)}, u32[]{:S(2)}, u32[]{:S(2)}) %collective-permute-start.2) | collective-permute-done | bytes 262176 | tf_op jit(solution)/shard_map/ppermute | solution.py:343
  136.1 0.7 copy-done.10
  136.8 5.3 %all-to-all-done.5.grads_ref = bf16[8,256,128]{2,1,0:T(8,128)(2,1)S(1)} async-done(((bf16[8,256,128]{2,1,0:T(8,128)(2,1)}), bf16[8,256,128]{2,1,0:T(8,128)(2,1)S(1)}, u32[]{:S(2)}, u32[]{:S(2)}) %all-to-all-start.5) | async-done | bytes 524320 | tf_op jit(solution)/shard_map/all_to_all | solution.py:442
  142.2 0.8 copy-done.4
  143.0 3.5 %all-to-all-start.6 = ((bf16[4,8,64,128]{3,2,1,0:T(8,128)(2,1)}), bf16[4,8,64,128]{3,2,1,0:T(8,128)(2,1)S(1)}, u32[]{:S(2)}, u32[]{:S(2)}) async-start(bf16[4,8,64,128]{3,2,1,0:T(8,128)(2,1)} %copy-done.4), calls=%async_computation.6 | async-start | bytes 1048576 | tf_op jit(solution)/shard_map/all_to_all | solution.py:452
  146.5 0.1 pad_add_fusion.place_ref
  146.6 8.3 %all-to-all-done.6.grads_ref = bf16[4,8,64,128]{3,2,1,0:T(8,128)(2,1)S(1)} async-done(((bf16[4,8,64,128]{3,2,1,0:T(8,128)(2,1)}), bf16[4,8,64,128]{3,2,1,0:T(8,128)(2,1)S(1)}, u32[]{:S(2)}, u32[]{:S(2)}) %all-to-all-start.6) | async-done | bytes 524320 | tf_op jit(solution)/shard_map/all_to_all | solution.py:452
  154.9 0.0 copy-done.6
  154.9 0.9 copy-done.11
  155.8 1.0 shard_map.94
  156.8 1.9 %collective-permute-start.3 = (bf16[4,64,512]{2,1,0:T(8,128)(2,1)S(1)}, bf16[4,64,512]{2,1,0:T(8,128)(2,1)S(1)}, u32[]{:S(2)}, u32[]{:S(2)}) collective-permute-start(bf16[4,64,512]{2,1,0:T(8,128)(2,1)S(1)} %get-tuple-element.51), channel_id=1, source_target_pairs={{0,16},{16,0},{1,17},{17,1},{2,18},{18,2},{3,19},{19,3},{4,20},{20... | collective-permute-start | bytes 786440 | tf_op jit(solution)/shard_map/ppermute | solution.py:343
  158.8 1.1 shard_map.95
  159.9 0.4 collective-permute-done.3.other_ref
  160.3 0.1 shard_map.96
  160.3 14.9 %all_to_all.44.parts_ref = bf16[4,64,512]{2,1,0:T(8,128)(2,1)S(1)} all-to-all(bf16[4,64,512]{2,1,0:T(8,128)(2,1)S(1)} %shard_map.96), channel_id=1, replica_groups=mesh['ylo'=4,'x'=4,'core'=2,'z'=8,'yhi'=2] {'ylo'}, dimensions={0} | all-to-all | bytes 524288 | tf_op jit(solution)/shard_map/all_to_all | solution.py:477
  175.2 0.7 shard_map.97
  (18 shorter events, 0.2 us)
Async XLA Ops:
  13.7 20.8 %copy-start.14 = (f32[128,8]{0,1:T(8,128)S(1)}, f32[128,8]{0,1:T(8,128)}, u32[]{:S(2)}) copy-start(f32[128,8]{0,1:T(8,128)} %param.8) | copy-start | bytes 12292
  13.7 20.9 %copy-start = (f32[128,512]{1,0:T(8,128)S(1)}, f32[128,512]{1,0:T(8,128)}, u32[]{:S(2)}) copy-start(f32[128,512]{1,0:T(8,128)} %x_ref.7) | copy-start | bytes 786436
  13.7 20.9 %copy-start.1 = (f32[128,512]{1,0:T(8,128)S(1)}, f32[128,512]{1,0:T(8,128)}, u32[]{:S(2)}) copy-start(f32[128,512]{1,0:T(8,128)} %dy_ref.5) | copy-start | bytes 786436
  13.7 23.4 %copy-start.7 = (bf16[128,512]{1,0:T(8,128)(2,1)S(1)}, bf16[128,512]{1,0:T(8,128)(2,1)}, u32[]{:S(2)}) copy-start(bf16[128,512]{1,0:T(8,128)(2,1)} %x_ref.5) | copy-start | bytes 393220
  32.6 4.5 %collective-permute-start = (bf16[16,64,512]{2,1,0:T(8,128)(2,1)S(1)}, bf16[16,64,512]{2,1,0:T(8,128)(2,1)S(1)}, u32[]{:S(2)}, u32[]{:S(2)}) collective-permute-start(bf16[16,64,512]{2,1,0:T(8,128)(2,1)S(1)} %bitcast.8), channel_id=1, source_target_pairs={{0,16},{16,0},{1,17},{17,1},{2,18},{18,2},{3,19},{19,3},{4,20},{20... | collective-permute-start | bytes 3145736 | tf_op jit(solution)/shard_map/ppermute | solution.py:343
  92.5 0.7 copy-start.5
  93.3 16.3 %all-to-all-start.4 = ((bf16[32,40,128]{2,1,0:T(8,128)(2,1)}), bf16[32,40,128]{2,1,0:T(8,128)(2,1)S(1)}, u32[]{:S(2)}, u32[]{:S(2)}) async-start(bf16[32,40,128]{2,1,0:T(8,128)(2,1)} %copy-done.5), calls=%async_computation.4 | async-start | bytes 655360 | tf_op jit(solution)/shard_map/all_to_all | solution.py:416
  99.7 8.9 %collective-permute-start.1 = (bf16[128,512]{1,0:T(8,128)(2,1)S(1)}, bf16[128,512]{1,0:T(8,128)(2,1)S(1)}, u32[]{:S(2)}, u32[]{:S(2)}) collective-permute-start(bf16[128,512]{1,0:T(8,128)(2,1)S(1)} %copy-done.7), channel_id=1, source_target_pairs={{0,32},{32,0},{64,96},{96,64},{1,33},{33,1},{65,97},{97,65},{2,34}... | collective-permute-start | bytes 393224 | tf_op jit(solution)/shard_map/ppermute | solution.py:343
  104.4 0.7 copy-start.8
  105.2 0.7 copy-start.12
  105.9 15.1 %copy-start.16 = (f32[8,128]{1,0:T(8,128)}, f32[8,128]{1,0:T(8,128)S(1)}, u32[]{:S(2)}) copy-start(f32[8,128]{1,0:T(8,128)S(1)} %get-tuple-element.43.inside_ref) | copy-start | bytes 12292
  109.6 1.0 copy-start.9
  121.0 0.8 copy-start.3
  121.8 20.4 %all-to-all-start.5 = ((bf16[8,256,128]{2,1,0:T(8,128)(2,1)}), bf16[8,256,128]{2,1,0:T(8,128)(2,1)S(1)}, u32[]{:S(2)}, u32[]{:S(2)}) async-start(bf16[8,256,128]{2,1,0:T(8,128)(2,1)} %copy-done.3), calls=%async_computation.5 | async-start | bytes 1048576 | tf_op jit(solution)/shard_map/all_to_all | solution.py:442
  125.3 10.8 %collective-permute-start.2 = (bf16[256,512]{1,0:T(8,128)(2,1)}, bf16[256,512]{1,0:T(8,128)(2,1)S(1)}, u32[]{:S(2)}, u32[]{:S(2)}) collective-permute-start(bf16[256,512]{1,0:T(8,128)(2,1)} %pad_maximum_fusion.low_ref), channel_id=1, source_target_pairs={{0,64},{32,96},{64,0},{96,32},{1,65},{33,97},{65,1},{97,33},{2,66}... | collective-permute-start | bytes 786440 | tf_op jit(solution)/shard_map/ppermute | solution.py:343
  128.6 1.0 copy-start.2
  129.6 0.9 copy-start.13
  130.5 0.7 copy-start.15
  131.2 0.7 copy-start.17
  134.1 20.7 %copy-start.6 = (bf16[256,512]{1,0:T(8,128)(2,1)S(1)}, bf16[256,512]{1,0:T(8,128)(2,1)}, u32[]{:S(2)}) copy-start(bf16[256,512]{1,0:T(8,128)(2,1)} %pad_maximum_fusion.low_ref) | copy-start | bytes 786436
  136.1 0.7 copy-start.10
  142.2 0.8 copy-start.4
  143.0 11.9 %all-to-all-start.6 = ((bf16[4,8,64,128]{3,2,1,0:T(8,128)(2,1)}), bf16[4,8,64,128]{3,2,1,0:T(8,128)(2,1)S(1)}, u32[]{:S(2)}, u32[]{:S(2)}) async-start(bf16[4,8,64,128]{3,2,1,0:T(8,128)(2,1)} %copy-done.4), calls=%async_computation.6 | async-start | bytes 1048576 | tf_op jit(solution)/shard_map/all_to_all | solution.py:452
  154.9 1.0 copy-start.11
  156.8 3.4 %collective-permute-start.3 = (bf16[4,64,512]{2,1,0:T(8,128)(2,1)S(1)}, bf16[4,64,512]{2,1,0:T(8,128)(2,1)S(1)}, u32[]{:S(2)}, u32[]{:S(2)}) collective-permute-start(bf16[4,64,512]{2,1,0:T(8,128)(2,1)S(1)} %get-tuple-element.51), channel_id=1, source_target_pairs={{0,16},{16,0},{1,17},{17,1},{2,18},{18,2},{3,19},{19,3},{4,20},{20... | collective-permute-start | bytes 786440 | tf_op jit(solution)/shard_map/ppermute | solution.py:343

commit v7 on v6

--- a/solution.py
+++ b/solution.py
@@ -293,20 +293,24 @@
                 out_ref[2 * high + k, 2 * column + core] = grads_ref[group, at : at + rows, :]
 
 
-def grad_weight_kernel(place_ref, grads_ref, low_ref, high_ref, keep_ref, send_ref):
+def half_weight(place_ref, grads_ref, x_ref, column, blocks, rows):
+    grads = [
+        grads_ref[place_ref[1] ^ k, 2 * column : 2 * column + 2].reshape(2 * rows, -1)
+        for k in blocks
+    ]
+    return dot(jnp.concatenate(grads, axis=1), x_ref[...])
+
+
+def near_weight_kernel(place_ref, grads_ref, x_ref, out_ref):
+    for column in range(out_ref.shape[0]):
+        out_ref[column] = half_weight(place_ref, grads_ref, x_ref, column, (0, 1), grads_ref.shape[2])
+
+
+def grad_weight_kernel(place_ref, grads_ref, x_ref, near_ref, keep_ref, send_ref):
     first = place_ref[0] == 0
-    line = place_ref[1]
-    columns, rows, width = keep_ref.shape
-    x = jnp.concatenate([low_ref[...], high_ref[...]], axis=0)
+    columns, rows, _ = keep_ref.shape
     for column in range(columns):
-        grads = jnp.concatenate(
-            [
-                grads_ref[line ^ k, 2 * column : 2 * column + 2].reshape(2 * rows, -1)
-                for k in range(grads_ref.shape[0])
-            ],
-            axis=1,
-        )
-        part = dot(grads, x)
+        part = near_ref[column] + half_weight(place_ref, grads_ref, x_ref, column, (2, 3), rows)
         one, other = part[:rows], part[rows:]
         keep_ref[column] = jnp.where(first, one, other)
         send_ref[column] = jnp.where(first, other, one).astype(BF16)
@@ -450,14 +454,24 @@
         row_blocks_kernel, shape((4, 2 * columns, rows_here, steps), BF16), 10**6, all_grads
     )
     row_grads = lax.all_to_all(blocks, "x", 0, 0)
+    place = jnp.concatenate([core, lax.axis_index("x").reshape(1)])
+    near_weight = call(
+        near_weight_kernel,
+        shape((columns, 2 * rows_here, width)),
+        steps * width * slabs * rows_here,
+        place,
+        row_grads,
+        pair,
+        smem=1,
+    )
     keep, send = call(
         grad_weight_kernel,
         (shape((columns, rows_here, width)), shape((columns, rows_here, width), BF16)),
-        2 * steps * width * slabs * rows_here,
-        jnp.concatenate([core, lax.axis_index("x").reshape(1)]),
+        steps * width * slabs * rows_here,
+        place,
         row_grads,
-        pair,
         far_pair,
+        near_weight,
         smem=1,
     )
     from_core = swap(send, "core")

time: 177 us -> 177 us (level)
  waiting for transfers between devices: 20.6 us -> 18.7 us
    ppermute x4, waiting for transfers between devices: 6.74 us -> 4.83 us  [flip(): lax.ppermute(block, axis, [(k, k ^ bit) for k in range(lax.axis_size(axis...]
    pallas_call x14 -> x15, Pallas kernels: 9.52 us -> 10.9 us  [call(): pl.pallas_call(kernel, out_shape=outs, in_specs=[pl.BlockSpec(memory_spac...]
    unnamed x37 -> x35, local copies, waits for them, and re-layouts: 9.78 us -> 9.79 us
  transfers between devices with their start and end apart: 7 -> 7, of which waited for: 7 -> 6; matrix products, arithmetic and copies ran while one was open for 1% -> 1% of each run, Pallas kernels for 3% -> 3%
where the time goes in v7:
time: 177 us; the launch traced here: 176 us
  blocking collectives  109 us (62%)
  starting transfers between devices  24.1 us (14%)
  waiting for transfers between devices  18.7 us (11%)
  Pallas kernels  10.9 us (6%)
  local copies, waits for them, and re-layouts  10.7 us (6%)
    all_to_all x2, blocking collectives, to_all(): lax.all_to_all(jnp.broadcast_to(block[None], (count,) + block.shape), axi...  30.9 us
    all_to_all x1, blocking collectives, on_device(): pieces = lax.all_to_all(partial.astype(F16), 'z', 0, 0).astype(F32)  28.6 us
    all_to_all x1, blocking collectives, on_device(): shares = lax.all_to_all(parts.astype(F16), TM, 0, 0).astype(F32)  15.6 us
    all_to_all x1, blocking collectives, on_device(): of_line = lax.all_to_all(of_chip, 'ylo', 0, 0)  14.9 us
    pallas_call x15, Pallas kernels, call(): pl.pallas_call(kernel, out_shape=outs, in_specs=[pl.BlockSpec(memory_spac...  10.9 us
    ppermute x4, starting transfers between devices, flip(): lax.ppermute(block, axis, [(k, k ^ bit) for k in range(lax.axis_size(axis...  10.7 us
    all_gather x1, blocking collectives, on_device(): halves_grad = lax.all_gather(own_grad, 'yhi')  10.1 us
    unnamed x35, local copies, waits for them, and re-layouts  9.79 us
  transfers between devices with their start and end apart: 7, of which 6 were waited for; matrix products, arithmetic and copies ran while one was open for 1% of the time, Pallas kernels for 3%

profile of v7, /device:TPU:56, one launch (start us, length us, event | category | flops | bytes accessed | tf_op | source)
XLA Modules:
  0.0 175.7 jit_solution(10478426808295193975)
XLA Ops:
  0.6 0.9 broadcast_in_dim.4
  1.5 12.1 %all_to_all.40 = bf16[4,64,512]{2,1,0:T(8,128)(2,1)S(1)} all-to-all(bf16[4,64,512]{2,1,0:T(8,128)(2,1)S(1)} %broadcast_in_dim.4), channel_id=1, replica_groups=mesh['ylo'=4,'x'=4,'core'=2,'z'=8,'yhi'=2] {'ylo'}, dimensions={0} | all-to-all | bytes 524288 | tf_op jit(solution)/shard_map/all_to_all | solution.py:343
  13.6 0.1 broadcast_in_dim.5
  13.7 0.0 copy-start.13
  13.7 0.0 copy-start
  13.7 0.0 copy-start.2
  13.7 0.0 copy-start.6
  13.7 18.9 %all_to_all.41 = bf16[4,4,64,512]{3,2,1,0:T(8,128)(2,1)S(1)} all-to-all(bf16[4,4,64,512]{3,2,1,0:T(8,128)(2,1)S(1)} %broadcast_in_dim.5), channel_id=1, replica_groups=mesh['ylo'=4,'x'=4,'core'=2,'z'=8,'yhi'=2] {'x'}, dimensions={0} | all-to-all | bytes 2097152 | tf_op jit(solution)/shard_map/all_to_all | solution.py:343
  32.6 1.9 %collective-permute-start = (bf16[16,64,512]{2,1,0:T(8,128)(2,1)S(1)}, bf16[16,64,512]{2,1,0:T(8,128)(2,1)S(1)}, u32[]{:S(2)}, u32[]{:S(2)}) collective-permute-start(bf16[16,64,512]{2,1,0:T(8,128)(2,1)S(1)} %bitcast.8), channel_id=1, source_target_pairs={{0,16},{16,0},{1,17},{17,1},{2,18},{18,2},{3,19},{19,3},{4,20},{20... | collective-permute-start | bytes 3145736 | tf_op jit(solution)/shard_map/ppermute | solution.py:347
  34.5 0.0 copy-done.13
  34.5 0.1 copy.9.log_ref
  34.6 0.0 copy-done
  34.6 0.0 copy-done.2
  34.6 0.9 shard_map.84
  35.5 1.6 collective-permute-done.other_ref
  37.1 0.0 copy-done.6
  37.1 1.0 shard_map.85
  38.1 0.1 convert_element_type.18
  38.2 28.6 %all_to_all.42 = f16[8,136,256]{2,1,0:T(8,128)(2,1)S(1)} all-to-all(f16[8,136,256]{2,1,0:T(8,128)(2,1)S(1)} %convert_element_type.18), channel_id=1, replica_groups=mesh['ylo'=4,'x'=4,'core'=2,'z'=8,'yhi'=2] {'z'}, dimensions={0} | all-to-all | bytes 1114112 | tf_op jit(solution)/shard_map/all_to_all | solution.py:391
  66.8 0.1 convert_element_type.19.pieces_ref
  66.9 0.1 shard_map.86
  67.0 9.0 %all-gather = f16[272,256]{1,0:T(8,128)(2,1)S(1)} all-gather(f16[136,256]{1,0:T(8,128)(2,1)S(1)} %convert_element_type.20), channel_id=2, replica_groups=mesh['ylo'=4,'x'=4,'core'=2,'z'=8,'yhi'=2] {'yhi'}, dimensions={0}, use_global_device_ids=true | all-gather | bytes 208896 | tf_op jit(solution)/shard_map/all_gather | solution.py:393
  76.1 0.6 shard_map.87
  76.7 15.6 %all_to_all.43 = f16[32,40,128]{2,1,0:T(8,128)(2,1)S(1)} all-to-all(f16[32,40,128]{2,1,0:T(8,128)(2,1)S(1)} %convert_element_type.22), channel_id=1, replica_groups=mesh['ylo'=4,'x'=4,'core'=2,'z'=8,'yhi'=2] {'ylo','x','core'}, dimensions={0} | all-to-all | bytes 655360 | tf_op jit(solution)/shard_map/all_to_all | solution.py:404
  92.3 0.9 shard_map.88
  93.3 6.5 %all-to-all-start.4 = ((bf16[32,40,128]{2,1,0:T(8,128)(2,1)}), bf16[32,40,128]{2,1,0:T(8,128)(2,1)S(1)}, u32[]{:S(2)}, u32[]{:S(2)}) async-start(bf16[32,40,128]{2,1,0:T(8,128)(2,1)} %shard_map.88), calls=%async_computation.4 | async-start | bytes 655360 | tf_op jit(solution)/shard_map/all_to_all | solution.py:420
  99.7 3.4 %collective-permute-start.1 = (bf16[128,512]{1,0:T(8,128)(2,1)S(1)}, bf16[128,512]{1,0:T(8,128)(2,1)S(1)}, u32[]{:S(2)}, u32[]{:S(2)}) collective-permute-start(bf16[128,512]{1,0:T(8,128)(2,1)S(1)} %copy-done.6), channel_id=1, source_target_pairs={{0,32},{32,0},{64,96},{96,64},{1,33},{33,1},{65,97},{97,65},{2,34}... | collective-permute-start | bytes 393224 | tf_op jit(solution)/shard_map/ppermute | solution.py:347
  103.1 1.3 shard_map.89
  104.4 0.0 copy-start.7
  104.4 0.7 copy-done.7
  105.2 0.7 copy-done.11
  105.9 0.6 copy-done.15
  106.5 2.2 %collective-permute-done.1 = bf16[128,512]{1,0:T(8,128)(2,1)S(1)} collective-permute-done((bf16[128,512]{1,0:T(8,128)(2,1)S(1)}, bf16[128,512]{1,0:T(8,128)(2,1)S(1)}, u32[]{:S(2)}, u32[]{:S(2)}) %collective-permute-start.1) | collective-permute-done | bytes 131104 | tf_op jit(solution)/shard_map/ppermute | solution.py:347
  108.7 0.9 pad_maximum_fusion.x_ref
  109.6 0.0 all-to-all-done.4.in_ref
  109.6 1.0 copy-done.8
  110.6 0.3 shard_map.90
  110.9 10.1 %all-gather.1 = bf16[512,128]{1,0:T(8,128)(2,1)S(1)} all-gather(bf16[256,128]{1,0:T(8,128)(2,1)S(1)} %shard_map.90), channel_id=3, replica_groups=mesh['ylo'=4,'x'=4,'core'=2,'z'=8,'yhi'=2] {'yhi'}, dimensions={0}, use_global_device_ids=true | all-gather | bytes 196608 | tf_op jit(solution)/shard_map/all_gather | solution.py:431
  121.0 0.8 copy-done.4
  121.8 3.5 %all-to-all-start.5 = ((bf16[8,256,128]{2,1,0:T(8,128)(2,1)}), bf16[8,256,128]{2,1,0:T(8,128)(2,1)S(1)}, u32[]{:S(2)}, u32[]{:S(2)}) async-start(bf16[8,256,128]{2,1,0:T(8,128)(2,1)} %copy-done.4), calls=%async_computation.5 | async-start | bytes 1048576 | tf_op jit(solution)/shard_map/all_to_all | solution.py:446
  125.3 3.5 %collective-permute-start.2 = (bf16[256,512]{1,0:T(8,128)(2,1)S(1)}, bf16[256,512]{1,0:T(8,128)(2,1)S(1)}, u32[]{:S(2)}, u32[]{:S(2)}) collective-permute-start(bf16[256,512]{1,0:T(8,128)(2,1)S(1)} %pad_maximum_fusion.x_ref), channel_id=1, source_target_pairs={{0,64},{32,96},{64,0},{96,32},{1,65},{33,97},{65,1},{97,33},{2,66}... | collective-permute-start | bytes 786440 | tf_op jit(solution)/shard_map/ppermute | solution.py:347
  128.8 0.0 copy-start.1
  128.8 0.9 copy-done.1
  129.7 0.9 copy-done.3
  130.7 0.9 copy-done.12
  131.6 0.7 copy-done.14
  132.3 0.7 copy-done.16
  133.0 2.2 %shard_map.92 = (f32[128,512]{1,0:T(8,128)}, f32[8,128]{1,0:T(8,128)}) custom-call(bf16[32,40,128]{2,1,0:T(8,128)(2,1)S(1)} %all-to-all-done.4.in_ref, f32[2,136,256]{2,1,0:T(8,128)S(1)} %convert.halves_ref, f32[128,512]{1,0:T(8,128)S(1)} %copy-done.1, f32[128,512]{1,0:T(8,128)S(1)} %copy-done.3, f32[128,8]{1,0:T(8,128)S(1)} %copy.9.log_ref, ...), custom_call_target="tpu_custom_call" | custom-call | flops 100000000 | bytes 1671168 | tf_op jit(solution)/shard_map/pallas_call | solution.py:84
  135.3 0.7 collective-permute-done.2.x_ref
  135.9 0.7 copy-done.9
  136.6 5.5 %all-to-all-done.5.grads_ref = bf16[8,256,128]{2,1,0:T(8,128)(2,1)S(1)} async-done(((bf16[8,256,128]{2,1,0:T(8,128)(2,1)}), bf16[8,256,128]{2,1,0:T(8,128)(2,1)S(1)}, u32[]{:S(2)}, u32[]{:S(2)}) %all-to-all-start.5) | async-done | bytes 524320 | tf_op jit(solution)/shard_map/all_to_all | solution.py:446
  142.2 0.8 copy-done.5
  143.0 3.5 %all-to-all-start.6 = ((bf16[4,8,64,128]{3,2,1,0:T(8,128)(2,1)}), bf16[4,8,64,128]{3,2,1,0:T(8,128)(2,1)S(1)}, u32[]{:S(2)}, u32[]{:S(2)}) async-start(bf16[4,8,64,128]{3,2,1,0:T(8,128)(2,1)} %copy-done.5), calls=%async_computation.6 | async-start | bytes 1048576 | tf_op jit(solution)/shard_map/all_to_all | solution.py:456
  146.5 0.1 pad_add_fusion.place_ref
  146.6 8.3 %all-to-all-done.6.grads_ref = bf16[4,8,64,128]{3,2,1,0:T(8,128)(2,1)S(1)} async-done(((bf16[4,8,64,128]{3,2,1,0:T(8,128)(2,1)}), bf16[4,8,64,128]{3,2,1,0:T(8,128)(2,1)S(1)}, u32[]{:S(2)}, u32[]{:S(2)}) %all-to-all-start.6) | async-done | bytes 524320 | tf_op jit(solution)/shard_map/all_to_all | solution.py:456
  154.9 0.8 shard_map.94.near_ref
  155.7 0.1 copy-done.10
  155.8 0.8 shard_map.95
  156.7 1.9 %collective-permute-start.3 = (bf16[4,64,512]{2,1,0:T(8,128)(2,1)S(1)}, bf16[4,64,512]{2,1,0:T(8,128)(2,1)S(1)}, u32[]{:S(2)}, u32[]{:S(2)}) collective-permute-start(bf16[4,64,512]{2,1,0:T(8,128)(2,1)S(1)} %get-tuple-element.51), channel_id=1, source_target_pairs={{0,16},{16,0},{1,17},{17,1},{2,18},{18,2},{3,19},{19,3},{4,20},{20... | collective-permute-start | bytes 786440 | tf_op jit(solution)/shard_map/ppermute | solution.py:347
  158.6 1.1 shard_map.96
  159.7 0.4 collective-permute-done.3.other_ref
  160.1 0.1 shard_map.97
  160.2 14.9 %all_to_all.44.parts_ref = bf16[4,64,512]{2,1,0:T(8,128)(2,1)S(1)} all-to-all(bf16[4,64,512]{2,1,0:T(8,128)(2,1)S(1)} %shard_map.97), channel_id=1, replica_groups=mesh['ylo'=4,'x'=4,'core'=2,'z'=8,'yhi'=2] {'ylo'}, dimensions={0} | all-to-all | bytes 524288 | tf_op jit(solution)/shard_map/all_to_all | solution.py:491
  175.0 0.7 shard_map.98
  (17 shorter events, 0.2 us)
Async XLA Ops:
  13.7 20.8 %copy-start.13 = (f32[128,8]{0,1:T(8,128)S(1)}, f32[128,8]{0,1:T(8,128)}, u32[]{:S(2)}) copy-start(f32[128,8]{0,1:T(8,128)} %param.8) | copy-start | bytes 12292
  13.7 20.9 %copy-start = (f32[128,512]{1,0:T(8,128)S(1)}, f32[128,512]{1,0:T(8,128)}, u32[]{:S(2)}) copy-start(f32[128,512]{1,0:T(8,128)} %x_ref.7) | copy-start | bytes 786436
  13.7 20.9 %copy-start.2 = (f32[128,512]{1,0:T(8,128)S(1)}, f32[128,512]{1,0:T(8,128)}, u32[]{:S(2)}) copy-start(f32[128,512]{1,0:T(8,128)} %dy_ref.5) | copy-start | bytes 786436
  13.7 23.4 %copy-start.6 = (bf16[128,512]{1,0:T(8,128)(2,1)S(1)}, bf16[128,512]{1,0:T(8,128)(2,1)}, u32[]{:S(2)}) copy-start(bf16[128,512]{1,0:T(8,128)(2,1)} %x_ref.5) | copy-start | bytes 393220
  32.6 4.5 %collective-permute-start = (bf16[16,64,512]{2,1,0:T(8,128)(2,1)S(1)}, bf16[16,64,512]{2,1,0:T(8,128)(2,1)S(1)}, u32[]{:S(2)}, u32[]{:S(2)}) collective-permute-start(bf16[16,64,512]{2,1,0:T(8,128)(2,1)S(1)} %bitcast.8), channel_id=1, source_target_pairs={{0,16},{16,0},{1,17},{17,1},{2,18},{18,2},{3,19},{19,3},{4,20},{20... | collective-permute-start | bytes 3145736 | tf_op jit(solution)/shard_map/ppermute | solution.py:347
  93.3 16.3 %all-to-all-start.4 = ((bf16[32,40,128]{2,1,0:T(8,128)(2,1)}), bf16[32,40,128]{2,1,0:T(8,128)(2,1)S(1)}, u32[]{:S(2)}, u32[]{:S(2)}) async-start(bf16[32,40,128]{2,1,0:T(8,128)(2,1)} %shard_map.88), calls=%async_computation.4 | async-start | bytes 655360 | tf_op jit(solution)/shard_map/all_to_all | solution.py:420
  99.7 8.9 %collective-permute-start.1 = (bf16[128,512]{1,0:T(8,128)(2,1)S(1)}, bf16[128,512]{1,0:T(8,128)(2,1)S(1)}, u32[]{:S(2)}, u32[]{:S(2)}) collective-permute-start(bf16[128,512]{1,0:T(8,128)(2,1)S(1)} %copy-done.6), channel_id=1, source_target_pairs={{0,32},{32,0},{64,96},{96,64},{1,33},{33,1},{65,97},{97,65},{2,34}... | collective-permute-start | bytes 393224 | tf_op jit(solution)/shard_map/ppermute | solution.py:347
  104.4 0.7 copy-start.7
  105.2 0.7 copy-start.11
  105.9 0.6 copy-start.15
  109.6 1.0 copy-start.8
  121.0 0.8 copy-start.4
  121.8 20.4 %all-to-all-start.5 = ((bf16[8,256,128]{2,1,0:T(8,128)(2,1)}), bf16[8,256,128]{2,1,0:T(8,128)(2,1)S(1)}, u32[]{:S(2)}, u32[]{:S(2)}) async-start(bf16[8,256,128]{2,1,0:T(8,128)(2,1)} %copy-done.4), calls=%async_computation.5 | async-start | bytes 1048576 | tf_op jit(solution)/shard_map/all_to_all | solution.py:446
  125.3 10.6 %collective-permute-start.2 = (bf16[256,512]{1,0:T(8,128)(2,1)S(1)}, bf16[256,512]{1,0:T(8,128)(2,1)S(1)}, u32[]{:S(2)}, u32[]{:S(2)}) collective-permute-start(bf16[256,512]{1,0:T(8,128)(2,1)S(1)} %pad_maximum_fusion.x_ref), channel_id=1, source_target_pairs={{0,64},{32,96},{64,0},{96,32},{1,65},{33,97},{65,1},{97,33},{2,66}... | collective-permute-start | bytes 786440 | tf_op jit(solution)/shard_map/ppermute | solution.py:347
  128.8 1.0 copy-start.1
  129.7 0.9 copy-start.3
  130.7 0.9 copy-start.12
  131.6 0.7 copy-start.14
  132.3 0.7 copy-start.16
  135.9 0.7 copy-start.9
  142.2 0.8 copy-start.5
  143.0 11.9 %all-to-all-start.6 = ((bf16[4,8,64,128]{3,2,1,0:T(8,128)(2,1)}), bf16[4,8,64,128]{3,2,1,0:T(8,128)(2,1)S(1)}, u32[]{:S(2)}, u32[]{:S(2)}) async-start(bf16[4,8,64,128]{3,2,1,0:T(8,128)(2,1)} %copy-done.5), calls=%async_computation.6 | async-start | bytes 1048576 | tf_op jit(solution)/shard_map/all_to_all | solution.py:456
  154.9 1.0 copy-start.10
  156.7 3.4 %collective-permute-start.3 = (bf16[4,64,512]{2,1,0:T(8,128)(2,1)S(1)}, bf16[4,64,512]{2,1,0:T(8,128)(2,1)S(1)}, u32[]{:S(2)}, u32[]{:S(2)}) collective-permute-start(bf16[4,64,512]{2,1,0:T(8,128)(2,1)S(1)} %get-tuple-element.51), channel_id=1, source_target_pairs={{0,16},{16,0},{1,17},{17,1},{2,18},{18,2},{3,19},{19,3},{4,20},{20... | collective-permute-start | bytes 786440 | tf_op jit(solution)/shard_map/ppermute | solution.py:347
